TPU v7x, 32 devices: a whole 2x2x4 slice. The times are simulated.
32 devices in a mesh: ctx: 8 (over y, x, core), wsh: 4 (over z).
Axes of the slice: x: 2, y: 2, z: 4, core: 2. Of those that a mesh axis runs over, the one named last changes fastest.
Arguments:
- hidden_in: bfloat16 [4, 1024, 1536], P('wsh', 'ctx'), may hold values from -6 to 6
- routes: int32 [1, 4, 1024, 4], P(None, 'wsh', 'ctx'), may hold values from 0 to 7, all different within a row; in each aligned block of 128 rows (0 to 127, 128 to 255, ..., all dimensions but the last counted through in order) at most 128 rows name the same one
- cotangent: float32 [4, 1024, 1536], P('wsh', 'ctx'), may hold values from -6 to 6
- norm_attn: bfloat16 [1, 1536], P(None, ('ctx', 'wsh')), may hold values from 0.25 to 1.75
- w_query: bfloat16 [1, 1536, 1536], P(None, ('ctx', 'wsh')), may hold values from -0.15625 to 0.15625
- key_projection: bfloat16 [1, 1536, 256], P(None, ('ctx', 'wsh')), may hold values from -0.15625 to 0.15625
- value_projection: bfloat16 [1, 1536, 256], P(None, ('ctx', 'wsh')), may hold values from -0.15625 to 0.15625
- w_out: bfloat16 [1, 1536, 1536], P(None, ('ctx', 'wsh')), may hold values from -2 to 2
- norm_moe: bfloat16 [1, 1536], P(None, ('ctx', 'wsh')), may hold values from 0.25 to 1.75
- w_router: bfloat16 [1, 1536, 8], P(None, ('ctx', 'wsh')), may hold values from -0.078125 to 0.078125
- w_gate: bfloat16 [1, 1536, 8, 768], P(None, 'ctx', 'wsh'), may hold values from -0.15625 to 0.15625
- w_up: bfloat16 [1, 1536, 8, 768], P(None, 'ctx', 'wsh'), may hold values from -0.15625 to 0.15625
- w_down: bfloat16 [1, 1536, 8, 768], P(None, 'ctx', 'wsh'), may hold values from -0.625 to 0.625
Outputs:
- output: float32 [4, 1024, 1536], P('wsh', 'ctx')
- input_grad: float32 [4, 1024, 1536], P('wsh', 'ctx')
- grad_norm_attn: float32 [1, 1536], P(None, ('ctx', 'wsh'))
- grad_w_query: float32 [1, 1536, 1536], P(None, ('ctx', 'wsh'))
- grad_w_key: float32 [1, 1536, 256], P(None, ('ctx', 'wsh'))
- grad_w_value: float32 [1, 1536, 256], P(None, ('ctx', 'wsh'))
- grad_w_out: float32 [1, 1536, 1536], P(None, ('ctx', 'wsh'))
- grad_norm_moe: float32 [1, 1536], P(None, ('ctx', 'wsh'))
- grad_w_router: float32 [1, 1536, 8], P(None, ('ctx', 'wsh'))
- grad_w_gate: float32 [1, 1536, 8, 768], P(None, 'ctx', 'wsh')
- grad_w_up: float32 [1, 1536, 8, 768], P(None, 'ctx', 'wsh')
- grad_w_down: float32 [1, 1536, 8, 768], P(None, 'ctx', 'wsh')
Inputs may be any that keep to these rules, and one draw needn't show every extreme that they name: `routes`: each token names 4 different experts in each layer. Within the 128 tokens of one device (aligned blocks of each sequence) no expert is named more than 128 times, and in some blocks one is named exactly 128 times.
All inputs are finite; a program needn't handle non-finite values.
Results may differ from a plain program's by a relative error of at most 0.02.
Values may be sent and summed in bfloat16 or wider, within the bound.
A program may use at most 192 MiB of HBM per device.

v0:
```python
import jax
import jax.numpy as jnp
from jax import lax
from jax.sharding import PartitionSpec as P

QUERY_HEADS = 12
KEY_VALUE_HEADS = 2
HEAD_DIM = 128
TOP = 4
CAP = 128


NORM_EPSILON = 1e-06
ROTARY_BASE = 1000000.0


def shifted(value, axis, steps):
    count = lax.axis_size(axis)
    pairs = [(source, (source + steps) % count) for source in range(count)]
    return lax.ppermute(value, axis, pairs)


def normalize(hidden_state, gain):
    return (
        hidden_state
        * lax.rsqrt(jnp.mean(hidden_state * hidden_state, axis=-1, keepdims=True) + NORM_EPSILON)
        * gain
    )


def rotary(token_positions, head_size):
    half_size = head_size // 2
    frequency = ROTARY_BASE ** (-jnp.arange(half_size, dtype=jnp.float32) * 2.0 / head_size)
    angles = token_positions.astype(jnp.float32)[:, None] * frequency[None, :]
    return (jnp.cos(angles)[:, None, :], jnp.sin(angles)[:, None, :])


def apply_rotary(values_in, cosine, sine_rows, direction):
    half_size = values_in.shape[-1] // 2
    first_half = values_in[..., :half_size]
    second = values_in[..., half_size:]
    return jnp.concatenate(
        [
            first_half * cosine - direction * second * sine_rows,
            second * cosine + direction * first_half * sine_rows,
        ],
        axis=-1,
    )


def slot_targets(picks_in, matches):
    flat_matches = matches.reshape(-1, matches.shape[-1]).astype(jnp.int32)
    earlier = jnp.cumsum(flat_matches, axis=0) - flat_matches
    return picks_in.reshape(-1) * CAP + jnp.sum(earlier * flat_matches, axis=1)


def score_rows(query_low, key_rows, token_positions):
    total_rows = query_low.shape[0]
    head_size = query_low.shape[2]
    grouped_heads = query_low.reshape(total_rows, key_rows.shape[1], -1, head_size)
    scores = jnp.einsum(
        "qhgd,khd->hgqk", grouped_heads, key_rows, preferred_element_type=jnp.float32
    ) * head_size ** (-0.5)
    allowed = jnp.arange(key_rows.shape[0], dtype=jnp.int32)[None, :] <= token_positions[:, None]
    return (grouped_heads, jnp.where(allowed[None, None], scores, -1e30))


def attend(query_low, key_rows, value_rows, token_positions):
    grouped_heads, scores = score_rows(query_low, key_rows, token_positions)
    highest = jnp.max(scores, axis=-1, keepdims=True)
    log_total = highest + jnp.log(jnp.sum(jnp.exp(scores - highest), axis=-1, keepdims=True))
    weights = jnp.exp(scores - log_total).astype(jnp.bfloat16)
    attended = jnp.einsum("hgqk,khd->qhgd", weights, value_rows, preferred_element_type=jnp.float32)
    return (attended.reshape(query_low.shape[0], -1), log_total)


def attend_grad(query_low, key_rows, value_rows, token_positions, log_total, grad_mixed):
    grouped_heads, scores = score_rows(query_low, key_rows, token_positions)
    score_scale = query_low.shape[-1] ** (-0.5)
    softmax_rows = jnp.exp(scores - log_total)
    weights = softmax_rows.astype(jnp.bfloat16)
    grad_grouped = grad_mixed.reshape(grouped_heads.shape)
    grad_weights = jnp.einsum(
        "qhgd,khd->hgqk", grad_grouped, value_rows, preferred_element_type=jnp.float32
    )
    grad_values = jnp.einsum(
        "hgqk,qhgd->khd", weights, grad_grouped, preferred_element_type=jnp.float32
    )
    row_inner = jnp.sum(softmax_rows * grad_weights, axis=-1, keepdims=True)
    grad_scores = (softmax_rows * (grad_weights - row_inner)).astype(jnp.bfloat16)
    grad_query = (
        jnp.einsum("hgqk,khd->qhgd", grad_scores, key_rows, preferred_element_type=jnp.float32)
        * score_scale
    )
    grad_keys = (
        jnp.einsum("hgqk,qhgd->khd", grad_scores, grouped_heads, preferred_element_type=jnp.float32)
        * score_scale
    )
    return (grad_query.reshape(query_low.shape), grad_keys, grad_values)


def collect_key_grads(grad_keys, grad_values, total_rows):
    cycle_size = lax.axis_size("ctx")
    own_index = lax.axis_index("ctx")
    both_grads = jnp.stack([grad_keys, grad_values])

    def block_piece(block_index):
        return lax.dynamic_slice_in_dim(both_grads, block_index * total_rows, total_rows, 1)

    def cycle_step(step_index, carried):
        moved = shifted(carried.astype(jnp.bfloat16), "ctx", -1).astype(carried.dtype)
        block_index = (own_index + step_index) % cycle_size
        weight_now = jnp.where(step_index < cycle_size, 1.0, 0.0).astype(jnp.float32)
        return moved + weight_now * block_piece(block_index)

    collected = lax.fori_loop(1, cycle_size + 1, cycle_step, block_piece(own_index))
    return (collected[0], collected[1])


def forward_layer(hidden_state, picks_in, dense_set, expert_set):
    gain_attn, query_matrix, key_matrix, value_matrix, output_matrix, gain_moe, router_matrix = (
        dense_set
    )
    gate_w, up_w, down_w = expert_set
    total_rows, model_width = hidden_state.shape
    token_positions = lax.axis_index("ctx") * total_rows + jnp.arange(total_rows, dtype=jnp.int32)
    cosine, sine_rows = rotary(token_positions, HEAD_DIM)
    attention_normed = normalize(hidden_state, gain_attn.astype(jnp.float32)).astype(jnp.bfloat16)
    query_unrotated = jnp.dot(
        attention_normed, query_matrix, preferred_element_type=jnp.float32
    ).reshape(total_rows, QUERY_HEADS, HEAD_DIM)
    key_unrotated = jnp.dot(
        attention_normed, key_matrix, preferred_element_type=jnp.float32
    ).reshape(total_rows, KEY_VALUE_HEADS, HEAD_DIM)
    query_low = apply_rotary(query_unrotated, cosine, sine_rows, 1.0).astype(jnp.bfloat16)
    key_low = apply_rotary(key_unrotated, cosine, sine_rows, 1.0).astype(jnp.bfloat16)
    value_low = (
        jnp.dot(attention_normed, value_matrix, preferred_element_type=jnp.float32)
        .astype(jnp.bfloat16)
        .reshape(total_rows, KEY_VALUE_HEADS, HEAD_DIM)
    )
    key_rows, value_rows = (
        lax.all_gather(key_low, "ctx", axis=0, tiled=True),
        lax.all_gather(value_low, "ctx", axis=0, tiled=True),
    )
    attended, log_total = attend(query_low, key_rows, value_rows, token_positions)
    mixed_reduced = attended.astype(jnp.bfloat16)
    post_attention = hidden_state + lax.dot_general(
        mixed_reduced, output_matrix, (((1,), (1,)), ((), ())), preferred_element_type=jnp.float32
    )
    expert_normed = normalize(post_attention, gain_moe.astype(jnp.float32)).astype(jnp.bfloat16)
    router_logits = jnp.dot(expert_normed, router_matrix, preferred_element_type=jnp.float32)
    expert_count = router_logits.shape[1]
    matches = picks_in[:, :, None] == jnp.arange(expert_count, dtype=jnp.int32)[None, None, :]
    gate_weights = jax.nn.softmax(
        jnp.sum(jnp.where(matches, router_logits[:, None, :], 0.0), axis=-1), axis=-1
    )
    targets = slot_targets(picks_in, matches)
    outgoing = (
        jnp.zeros((expert_count * CAP, model_width), jnp.bfloat16)
        .at[targets]
        .set(jnp.repeat(expert_normed, TOP, axis=0))
    )
    group_count = lax.axis_size("wsh")
    local_count = gate_w.shape[1]
    arrived = lax.all_to_all(
        outgoing.reshape(group_count, local_count, CAP, model_width),
        "wsh",
        split_axis=0,
        concat_axis=0,
        tiled=True,
    )
    gate_pre = jnp.einsum("sjcd,djf->sjcf", arrived, gate_w, preferred_element_type=jnp.float32)
    up_pre = jnp.einsum("sjcd,djf->sjcf", arrived, up_w, preferred_element_type=jnp.float32)
    activations = (jax.nn.silu(gate_pre) * up_pre).astype(jnp.bfloat16)
    produced = jnp.einsum(
        "sjcf,djf->sjcd", activations, down_w, preferred_element_type=jnp.float32
    ).astype(jnp.bfloat16)
    returned = lax.all_to_all(produced, "wsh", split_axis=0, concat_axis=0, tiled=True)
    returned, arrived, gate_pre, up_pre = (returned, arrived, gate_pre, up_pre)
    picked = (
        returned.reshape(-1, model_width)[targets]
        .reshape(total_rows, TOP, model_width)
        .astype(jnp.float32)
    )
    after_moe = post_attention + jnp.sum(gate_weights[:, :, None] * picked, axis=1)
    stored = (
        hidden_state,
        attention_normed,
        query_low,
        key_low,
        value_low,
        log_total,
        mixed_reduced,
        post_attention,
        expert_normed,
        matches,
        gate_weights,
        targets,
        picked,
        arrived,
        gate_pre,
        up_pre,
    )
    return (after_moe, stored, (key_rows, value_rows))


def backward_layer(incoming, stored, dense_set, expert_set, key_rows, value_rows):
    (
        hidden_state,
        attention_normed,
        query_low,
        key_low,
        value_low,
        log_total,
        mixed_reduced,
        post_attention,
        expert_normed,
        matches,
        gate_weights,
        targets,
        picked,
        arrived,
        gate_pre,
        up_pre,
    ) = stored
    gain_attn, query_matrix, key_matrix, value_matrix, output_matrix, gain_moe, router_matrix = (
        dense_set
    )
    gate_w, up_w, down_w = expert_set
    total_rows, model_width = hidden_state.shape
    token_positions = lax.axis_index("ctx") * total_rows + jnp.arange(total_rows, dtype=jnp.int32)
    cosine, sine_rows = rotary(token_positions, HEAD_DIM)
    grad_y = (gate_weights[:, :, None] * incoming[:, None, :]).astype(jnp.bfloat16)
    grad_gates = jnp.sum(incoming[:, None, :] * picked, axis=-1)
    grad_chosen = gate_weights * (
        grad_gates - jnp.sum(gate_weights * grad_gates, axis=-1, keepdims=True)
    )
    grad_logits = jnp.sum(jnp.where(matches, grad_chosen[:, :, None], 0.0), axis=1).astype(
        jnp.bfloat16
    )
    slot_total = arrived.shape[0] * arrived.shape[1] * arrived.shape[2]
    outgoing = (
        jnp.zeros((slot_total, model_width), jnp.bfloat16)
        .at[targets]
        .set(grad_y.reshape(-1, model_width))
    )
    grad_arrived = lax.all_to_all(
        outgoing.reshape(arrived.shape), "wsh", split_axis=0, concat_axis=0, tiled=True
    )
    grad_acts = jnp.einsum(
        "sjcd,djf->sjcf", grad_arrived, down_w, preferred_element_type=jnp.float32
    )
    sigmoid_gate = jax.nn.sigmoid(gate_pre)
    silu_gate = jax.nn.silu(gate_pre)
    activations = (silu_gate * up_pre).astype(jnp.bfloat16)
    grad_gate = (
        grad_acts * up_pre * sigmoid_gate * (1.0 + gate_pre * (1.0 - sigmoid_gate))
    ).astype(jnp.bfloat16)
    grad_up = (grad_acts * silu_gate).astype(jnp.bfloat16)
    grad_rows = (
        jnp.einsum("sjcf,djf->sjcd", grad_gate, gate_w, preferred_element_type=jnp.float32)
        + jnp.einsum("sjcf,djf->sjcd", grad_up, up_w, preferred_element_type=jnp.float32)
    ).astype(jnp.bfloat16)
    grad_back = lax.all_to_all(grad_rows, "wsh", split_axis=0, concat_axis=0, tiled=True)
    expert_grads = (
        lax.psum_scatter(
            jnp.einsum(
                "sjcd,sjcf->djf", arrived, grad_gate, preferred_element_type=jnp.float32
            ).astype(jnp.bfloat16),
            "ctx",
            scatter_dimension=0,
            tiled=True,
        ).astype(jnp.float32),
        lax.psum_scatter(
            jnp.einsum(
                "sjcd,sjcf->djf", arrived, grad_up, preferred_element_type=jnp.float32
            ).astype(jnp.bfloat16),
            "ctx",
            scatter_dimension=0,
            tiled=True,
        ).astype(jnp.float32),
        lax.psum_scatter(
            jnp.einsum(
                "sjcd,sjcf->djf", grad_arrived, activations, preferred_element_type=jnp.float32
            ).astype(jnp.bfloat16),
            "ctx",
            scatter_dimension=0,
            tiled=True,
        ).astype(jnp.float32),
    )
    returned_rows = (
        grad_back.reshape(-1, model_width)[targets]
        .reshape(total_rows, TOP, model_width)
        .astype(jnp.float32)
    )
    grad_normed_moe = jnp.sum(returned_rows, axis=1) + lax.dot_general(
        grad_logits, router_matrix, (((1,), (1,)), ((), ())), preferred_element_type=jnp.float32
    )
    router_term = jnp.einsum(
        "td,te->de", expert_normed, grad_logits, preferred_element_type=jnp.float32
    )
    unused_moe, pull_moe = jax.vjp(normalize, post_attention, gain_moe.astype(jnp.float32))
    grad_after_norm, gain_moe_term = pull_moe(grad_normed_moe)
    grad_after_attn = incoming + grad_after_norm
    grad_attn = grad_after_attn.astype(jnp.bfloat16)
    out_term = jnp.einsum("td,tj->dj", grad_attn, mixed_reduced, preferred_element_type=jnp.float32)
    grad_mixed = jnp.dot(grad_attn, output_matrix, preferred_element_type=jnp.float32).astype(
        jnp.bfloat16
    )
    grad_query, grad_keys, grad_values = attend_grad(
        query_low, key_rows, value_rows, token_positions, log_total, grad_mixed
    )
    grad_key, grad_value = collect_key_grads(grad_keys, grad_values, total_rows)
    grad_query_raw = (
        apply_rotary(grad_query, cosine, sine_rows, -1.0)
        .reshape(total_rows, -1)
        .astype(jnp.bfloat16)
    )
    grad_key_raw = (
        apply_rotary(grad_key, cosine, sine_rows, -1.0).reshape(total_rows, -1).astype(jnp.bfloat16)
    )
    grad_value_raw = grad_value.reshape(total_rows, -1).astype(jnp.bfloat16)
    contract_last = (((1,), (1,)), ((), ()))
    grad_normed_attn = lax.dot_general(
        grad_query_raw, query_matrix, contract_last, preferred_element_type=jnp.float32
    )
    grad_normed_attn = grad_normed_attn + lax.dot_general(
        grad_key_raw, key_matrix, contract_last, preferred_element_type=jnp.float32
    )
    grad_normed_attn = grad_normed_attn + lax.dot_general(
        grad_value_raw, value_matrix, contract_last, preferred_element_type=jnp.float32
    )
    query_term = jnp.einsum(
        "td,tf->df", attention_normed, grad_query_raw, preferred_element_type=jnp.float32
    )
    key_term = jnp.einsum(
        "td,tf->df", attention_normed, grad_key_raw, preferred_element_type=jnp.float32
    )
    value_term = jnp.einsum(
        "td,tf->df", attention_normed, grad_value_raw, preferred_element_type=jnp.float32
    )
    unused_attn, pull_attn = jax.vjp(normalize, hidden_state, gain_attn.astype(jnp.float32))
    grad_before, gain_attn_term = pull_attn(grad_normed_attn)
    layer_grads = (
        lax.psum_scatter(gain_attn_term, ("ctx", "wsh"), scatter_dimension=0, tiled=True),
        lax.psum_scatter(query_term, ("ctx", "wsh"), scatter_dimension=0, tiled=True),
        lax.psum_scatter(key_term, ("ctx", "wsh"), scatter_dimension=0, tiled=True),
        lax.psum_scatter(value_term, ("ctx", "wsh"), scatter_dimension=0, tiled=True),
        lax.psum_scatter(out_term, ("ctx", "wsh"), scatter_dimension=0, tiled=True),
        lax.psum_scatter(gain_moe_term, ("ctx", "wsh"), scatter_dimension=0, tiled=True),
        lax.psum_scatter(router_term, ("ctx", "wsh"), scatter_dimension=0, tiled=True),
    )
    return (grad_after_attn + grad_before, layer_grads, expert_grads)


def body(
    hidden_in,
    routes,
    cotangent,
    norm_attn,
    w_query,
    key_projection,
    value_projection,
    w_out,
    norm_moe,
    w_router,
    w_gate,
    w_up,
    w_down,
):
    hidden_state = hidden_in[0].astype(jnp.float32)
    layer_number = 0
    dense_set = (
        lax.all_gather(norm_attn[layer_number], ("ctx", "wsh"), axis=0, tiled=True),
        lax.all_gather(w_query[layer_number], ("ctx", "wsh"), axis=0, tiled=True),
        lax.all_gather(key_projection[layer_number], ("ctx", "wsh"), axis=0, tiled=True),
        lax.all_gather(value_projection[layer_number], ("ctx", "wsh"), axis=0, tiled=True),
        lax.all_gather(w_out[layer_number], ("ctx", "wsh"), axis=0, tiled=True),
        lax.all_gather(norm_moe[layer_number], ("ctx", "wsh"), axis=0, tiled=True),
        lax.all_gather(w_router[layer_number], ("ctx", "wsh"), axis=0, tiled=True),
    )
    expert_set = (
        lax.all_gather(w_gate[layer_number], "ctx", axis=0, tiled=True),
        lax.all_gather(w_up[layer_number], "ctx", axis=0, tiled=True),
        lax.all_gather(w_down[layer_number], "ctx", axis=0, tiled=True),
    )
    hidden_state, stored, gathered = forward_layer(
        hidden_state, routes[layer_number, 0], dense_set, expert_set
    )
    records = [(stored, None, None, None)]
    incoming = cotangent[0]
    dense_grads = []
    expert_grads = []
    layer_number = 0
    stored, dense_set, expert_set, gathered = records[layer_number]
    dense_set = (
        lax.all_gather(norm_attn[layer_number], ("ctx", "wsh"), axis=0, tiled=True),
        lax.all_gather(w_query[layer_number], ("ctx", "wsh"), axis=0, tiled=True),
        lax.all_gather(key_projection[layer_number], ("ctx", "wsh"), axis=0, tiled=True),
        lax.all_gather(value_projection[layer_number], ("ctx", "wsh"), axis=0, tiled=True),
        lax.all_gather(w_out[layer_number], ("ctx", "wsh"), axis=0, tiled=True),
        lax.all_gather(norm_moe[layer_number], ("ctx", "wsh"), axis=0, tiled=True),
        lax.all_gather(w_router[layer_number], ("ctx", "wsh"), axis=0, tiled=True),
    )
    expert_set = (
        lax.all_gather(w_gate[layer_number], "ctx", axis=0, tiled=True),
        lax.all_gather(w_up[layer_number], "ctx", axis=0, tiled=True),
        lax.all_gather(w_down[layer_number], "ctx", axis=0, tiled=True),
    )
    gathered = (
        lax.all_gather(stored[3], "ctx", axis=0, tiled=True),
        lax.all_gather(stored[4], "ctx", axis=0, tiled=True),
    )
    incoming, layer_grads, layer_expert = backward_layer(
        incoming, stored, dense_set, expert_set, gathered[0], gathered[1]
    )
    dense_grads.insert(0, layer_grads)
    expert_grads.insert(0, layer_expert)
    stacked_dense = [
        jnp.stack([grads_item[position] for grads_item in dense_grads]) for position in range(7)
    ]
    stacked_expert = [
        jnp.stack([grads_item[position] for grads_item in expert_grads]) for position in range(3)
    ]
    return (
        hidden_state[None],
        incoming[None],
        stacked_dense[0],
        stacked_dense[1],
        stacked_dense[2],
        stacked_dense[3],
        stacked_dense[4],
        stacked_dense[5],
        stacked_dense[6],
        stacked_expert[0],
        stacked_expert[1],
        stacked_expert[2],
    )


def solution(mesh):
    return jax.shard_map(
        body,
        mesh=mesh,
        in_specs=(
            P("wsh", "ctx", None),
            P(None, "wsh", "ctx", None),
            P("wsh", "ctx", None),
            P(None, ("ctx", "wsh")),
            P(None, ("ctx", "wsh"), None),
            P(None, ("ctx", "wsh"), None),
            P(None, ("ctx", "wsh"), None),
            P(None, ("ctx", "wsh"), None),
            P(None, ("ctx", "wsh")),
            P(None, ("ctx", "wsh"), None),
            P(None, "ctx", "wsh", None),
            P(None, "ctx", "wsh", None),
            P(None, "ctx", "wsh", None),
        ),
        out_specs=(
            P("wsh", "ctx", None),
            P("wsh", "ctx", None),
            P(None, ("ctx", "wsh")),
            P(None, ("ctx", "wsh"), None),
            P(None, ("ctx", "wsh"), None),
            P(None, ("ctx", "wsh"), None),
            P(None, ("ctx", "wsh"), None),
            P(None, ("ctx", "wsh")),
            P(None, ("ctx", "wsh"), None),
            P(None, "ctx", "wsh", None),
            P(None, "ctx", "wsh", None),
            P(None, "ctx", "wsh", None),
        ),
        check_vma=False,
    )
```

profile of v0, /device:TPU:15, one launch (start us, length us, event | category | flops | bytes accessed | tf_op | source)
XLA Modules:
  0.0 1417.5 jit_solution(16765952336587410853)
XLA Ops:
  13.6 39.7 %all-reduce.8 = (bf16[1536]{0:T(1024)(128)(2,1)S(1)}, bf16[1536]{0:T(1024)(128)(2,1)S(1)}) all-reduce(bf16[1536]{0:T(1024)(128)(2,1)S(1)} %dynamic-update-slice, bf16[1536]{0:T(1024)(128)(2,1)S(1)} %dynamic-update-slice.1), channel_id=2, replica_groups=mesh['ctx'=8,'wsh'=4] {'ctx','wsh'}, use_global_device_ids=true, to_apply=%add | all-reduce | flops 3072 | bytes 12288
  53.5 69.9 %all-gather.1 = bf16[1,1536,256]{2,1,0:T(8,128)(2,1)S(1)} all-gather(bf16[1,48,256]{2,1,0:T(8,128)(2,1)S(1)} %copy-done.43), channel_id=3, replica_groups=mesh['ctx'=8,'wsh'=4] {'ctx','wsh'}, dimensions={1}, use_global_device_ids=true | all-gather | bytes 811008 | tf_op jit(solution)/shard_map/all_gather | solution.py:378
  124.8 73.4 %all-gather.2 = bf16[1,1536,256]{2,1,0:T(8,128)(2,1)S(1)} all-gather(bf16[1,48,256]{2,1,0:T(8,128)(2,1)S(1)} %copy-done.44), channel_id=4, replica_groups=mesh['ctx'=8,'wsh'=4] {'ctx','wsh'}, dimensions={1}, use_global_device_ids=true | all-gather | bytes 811008 | tf_op jit(solution)/shard_map/all_gather | solution.py:377
  201.5 17.4 %all_gather.50 = bf16[1024,2,128]{0,2,1:T(8,128)(2,1)S(1)} all-gather(bf16[128,2,128]{0,2,1:T(8,128)(2,1)S(1)} %bitcast.370), channel_id=1, replica_groups=mesh['ctx'=8,'wsh'=4] {'ctx'}, dimensions={0}, use_global_device_ids=true | all-gather | bytes 589824 | tf_op jit(solution)/shard_map/all_gather | solution.py:144
  218.9 12.5 all_gather.52
  232.2 6.7 copy.212
  255.9 5.4 scatter_custom_fusion
  261.3 5.4 all-to-all-start
  274.3 124.8 %all-gather.6 = bf16[1,1536,8]{2,0,1:T(2,128)(2,1)} all-gather(bf16[1,48,8]{2,0,1:T(2,128)(2,1)} %copy.217), channel_id=8, replica_groups=mesh['ctx'=8,'wsh'=4] {'ctx','wsh'}, dimensions={1}, use_global_device_ids=true | all-gather | bytes 25344 | tf_op jit(solution)/shard_map/all_gather | solution.py:381
  416.0 8.7 all-to-all-start.2
  424.7 7.5 fusion.6
  432.2 7.5 fusion.10
  439.7 51.8 %all-to-all-done.2 = bf16[4,2,128,1536]{3,2,1,0:T(8,128)(2,1)S(1)} async-done(((bf16[4,2,128,1536]{3,2,1,0:T(8,128)(2,1)}), bf16[4,2,128,1536]{3,2,1,0:T(8,128)(2,1)S(1)}, u32[]{:S(2)}, u32[]{:S(2)}) %all-to-all-start.2) | async-done | bytes 3145760 | tf_op jit(solution)/shard_map/all_to_all | solution.py:248
  491.5 9.2 fusion.39
  505.5 6.4 all-to-all-start.1
  517.0 5.3 fusion.34
  524.2 55.7 %all-to-all-done.1 = bf16[4,2,128,1536]{3,2,1,0:T(8,128)(2,1)S(1)} async-done(((bf16[4,2,128,1536]{3,2,1,0:T(8,128)(2,1)}), bf16[4,2,128,1536]{3,2,1,0:T(8,128)(2,1)S(1)}, u32[]{:S(2)}, u32[]{:S(2)}) %all-to-all-start.1) | async-done | bytes 3145760 | tf_op jit(solution)/shard_map/all_to_all | solution.py:179
  581.6 6.7 all-to-all-start.3
  589.7 7.3 fusion.27
  597.0 6.2 fusion.28
  603.2 6.8 gather_fusion
  625.8 7.1 fusion.29
  633.0 12.5 copy.246
  645.5 12.6 copy.249
  658.1 12.6 copy.252
  706.5 87.1 %while.15 = (s32[]{:T(128)}, f32[2,128,2,128]{3,2,1,0:T(2,128)}, s32[]{:T(128)}, f32[2,1024,2,128]{1,3,2,0:T(8,128)}, s32[]{:T(128)}, /*index=5*/s32[]{:T(128)},...) while((s32[]{:T(128)}, f32[2,128,2,128]{3,2,1,0:T(2,128)}, s32[]{:T(128)}, ...), condition=%wide.region_20.21_spmd, body=%wide.region_19.20_spmd.sunk | while | flops 262164 | bytes 2621794 | solution.py:116
  823.0 38.2 %all-reduce.7 = (f32[1536]{0:T(1024)S(1)}, f32[1536]{0:T(1024)S(1)}) all-reduce(f32[1536]{0:T(1024)S(1)} %get-tuple-element.176, f32[1536]{0:T(1024)S(1)} %copy-done.39), channel_id=12, replica_groups=mesh['ctx'=8,'wsh'=4] {'ctx','wsh'}, use_global_device_ids=true, to_apply=%region_23.24.clone | all-reduce | flops 3072 | bytes 24576
  864.3 57.9 %all-reduce.12.cloned.1.call-done = (bf16[1536,2,768]{2,1,0:T(2,128)(2,1)}, bf16[1536,2,768]{2,1,0:T(2,128)(2,1)}, bf16[1536,2,768]{2,1,0:T(2,128)(2,1)}) async-done(((bf16[1536,2,768]{2,1,0:T(2,128)(2,1)}, bf16[1536,2,768]{2,1,0:T(2,128)(2,1)}, bf16[1536,2,768]{2,1,0:T(2,128)(2,1)}), (bf16[1536,2,768]{2,1,0:T(2,128)(2,1)}, bf16[1536,2,768]{2,1,0:T(2,128)(2,1)}, ...) | async-done | bytes 14155792
  928.2 96.4 %reduce-scatter.10.cloned.1.call-done = f32[48,256]{1,0:T(8,128)} async-done(((f32[1536,256]{1,0:T(8,128)}), f32[48,256]{1,0:T(8,128)}) %reduce-scatter.10.cloned.1.call-update) | async-done | bytes 49168 | tf_op jit(solution)/shard_map/reduce_scatter | solution.py:348
  1024.5 102.7 %reduce-scatter.12.cloned.1.call-done = f32[48,256]{1,0:T(8,128)} async-done(((f32[1536,256]{1,0:T(8,128)}), f32[48,256]{1,0:T(8,128)}) %reduce-scatter.12.cloned.1.call-update) | async-done | bytes 49168 | tf_op jit(solution)/shard_map/reduce_scatter | solution.py:349
  1127.3 142.1 %reduce-scatter.8.cloned.1.call-done = f32[48,1536]{1,0:T(8,128)} async-done(((f32[1536,1536]{1,0:T(8,128)}), f32[48,1536]{1,0:T(8,128)}) %reduce-scatter.8.cloned.1.call-update) | async-done | bytes 294928 | tf_op jit(solution)/shard_map/reduce_scatter | solution.py:347
  1269.4 141.1 %reduce-scatter.14.cloned.1.call-done = f32[48,1536]{1,0:T(8,128)} async-done(((f32[1536,1536]{1,0:T(8,128)}), f32[48,1536]{1,0:T(8,128)}) %reduce-scatter.14.cloned.1.call-update) | async-done | bytes 294928 | tf_op jit(solution)/shard_map/reduce_scatter | solution.py:350
  (308 shorter events, 243.7 us)
Async XLA Ops:
  7.2 46.1 %copy-start.2 = (bf16[1,128,1536]{2,1,0:T(8,128)(2,1)S(1)}, bf16[1,128,1536]{2,1,0:T(8,128)(2,1)}, u32[]{:S(2)}) copy-start(bf16[1,128,1536]{2,1,0:T(8,128)(2,1)} %param.15) | copy-start | bytes 1179652
  7.2 46.3 %copy-start.43 = (bf16[1,48,256]{2,1,0:T(8,128)(2,1)S(1)}, bf16[1,48,256]{2,1,0:T(8,128)(2,1)}, u32[]{:S(2)}) copy-start(bf16[1,48,256]{2,1,0:T(8,128)(2,1)} %param.21) | copy-start | bytes 73732
  7.2 224.9 %all-gather.16.cloned.1.call-start = ((), (), s32[]{:S(2)}) async-start(), calls=%async_computation.13 | async-start | bytes 4866048 | tf_op jit(solution)/shard_map/all_gather | solution.py:376
  8.0 241.1 %all-gather.18.cloned.1.call-start = ((), (), s32[]{:S(2)}) async-start(), calls=%async_computation.14 | async-start | bytes 4866048 | tf_op jit(solution)/shard_map/all_gather | solution.py:379
  8.7 116.1 %copy-start.44 = (bf16[1,48,256]{2,1,0:T(8,128)(2,1)S(1)}, bf16[1,48,256]{2,1,0:T(8,128)(2,1)}, u32[]{:S(2)}) copy-start(bf16[1,48,256]{2,1,0:T(8,128)(2,1)} %param.20) | copy-start | bytes 73732
  8.7 416.0 %all-gather.22.cloned.1.call-start = ((), (), s32[]{:S(2)}) async-start(), calls=%async_computation.16 | async-start | bytes 5308416 | tf_op jit(solution)/shard_map/all_gather | solution.py:385
  10.7 421.5 %all-gather.20.cloned.1.call-start = ((), (), s32[]{:S(2)}) async-start(), calls=%async_computation.15 | async-start | bytes 5308416 | tf_op jit(solution)/shard_map/all_gather | solution.py:384
  53.5 145.0 %copy-start.48 = (f32[128]{0:T(128)}, f32[128]{0:T(128)S(1)}, u32[]{:S(2)}) copy-start(f32[128]{0:T(128)S(1)} %fusion.73) | copy-start | bytes 1540
  53.5 185.3 %copy-start.41 = (f32[128]{0:T(128)}, f32[128]{0:T(128)S(1)}, u32[]{:S(2)}) copy-start(f32[128]{0:T(128)S(1)} %fusion.123) | copy-start | bytes 1540
  198.1 40.7 %copy-start.7 = (bf16[1,1536,256]{2,1,0:T(8,128)(2,1)}, bf16[1,1536,256]{2,1,0:T(8,128)(2,1)S(1)}, u32[]{:S(2)}) copy-start(bf16[1,1536,256]{2,1,0:T(8,128)(2,1)S(1)} %all-gather.2) | copy-start | bytes 2359300
  200.9 41.7 %copy-start.29 = (f32[128,64]{0,1:T(8,128)}, f32[128,64]{0,1:T(8,128)S(1)}, u32[]{:S(2)}) copy-start(f32[128,64]{0,1:T(8,128)S(1)} %get-tuple-element.208) | copy-start | bytes 98308
  261.3 154.7 %all-to-all-start = ((bf16[4,2,128,1536]{3,2,1,0:T(8,128)(2,1)}), bf16[4,2,128,1536]{3,2,1,0:T(8,128)(2,1)}, u32[]{:S(2)}, u32[]{:S(2)}) async-start(bf16[4,2,128,1536]{3,2,1,0:T(8,128)(2,1)} %bitcast.28), calls=%async_computation | async-start | bytes 6291456 | tf_op jit(solution)/shard_map/all_to_all | solution.py:166
  266.7 173.1 %all-gather.24.cloned.1.call-start = ((), (), s32[]{:S(2)}) async-start(), calls=%async_computation.17 | async-start | bytes 5308416 | tf_op jit(solution)/shard_map/all_gather | solution.py:386
  416.0 75.5 %all-to-all-start.2 = ((bf16[4,2,128,1536]{3,2,1,0:T(8,128)(2,1)}), bf16[4,2,128,1536]{3,2,1,0:T(8,128)(2,1)S(1)}, u32[]{:S(2)}, u32[]{:S(2)}) async-start(bf16[4,2,128,1536]{3,2,1,0:T(8,128)(2,1)} %bitcast.44), calls=%async_computation.2 | async-start | bytes 6291456 | tf_op jit(solution)/shard_map/all_to_all | solution.py:248
  505.5 74.5 %all-to-all-start.1 = ((bf16[4,2,128,1536]{3,2,1,0:T(8,128)(2,1)}), bf16[4,2,128,1536]{3,2,1,0:T(8,128)(2,1)S(1)}, u32[]{:S(2)}, u32[]{:S(2)}) async-start(bf16[4,2,128,1536]{3,2,1,0:T(8,128)(2,1)} %copy.228), calls=%async_computation.1 | async-start | bytes 6291456 | tf_op jit(solution)/shard_map/all_to_all | solution.py:179
  581.6 89.4 %all-to-all-start.3 = ((bf16[4,2,128,1536]{3,2,1,0:T(8,128)(2,1)}), bf16[4,2,128,1536]{3,2,1,0:T(8,128)(2,1)S(1)}, u32[]{:S(2)}, u32[]{:S(2)}) async-start(bf16[4,2,128,1536]{3,2,1,0:T(8,128)(2,1)} %copy.231), calls=%async_computation.3 | async-start | bytes 6291456 | tf_op jit(solution)/shard_map/all_to_all | solution.py:265
  588.2 274.7 %reduce-scatter.16.cloned.1.call-start = ((), (), s32[]{:S(2)}) async-start(), calls=%async_computation.18 | async-start | bytes 811008
  625.8 296.5 %all-reduce.12.cloned.1.call-start = ((), (), s32[]{:S(2)}) async-start(), calls=%async_computation.19 | async-start | bytes 28311552
  670.8 353.8 %reduce-scatter.10.cloned.1.call-start = ((), (), s32[]{:S(2)}) async-start(), calls=%async_computation.10 | async-start | bytes 1622016 | tf_op jit(solution)/shard_map/reduce_scatter | solution.py:348
  706.5 91.3 %copy-start.42 = (f32[128]{0:T(128)S(1)}, f32[128]{0:T(128)}, u32[]{:S(2)}) copy-start(f32[128]{0:T(128)} %copy-done.41) | copy-start | bytes 1540
  708.4 5.6 collective-permute-start
  717.5 5.6 collective-permute-start
  726.5 5.6 collective-permute-start
  735.6 8.4 collective-permute-start
  747.4 8.6 collective-permute-start
  759.5 8.4 collective-permute-start
  771.3 8.6 collective-permute-start
  783.3 8.6 collective-permute-start
  799.4 327.8 %reduce-scatter.12.cloned.1.call-start = ((), (), s32[]{:S(2)}) async-start(), calls=%async_computation.11 | async-start | bytes 1622016 | tf_op jit(solution)/shard_map/reduce_scatter | solution.py:349
  802.7 466.7 %reduce-scatter.8.cloned.1.call-start = ((), (), s32[]{:S(2)}) async-start(), calls=%async_computation.9 | async-start | bytes 9732096 | tf_op jit(solution)/shard_map/reduce_scatter | solution.py:347
  809.8 600.7 %reduce-scatter.14.cloned.1.call-start = ((), (), s32[]{:S(2)}) async-start(), calls=%async_computation.12 | async-start | bytes 9732096 | tf_op jit(solution)/shard_map/reduce_scatter | solution.py:350
  822.0 39.7 %copy-start.49 = (f32[128]{0:T(128)S(1)}, f32[128]{0:T(128)}, u32[]{:S(2)}) copy-start(f32[128]{0:T(128)} %copy-done.48) | copy-start | bytes 1540
  (51 other events, 202.5 us)
Sparse Core Ops, SparseCore 0:
  10.9 66.2 all-gather.15
  80.0 65.9 all-gather.17
  148.4 37.7 all-gather.21
  188.5 43.3 all-gather.19
  269.7 39.0 all-gather.23
  625.9 94.2 reduce-scatter.15
  724.3 197.9 all-reduce.11
  928.9 95.5 reduce-scatter.9
  1031.2 96.0 reduce-scatter.11
  1134.6 134.7 reduce-scatter.7
  1275.8 134.5 reduce-scatter.13
where the time goes:
time: 1430 us; the launch traced here: 1420 us
  waiting for transfers between devices  680 us (48%)
  blocking collectives  376 us (26%)
  local copies, waits for them, and re-layouts  140 us (10%)
  matrix products  107 us (7%)
  other arithmetic  70.1 us (5%)
  starting transfers between devices  28.7 us (2%)
  between operations  16 us (1%)
    reduce_scatter x1, waiting for transfers between devices, backward_layer(): lax.psum_scatter(query_term, ('ctx', 'wsh'), scatter_dimension=0, tiled=T...  142 us
    reduce_scatter x1, waiting for transfers between devices, backward_layer(): lax.psum_scatter(out_term, ('ctx', 'wsh'), scatter_dimension=0, tiled=True)  141 us
    all_gather x1, blocking collectives, body(): lax.all_gather(w_router[layer_number], ('ctx', 'wsh'), axis=0, tiled=True)  125 us
    reduce_scatter x1, waiting for transfers between devices, backward_layer(): lax.psum_scatter(value_term, ('ctx', 'wsh'), scatter_dimension=0, tiled=T...  103 us
    reduce_scatter x1, waiting for transfers between devices, backward_layer(): lax.psum_scatter(key_term, ('ctx', 'wsh'), scatter_dimension=0, tiled=True)  96.4 us
    unnamed x2, blocking collectives  77.8 us
    all_gather x1, blocking collectives, body(): lax.all_gather(key_projection[layer_number], ('ctx', 'wsh'), axis=0, tile...  73.4 us
    all_gather x1, blocking collectives, body(): lax.all_gather(value_projection[layer_number], ('ctx', 'wsh'), axis=0, ti...  69.9 us
  transfers between devices with their start and end apart: 23, of which 15 were waited for; matrix products, arithmetic and copies ran while one was open for 21% of the time, Pallas kernels for 0%

commit v1 on v0

--- a/solution.py
+++ b/solution.py
@@ -1,17 +1,880 @@
+import functools
 import jax
 import jax.numpy as jnp
 from jax import lax
+from jax.experimental import pallas as pl
+from jax.experimental.pallas import tpu as pltpu
 from jax.sharding import PartitionSpec as P
 
 QUERY_HEADS = 12
 KEY_VALUE_HEADS = 2
 HEAD_DIM = 128
-TOP = 4
 CAP = 128
-
-
 NORM_EPSILON = 1e-06
 ROTARY_BASE = 1000000.0
+MESH = pl.DeviceIdType.MESH
+HEAD = 128
+TOP = 4
+EPS = 1e-06
+BASE = 1000000.0
+F32 = jnp.float32
+BF16 = jnp.bfloat16
+
+
+def dot(a, b):
+    return lax.dot_general(a, b, (((1,), (0,)), ((), ())), preferred_element_type=F32)
+
+
+def dot_t(a, b):
+    return lax.dot_general(a, b, (((1,), (1,)), ((), ())), preferred_element_type=F32)
+
+
+def t_dot(a, b):
+    return lax.dot_general(a, b, (((0,), (0,)), ((), ())), preferred_element_type=F32)
+
+
+class Place:
+    def __init__(self, nctx, nz):
+        self.nctx, self.nz, self.nch = nctx, nz, nctx // 2
+        self.c = lax.axis_index("ctx")
+        self.z = lax.axis_index("wsh")
+        self.chip = self.c // 2
+        self.core = self.c % 2
+        self.sib = self.chip * 2 + 1 - self.core
+        self.square = self.nch == 4
+
+    def xchip(self):
+        return self.chip + 1 - 2 * (self.chip % 2)
+
+    def ychip(self):
+        return (self.chip + 2) % 4
+
+    def zto(self, dz):
+        return (self.z + dz) % self.nz
+
+    def zfrom(self, dz):
+        return (self.z + self.nz - dz) % self.nz
+
+
+class Sends:
+    def __init__(self, sems, count):
+        self.sems, self.count, self.used, self.live = sems, count, 0, []
+
+    def start(self, src, dst, rsem, dev):
+        assert self.used < self.count
+        cp = pltpu.make_async_remote_copy(
+            src_ref=src,
+            dst_ref=dst,
+            send_sem=self.sems.at[self.used],
+            recv_sem=rsem,
+            device_id=dev,
+            device_id_type=MESH,
+        )
+        cp.start()
+        self.used += 1
+        self.live.append(cp)
+        return cp
+
+    def local(self, src, dst):
+        assert self.used < self.count
+        cp = pltpu.make_async_copy(src, dst, self.sems.at[self.used])
+        cp.start()
+        self.used += 1
+        return cp
+
+    def drain(self):
+        for cp in self.live:
+            cp.wait_send()
+        self.live = []
+
+
+def arrived(ref, sem):
+    pltpu.make_async_copy(ref, ref, sem).wait()
+
+
+def greet(pl_, plane=True, column=True):
+    bar = pltpu.get_barrier_semaphore()
+    n = 0
+    if plane:
+        for k in range(1, pl_.nctx):
+            pl.semaphore_signal(
+                bar, inc=1, device_id=((pl_.c + k) % pl_.nctx, pl_.z), device_id_type=MESH
+            )
+            n += 1
+    if column:
+        for k in range(1, pl_.nz):
+            pl.semaphore_signal(bar, inc=1, device_id=(pl_.c, pl_.zto(k)), device_id_type=MESH)
+            n += 1
+    pl.semaphore_wait(bar, n)
+
+
+def rms(x, width):
+    return lax.rsqrt(jnp.sum(x * x, axis=-1, keepdims=True) * (1.0 / width) + EPS)
+
+
+def gain_row(extra, lane):
+    pick = (lax.broadcasted_iota(jnp.int32, (16, extra.shape[1]), 1) == lane).astype(BF16)
+    return dot_t(pick, extra)[0:1]
+
+
+def rope(x, cos, sin):
+    return x * cos + pltpu.roll(x, HEAD // 2, 1) * sin
+
+
+def attend_kernel(
+    cfg,
+    h_ref, g_ref, mask_ref, cos_ref, sin_ref, pa_ref, pb_ref, we_ref,
+    wa_out, wb_out, we_out, q_out, kv_out, lse_out, ob_out, xa_out, h1_out, xm_out, g_out, gt_out,
+    wa, wb, za, zb, hbuf, xa, qs, kv, obs, part, pget, lses, xms, gts, xmall, gall, gtall,
+    ssem, ra, rb, re, rza, rzb, rmisc, rkv, rxm, rxf,
+):
+    nctx, nz, width, rp, t0, heads, fc = cfg
+    pc = Place(nctx, nz)
+    nch = pc.nch
+    t2 = 2 * t0
+    qw = heads * HEAD
+    kw = qw + 2 * HEAD
+    dp = wa.shape[0]
+    snd = Sends(ssem, ssem.shape[0])
+    core, z, c, chip = pc.core, pc.z, pc.c, pc.chip
+    greet(pc)
+
+    for dz in range(1, nz):
+        snd.start(pa_ref, za.at[z], rza.at[dz], (c, pc.zto(dz)))
+    snd.start(h_ref, hbuf.at[core], rmisc.at[0], (pc.sib, z))
+    for dz in range(1, nz):
+        snd.start(pb_ref, zb.at[z], rzb.at[dz], (c, pc.zto(dz)))
+
+    def rows(cc, s, count=1):
+        return pl.ds(pl.multiple_of((cc * nz + s) * rp, 16), count * rp)
+
+    def spread(src, dst, rs, s):
+        here = dst.at[rows(c, s)]
+        sem = rs.at[c * nz + s]
+        snd.start(src.at[1 - core], here, sem, (pc.sib, z))
+        if pc.square:
+            chips = [pc.xchip(), pc.ychip()]
+        else:
+            chips = [(chip + k) % nch for k in range(1, nch)]
+        for q in chips:
+            for k in range(2):
+                snd.start(src.at[k], here, sem, (q * 2 + k, z))
+
+    def forward(dst, rs, s):
+        for source, to in ((pc.ychip() * 2, pc.xchip()), (pc.xchip() * 2 + 1, pc.ychip())):
+            here = dst.at[rows(source, s)]
+            sem = rs.at[source * nz + s]
+            arrived(here, sem)
+            snd.start(here, here, sem, (to * 2 + core, z))
+
+    def settle(dst, rs):
+        for k in range(1, nctx):
+            if pc.square:
+                continue
+            for s in range(nz):
+                cc = (c + k) % nctx
+                arrived(dst.at[rows(cc, s)], rs.at[cc * nz + s])
+        if pc.square:
+            xs, ys, ds = pc.xchip() * 2, pc.ychip() * 2, (3 - chip) * 2
+            for cc in (pc.sib, xs, ys + 1, ds, ds + 1):
+                for s in range(nz):
+                    arrived(dst.at[rows(cc, s)], rs.at[cc * nz + s])
+
+    own_a = snd.local(pa_ref.at[core], wa.at[rows(c, z)])
+    own_b = snd.local(pb_ref.at[core], wb.at[rows(c, z)])
+    spread(pa_ref, wa, ra, z)
+    keep = [own_a, own_b]
+    for dz in range(1, nz):
+        s = pc.zfrom(dz)
+        arrived(za.at[s], rza.at[dz])
+        spread(za.at[s], wa, ra, s)
+        keep.append(snd.local(za.at[s, core], wa.at[rows(c, s)]))
+        if pc.square:
+            forward(wa, ra, pc.zfrom(dz - 1))
+    if pc.square:
+        forward(wa, ra, pc.zfrom(nz - 1))
+    spread(pb_ref, wb, rb, z)
+    for dz in range(1, nz):
+        s = pc.zfrom(dz)
+        arrived(zb.at[s], rzb.at[dz])
+        spread(zb.at[s], wb, rb, s)
+        keep.append(snd.local(zb.at[s, core], wb.at[rows(c, s)]))
+    gall[z, core] = g_ref[...]
+    for dz in range(1, nz):
+        snd.start(g_ref, gall.at[z, core], rxm.at[dz], (c, pc.zto(dz)))
+    snd.start(g_ref, gall.at[z, core], rxf.at[0], (pc.sib, z))
+
+    hbuf[core] = h_ref[...]
+    arrived(hbuf.at[1 - core], rmisc.at[0])
+    for cp in keep:
+        cp.wait()
+    settle(wa, ra)
+    extra = wa[:, kw:]
+    ga = gain_row(extra, 8)
+    gm = gain_row(extra, 9)
+    for k in range(2):
+        hk = hbuf[k].astype(F32)
+        xa[pl.ds(k * t0, t0)] = (hk * rms(hk, width) * ga).astype(BF16)
+    cos, sin = cos_ref[...], sin_ref[...]
+    mine = pl.ds(pl.multiple_of(chip * t2, t2), t2)
+    xav = xa[...]
+    kraw = dot(xav, wa[:, qw:kw])
+    kv[mine, 0:HEAD] = rope(kraw[:, :HEAD], cos, sin).astype(BF16)
+    kv[mine, HEAD:] = kraw[:, HEAD:].astype(BF16)
+    for k in range(1, nch):
+        snd.start(kv.at[mine], kv.at[mine], rkv.at[k], (((chip + k) % nch) * 2 + core, z))
+    for hd in range(heads):
+        cols = slice(hd * HEAD, (hd + 1) * HEAD)
+        qs[:, cols] = rope(dot(xav, wa[:, cols]), cos, sin).astype(BF16)
+    if pc.square:
+        for dz in range(nz):
+            forward(wb, rb, pc.zfrom(dz))
+    def mats(m, cc):
+        per = nz * rp
+        return we_out.at[m, pl.ds(pl.multiple_of(cc * per, 16), per)]
+
+    own_e = [snd.local(we_ref.at[core, m], mats(m, c)) for m in range(3)]
+    for m in range(3):
+        here = mats(m, c)
+        sem = re.at[m * nctx + c]
+        for k in range(1, nch):
+            q = (chip + k) % nch
+            for half in range(2):
+                snd.start(we_ref.at[half, m], here, sem, (q * 2 + half, z))
+        snd.start(we_ref.at[1 - core, m], here, sem, (pc.sib, z))
+    for k in range(1, nch):
+        other = pl.ds(pl.multiple_of(((chip + nch - k) % nch) * t2, t2), t2)
+        arrived(kv.at[other], rkv.at[k])
+
+    keys = nch * t2
+    scale = HEAD ** -0.5
+    ok = lax.broadcasted_iota(jnp.int32, (t2, keys), 1) <= (
+        chip * t2 + lax.broadcasted_iota(jnp.int32, (t2, keys), 0)
+    )
+
+    lane = lax.broadcasted_iota(jnp.int32, (t2, 128), 1)
+    lses[...] = jnp.zeros((t2, 128), F32)
+
+    def one_head(hd, carry):
+        cols = pl.ds(pl.multiple_of(hd * HEAD, HEAD), HEAD)
+        s = dot_t(qs[:, cols], kv[:, 0:HEAD]) * scale
+        s = jnp.where(ok, s, -1e30)
+        m = jnp.max(s, axis=-1, keepdims=True)
+        e = jnp.exp(s - m)
+        total = jnp.sum(e, axis=-1, keepdims=True)
+        lses[...] = jnp.where(lane == hd, m + jnp.log(total), lses[...])
+        p = (e * (1.0 / total)).astype(BF16)
+        obs[:, cols] = dot(p, kv[:, HEAD:]).astype(BF16)
+        return carry
+
+    lax.fori_loop(0, heads, one_head, 0)
+    settle(wb, rb)
+    acc = dot_t(obs[...], wb[...])
+    for k in range(2):
+        part[k] = acc[k * t0:(k + 1) * t0]
+    snd.start(part.at[1 - core], pget, rmisc.at[1], (pc.sib, z))
+    arrived(pget, rmisc.at[1])
+    h1 = h_ref[...].astype(F32) + part[core] + pget[...]
+    h1_out[...] = h1
+    xm = (h1 * rms(h1, width) * gm).astype(BF16)
+    xms[...] = xm
+    logits = jnp.where(mask_ref[...] > 0.0, dot(xm, extra), -1e30)
+    top = jnp.max(logits, axis=-1, keepdims=True)
+    e = jnp.where(mask_ref[...] > 0.0, jnp.exp(logits - top), 0.0)
+    gts[...] = e / jnp.sum(e, axis=-1, keepdims=True)
+    for dz in range(1, nz):
+        to = (c, pc.zto(dz))
+        snd.start(xms, xmall.at[z, core], rxm.at[nz + dz], to)
+        snd.start(gts, gtall.at[z, core], rxm.at[2 * nz + dz], to)
+    snd.start(xms, xmall.at[z, core], rxf.at[nz], (pc.sib, z))
+    snd.start(gts, gtall.at[z, core], rxf.at[2 * nz], (pc.sib, z))
+    xmall[z, core] = xm
+    gtall[z, core] = gts[...]
+    outs = [
+        snd.local(wa, wa_out), snd.local(wb, wb_out), snd.local(kv, kv_out), snd.local(qs, q_out),
+        snd.local(lses, lse_out), snd.local(obs, ob_out), snd.local(xa, xa_out),
+    ]
+    for dz in range(1, nz):
+        s = pc.zfrom(dz)
+        for i, buf in enumerate((gall, xmall, gtall)):
+            here = buf.at[s, core]
+            arrived(here, rxm.at[i * nz + dz])
+            snd.start(here, here, rxf.at[i * nz + dz], (pc.sib, z))
+    for dz in range(nz):
+        s = pc.zfrom(dz)
+        for i, buf in enumerate((gall, xmall, gtall)):
+            arrived(buf.at[s, 1 - core], rxf.at[i * nz + dz])
+    outs += [snd.local(xmall, xm_out), snd.local(gall, g_out), snd.local(gtall, gt_out)]
+    for m in range(3):
+        for k in range(1, nctx):
+            cc = (c + k) % nctx
+            arrived(mats(m, cc), re.at[m * nctx + cc])
+    for cp in outs + own_e:
+        cp.wait()
+    snd.drain()
+
+
+def attend_call(cfg, h, g, mask, cos, sin, pa, pb, we):
+    nctx, nz, width, rp, t0, heads, fc = cfg
+    nch, t2, dp = nctx // 2, 2 * t0, nctx * nz * rp
+    ca, cb = pa.shape[2], pb.shape[2]
+    keys = nch * t2
+    vm = pl.BlockSpec(memory_space=pltpu.VMEM)
+    hb = pl.BlockSpec(memory_space=pltpu.HBM)
+    sds = jax.ShapeDtypeStruct
+    nsend = 4 * nz + 2 * nz * (2 * nctx) + 3 * nctx + 8 * nz + 40 + nch
+    dma = pltpu.SemaphoreType.DMA
+    return pl.pallas_call(
+        functools.partial(attend_kernel, cfg),
+        out_shape=(
+            sds((dp, ca), BF16), sds((dp, cb), BF16), sds((3, dp, fc), BF16),
+            sds((t2, heads * HEAD), BF16), sds((keys, 2 * HEAD), BF16), sds((t2, 128), F32),
+            sds((t2, heads * HEAD), BF16), sds((t2, dp), BF16), sds((t0, dp), F32),
+            sds((nz, 2, t0, dp), BF16), sds((nz, 2, t0, dp), BF16), sds((nz, 2, t0, 128), F32),
+        ),
+        in_specs=[vm, vm, vm, vm, vm, vm, vm, hb],
+        out_specs=(hb, hb, hb, hb, hb, hb, hb, hb, vm, hb, hb, hb),
+        scratch_shapes=[
+            pltpu.VMEM((dp, ca), BF16), pltpu.VMEM((dp, cb), BF16),
+            pltpu.VMEM((nz, 2, rp, ca), BF16), pltpu.VMEM((nz, 2, rp, cb), BF16),
+            pltpu.VMEM((2, t0, dp), BF16), pltpu.VMEM((t2, dp), BF16),
+            pltpu.VMEM((t2, heads * HEAD), BF16), pltpu.VMEM((keys, 2 * HEAD), BF16),
+            pltpu.VMEM((t2, heads * HEAD), BF16),
+            pltpu.VMEM((2, t0, dp), F32), pltpu.VMEM((t0, dp), F32),
+            pltpu.VMEM((t2, 128), F32), pltpu.VMEM((t0, dp), BF16), pltpu.VMEM((t0, 128), F32),
+            pltpu.VMEM((nz, 2, t0, dp), BF16), pltpu.VMEM((nz, 2, t0, dp), BF16),
+            pltpu.VMEM((nz, 2, t0, 128), F32),
+            dma((nsend,)), dma((nctx * nz,)), dma((nctx * nz,)), dma((3 * nctx,)),
+            dma((nz,)), dma((nz,)), dma((2,)), dma((nch,)), dma((3 * nz,)), dma((3 * nz,)),
+        ],
+        compiler_params=pltpu.CompilerParams(
+            collective_id=0, has_side_effects=True, vmem_limit_bytes=60 * 2**20
+        ),
+        name="attend",
+    )(h, g, mask, cos, sin, pa, pb, we)
+
+
+def prepare(hidden, routes, cot, na, wq, wk, wv, wo, nm, wr, wg, wu, wd):
+    nctx, nz = lax.axis_size("ctx"), lax.axis_size("wsh")
+    t0, width = hidden.shape[1], hidden.shape[2]
+    r = wq.shape[1]
+    rp = -(-r // 16) * 16
+    ndev = nctx * nz
+    eloc, ff = wg.shape[2], wg.shape[3]
+    half = wq.shape[2] // 2
+    heads = half // HEAD
+    fc = eloc * ff // 2
+
+    def pad_features(x):
+        if rp == r:
+            return x
+        x = x.reshape(x.shape[0], ndev, r)
+        return jnp.pad(x, ((0, 0), (0, 0), (0, rp - r))).reshape(x.shape[0], ndev * rp)
+
+    def pad_rows(x):
+        return jnp.pad(x, ((0, rp - r), (0, 0))) if rp != r else x
+
+    def expert(w):
+        w = w.reshape(nz * r, eloc * ff)
+        if rp != r:
+            w = jnp.pad(w.reshape(nz, r, -1), ((0, 0), (0, rp - r), (0, 0))).reshape(nz * rp, -1)
+        return jnp.stack([w[:, :fc], w[:, fc:]])
+
+    h = pad_features(hidden[0])
+    g = pad_features(cot[0].astype(BF16))
+    experts = wr.shape[2]
+    extra = jnp.concatenate(
+        [wr[0], na[0][:, None], nm[0][:, None], jnp.zeros((r, 128 - experts - 2), BF16)], axis=1
+    )
+    pa = jnp.stack([
+        pad_rows(jnp.concatenate([
+            wq[0][:, k * half:(k + 1) * half], wk[0][:, k * HEAD:(k + 1) * HEAD],
+            wv[0][:, k * HEAD:(k + 1) * HEAD], extra], axis=1))
+        for k in range(2)])
+    pb = jnp.stack([pad_rows(wo[0][:, :half]), pad_rows(wo[0][:, half:])])
+    we = jnp.stack([expert(wg[0]), expert(wu[0]), expert(wd[0])], axis=1)
+    lanes = jnp.arange(128, dtype=jnp.int32)
+    mask = jnp.max((routes[0, 0][:, :, None] == lanes[None, None, :]).astype(F32), axis=1)
+    chip = lax.axis_index("ctx") // 2
+    pos = chip * 2 * t0 + jnp.arange(2 * t0, dtype=jnp.int32)
+    freq = BASE ** (-jnp.arange(HEAD // 2, dtype=F32) * 2.0 / HEAD)
+    ang = pos.astype(F32)[:, None] * freq[None, :]
+    cos, sin = jnp.cos(ang), jnp.sin(ang)
+    cosf = jnp.concatenate([cos, cos], axis=1)
+    sinf = jnp.concatenate([-sin, sin], axis=1)
+    cfg = (nctx, nz, width, rp, t0, heads, fc)
+    return cfg, h, g, mask, cosf, sinf, pa, pb, we
+
+class Reduce:
+    def __init__(self, pc, snd, slab, first, fx, fy, sems):
+        self.pc, self.snd, self.slab = pc, snd, slab
+        self.first, self.fx, self.fy, self.sems = first, fx, fy, sems
+        self.x, self.y, self.d = pc.xchip(), pc.ychip(), 3 - pc.chip
+
+    def to(self, chip):
+        return (chip * 2 + self.pc.core, self.pc.z)
+
+    def diagonal(self):
+        self.snd.start(self.slab(self.d, 0), self.first.at[0], self.sems.at[0], self.to(self.x))
+        self.snd.start(self.slab(self.d, 1), self.first.at[1], self.sems.at[1], self.to(self.y))
+
+    def straight_x(self):
+        self.snd.start(self.slab(self.x, 0), self.fx.at[0], self.sems.at[2], self.to(self.x))
+
+    def straight_y(self):
+        self.snd.start(self.slab(self.y, 1), self.fy.at[1], self.sems.at[5], self.to(self.y))
+
+    def merge(self, add):
+        arrived(self.first.at[0], self.sems.at[0])
+        add(self.slab(self.y, 0), self.first.at[0])
+        self.snd.start(self.slab(self.y, 0), self.fy.at[0], self.sems.at[4], self.to(self.y))
+        arrived(self.first.at[1], self.sems.at[1])
+        add(self.slab(self.x, 1), self.first.at[1])
+        self.snd.start(self.slab(self.x, 1), self.fx.at[1], self.sems.at[3], self.to(self.x))
+
+    def wait(self):
+        for w in range(2):
+            arrived(self.fx.at[w], self.sems.at[2 + w])
+            arrived(self.fy.at[w], self.sems.at[4 + w])
+
+
+def add_into(dst, src):
+    dst[...] = (dst[...].astype(F32) + src[...].astype(F32)).astype(BF16)
+
+
+def back_kernel(
+    cfg,
+    wa_in, wb_in, we_in, q_in, kv_in, lse_in, ob_in, xa_in, h1_in, xm_in, g_in, gt_in,
+    h_ref, cot_ref, cos_ref, sin_ref,
+    out_ref, ig_ref, eg_out, da_out, db_out, efirst, efx, efy,
+    wa, wb, we, qs, kv, lses, obs, xa, h1s, xm, gr, gts,
+    ggu, ap, keep, sibs, sibr, zr, okeep, ozr, kgg, sgg, rgg, zgg,
+    gat, gkv, gkvb, gkvr, graw, part, pget, exts,
+    esibr,
+    afirst, afx, afy, bfirst, bfx, bfy, zra, zrb, fa, fb, fra, frb, rowp,
+    ssem, lsem, sib_s, sib_r, z_s, z_r, osib_s, osib_r, oz_s, oz_r, rmisc, esem, asem, bsem,
+    rkv, rza, rzb,
+):
+    nctx, nz, width, rp, t0, heads, fc = cfg
+    pc = Place(nctx, nz)
+    nch = pc.nch
+    t2 = 2 * t0
+    qw = heads * HEAD
+    kw = qw + 2 * HEAD
+    dp = wa.shape[0]
+    core, z, c, chip = pc.core, pc.z, pc.c, pc.chip
+    per = nz * rp
+    snd = Sends(ssem, ssem.shape[0])
+    loads = Sends(lsem, lsem.shape[0])
+    sib = (pc.sib, z)
+
+    def slab_rows(q, w):
+        return pl.ds(pl.multiple_of((q * 2 + w) * per, 16), per)
+
+    l_we = [loads.local(we_in.at[m], we.at[m]) for m in range(3)]
+    l_xm = loads.local(xm_in, xm)
+    l_gr = loads.local(g_in, gr)
+    l_gt = loads.local(gt_in, gts)
+    later = [
+        loads.local(a, b)
+        for a, b in (
+            (wb_in, wb), (h1_in, h1s), (wa_in, wa), (ob_in, obs), (q_in, qs), (kv_in, kv),
+            (lse_in, lses), (xa_in, xa),
+        )
+    ]
+    greet(pc)
+    for cp in l_we + [l_xm, l_gr, l_gt]:
+        cp.wait()
+
+    eloc = cfg_eloc(cfg)
+    mine_e = z * eloc + (core * eloc) // 2
+    lane = lax.broadcasted_iota(jnp.int32, (t2, 128), 1)
+    mine0 = pl.ds(pl.multiple_of(core * t0, t0), t0)
+    sib0 = pl.ds(pl.multiple_of((1 - core) * t0, t0), t0)
+
+    def zof(i):
+        return (z + 1 + i) % nz
+
+    def blk(i):
+        return pl.ds(pl.multiple_of(zof(i) * t2, t2), t2)
+
+    def copy_to_sib(src, dst, ss, rs):
+        return pltpu.make_async_remote_copy(
+            src_ref=src, dst_ref=dst, send_sem=ss, recv_sem=rs, device_id=sib, device_id_type=MESH
+        )
+
+    def copy_to_z(i, src, dst, ss, rs):
+        return pltpu.make_async_remote_copy(
+            src_ref=src, dst_ref=dst, send_sem=ss, recv_sem=rs, device_id=(c, zof(i)),
+            device_id_type=MESH,
+        )
+
+    def g_copies(i):
+        return (
+            copy_to_sib(sibs.at[i], sibr.at[i], sib_s.at[i], sib_r.at[i]),
+            copy_to_sib(sgg.at[i], rgg.at[i], sib_s.at[nz + i], sib_r.at[nz + i]),
+        )
+
+    def gz_copies(i):
+        return (
+            copy_to_z(i, keep.at[i], zr.at[i], z_s.at[i], z_r.at[i]),
+            copy_to_z(i, kgg.at[i], zgg.at[i], z_s.at[nz + i], z_r.at[nz + i]),
+        )
+
+    def g_settle(i):
+        for cp in g_copies(i):
+            cp.wait()
+        keep[i] = (keep[i].astype(F32) + sibr[i].astype(F32)).astype(BF16)
+        kgg[i] = kgg[i] + rgg[i]
+
+    def rows_back(i, carry):
+        x = xm[blk(i)]
+        g = gr[blk(i)]
+        gate = jnp.sum(jnp.where(lane == mine_e, gts[blk(i)], 0.0), axis=1, keepdims=True)
+        pre = dot(x, we[0])
+        up = dot(x, we[1])
+        ga0 = dot(g, we[2])
+        sg = 1.0 / (1.0 + jnp.exp(-pre))
+        silu = pre * sg
+        act = silu * up
+        ggc = jnp.sum(act * ga0, axis=1, keepdims=True)
+        ggl = jnp.where(lane == mine_e, ggc, 0.0)
+        gact = gate * ga0
+        gg = (gact * up * sg * (1.0 + pre * (1.0 - sg))).astype(BF16)
+        gu = (gact * silu).astype(BF16)
+        ap[blk(i)] = (gate * act).astype(BF16)
+        ggu[blk(i), 0:fc] = gg
+        ggu[blk(i), fc:] = gu
+        gb = (dot_t(gg, we[0]) + dot_t(gu, we[1])).astype(BF16)
+        part[0:t0] = gb[:t0].astype(F32)
+        part[t0:] = gb[t0:].astype(F32)
+        keep[i] = part[mine0].astype(BF16)
+        sibs[i] = part[sib0].astype(BF16)
+        rowp[...] = ggl
+        kgg[i] = rowp[mine0]
+        sgg[i] = rowp[sib0]
+        for cp in g_copies(i):
+            cp.start()
+
+        @pl.when(i > 0)
+        def _():
+            g_settle(i - 1)
+            for cp in gz_copies(i - 1):
+                cp.start()
+
+        return carry
+
+    lax.fori_loop(0, nz, rows_back, 0)
+    g_settle(nz - 1)
+
+    def o_copy(i):
+        return copy_to_sib(sibs.at[i], sibr.at[i], osib_s.at[i], osib_r.at[i])
+
+    def oz_copy(i):
+        return copy_to_z(i, okeep.at[i], ozr.at[i], oz_s.at[i], oz_r.at[i])
+
+    def o_settle(i):
+        o_copy(i).wait()
+        okeep[i] = (okeep[i].astype(F32) + sibr[i].astype(F32)).astype(BF16)
+
+    def rows_out(i, carry):
+        part[...] = dot_t(ap[blk(i)], we[2])
+        okeep[i] = part[mine0].astype(BF16)
+        sibs[i] = part[sib0].astype(BF16)
+        o_copy(i).start()
+
+        @pl.when(i > 0)
+        def _():
+            o_settle(i - 1)
+            oz_copy(i - 1).start()
+
+        return carry
+
+    lax.fori_loop(0, nz, rows_out, 0)
+    o_settle(nz - 1)
+
+    ers = Reduce(pc, snd, lambda q, w: we.at[:, slab_rows(q, w)], efirst, efx, efy, esem)
+
+    for n, q in enumerate((ers.d, ers.x, ers.y, chip)):
+        cols = pl.ds(pl.multiple_of(q * 2 * per, 128), 2 * per)
+        gw = t_dot(xm[:, cols], ggu[...])
+        we[0, cols] = gw[:, :fc].astype(BF16)
+        we[1, cols] = gw[:, fc:].astype(BF16)
+        we[2, cols] = t_dot(gr[:, cols], ap[...]).astype(BF16)
+        if n == 0:
+            ers.diagonal()
+        elif n == 1:
+            ers.straight_x()
+        elif n == 2:
+            ers.straight_y()
+
+    for cp in later:
+        cp.wait()
+    gsum = keep[nz - 1].astype(F32)
+    ggs = kgg[nz - 1]
+    for i in range(nz - 1):
+        arrived(zr.at[i], z_r.at[i])
+        arrived(zgg.at[i], z_r.at[nz + i])
+        gsum = gsum + zr[i].astype(F32)
+        ggs = ggs + zgg[i]
+    own = pl.ds(pl.multiple_of(z * t2 + core * t0, t0), t0)
+    gate = gts[own]
+    glog = (gate * (ggs - jnp.sum(gate * ggs, axis=1, keepdims=True))).astype(BF16)
+    extra = wa[:, kw:]
+    gain_a = gain_row(extra, 8)
+    gain_m = gain_row(extra, 9)
+    gxm = gsum + dot_t(glog, extra)
+    h1 = h1s[...]
+    r = rms(h1, width)
+    n = h1 * r
+    gy = gxm * gain_m
+    g1 = cot_ref[...] + r * (gy - n * (jnp.sum(gy * n, axis=1, keepdims=True) * (1.0 / width)))
+    lane0 = lax.broadcasted_iota(jnp.int32, (t0, 128), 1)
+    ext = t_dot(xm[own], glog) + t_dot((gxm * n).astype(BF16), (lane0 == 9).astype(BF16))
+    exts[...] = ext
+    ig_ref[...] = g1
+    gat[mine0] = g1.astype(BF16)
+    snd.start(gat.at[mine0], gat.at[mine0], rmisc.at[0], sib)
+    arrived(gat.at[sib0], rmisc.at[0])
+    gav = gat[...]
+    go = dot(gav, wb[...]).astype(BF16)
+    brs = Reduce(pc, snd, lambda q, w: wb.at[slab_rows(q, w)], bfirst, bfx, bfy, bsem)
+
+    def out_grads(k, carry):
+        cols = pl.ds(pl.multiple_of(k * 2 * per, 128), 2 * per)
+        wb[cols] = t_dot(gat[:, cols], obs[...]).astype(BF16)
+        return carry
+
+    lax.fori_loop(0, nch, out_grads, 0)
+    obs[...] = go
+
+    keys = nch * t2
+    scale = HEAD ** -0.5
+    ok = lax.broadcasted_iota(jnp.int32, (t2, keys), 1) <= (
+        chip * t2 + lax.broadcasted_iota(jnp.int32, (t2, keys), 0)
+    )
+    cos, sin = cos_ref[...], sin_ref[...]
+    gkv[...] = jnp.zeros(gkv.shape, F32)
+
+    def one_head(hd, carry):
+        cols = pl.ds(pl.multiple_of(hd * HEAD, HEAD), HEAD)
+        s = dot_t(qs[:, cols], kv[:, 0:HEAD]) * scale
+        pe = jnp.where(ok, jnp.exp(s - jnp.sum(jnp.where(lane == hd, lses[...], 0.0), axis=1, keepdims=True)), 0.0)
+        gp = dot_t(obs[:, cols], kv[:, HEAD:])
+        delta = jnp.sum(pe * gp, axis=-1, keepdims=True)
+        gs = (pe * (gp - delta)).astype(BF16)
+        gq = dot(gs, kv[:, 0:HEAD]) * scale
+        graw[:, cols] = rope(gq, cos, -sin).astype(BF16)
+        gkv[:, 0:HEAD] += t_dot(gs, qs[:, cols])
+        gkv[:, HEAD:] += t_dot(pe.astype(BF16), obs[:, cols])
+        return carry
+
+    lax.fori_loop(0, heads, one_head, 0)
+    def fetch(src, room, col):
+        spot = [
+            room.at[pl.ds(m * per, per), pl.ds(col * fc, fc)] for m in range(3)
+        ]
+        cps = [loads.local(src.at[m], spot[m]) for m in range(3)]
+        return spot, cps
+
+    def add_mats(dst, src):
+        spot, cps = fetch(src, gr, 0)
+        for cp in cps:
+            cp.wait()
+        for m in range(3):
+            dst[m] = (dst[m].astype(F32) + spot[m][...].astype(F32)).astype(BF16)
+
+    ers.merge(add_mats)
+    mine = pl.ds(pl.multiple_of(chip * t2, t2), t2)
+    gkvb[...] = gkv[...].astype(BF16)
+    for k in range(1, nch):
+        q = (chip + k) % nch
+        snd.start(
+            gkvb.at[pl.ds(pl.multiple_of(q * t2, t2), t2)], gkvr.at[k - 1], rkv.at[k],
+            (q * 2 + core, z),
+        )
+    brs.diagonal()
+    brs.straight_x()
+    brs.straight_y()
+    gk = gkv[mine]
+    for k in range(1, nch):
+        arrived(gkvr.at[k - 1], rkv.at[k])
+        gk = gk + gkvr[k - 1].astype(F32)
+    graw[:, qw:qw + HEAD] = rope(gk[:, :HEAD] * scale, cos, -sin).astype(BF16)
+    graw[:, qw + HEAD:] = gk[:, HEAD:].astype(BF16)
+    part[...] = dot_t(graw[...], wa[:, :kw])
+    pget_src = part.at[sib0]
+    snd.start(pget_src, pget, rmisc.at[1], sib)
+    ars = Reduce(pc, snd, lambda q, w: wa.at[slab_rows(q, w)], afirst, afx, afy, asem)
+
+    def in_grads(k, carry):
+        cols = pl.ds(pl.multiple_of(k * 2 * per, 128), 2 * per)
+        wa[cols, 0:kw] = t_dot(xa[:, cols], graw[...]).astype(BF16)
+        return carry
+
+    lax.fori_loop(0, nch, in_grads, 0)
+    arrived(pget, rmisc.at[1])
+    gxa = part[mine0] + pget[...]
+    h = h_ref[...].astype(F32)
+    r = rms(h, width)
+    n = h * r
+    gy = gxa * gain_a
+    ig_ref[...] += r * (gy - n * (jnp.sum(gy * n, axis=1, keepdims=True) * (1.0 / width)))
+    wa[:, kw:] = (
+        exts[...] + t_dot((gxa * n).astype(BF16), (lane0 == 8).astype(BF16))
+    ).astype(BF16)
+    ars.diagonal()
+    ars.straight_x()
+    ars.straight_y()
+    brs.merge(add_into)
+
+    osum = okeep[nz - 1].astype(F32) + h1s[...]
+    for i in range(nz - 1):
+        arrived(ozr.at[i], oz_r.at[i])
+        osum = osum + ozr[i].astype(F32)
+    out_ref[...] = osum
+
+    ers.wait()
+    got = [
+        fetch(src.at[w], room, w) for src, room in ((efx, gr), (efy, xm)) for w in range(2)
+    ]
+    for _, cps in got:
+        for cp in cps:
+            cp.wait()
+    for w in range(2):
+        for m in range(3):
+            tot = we[m, slab_rows(chip, w)].astype(F32)
+            tot = tot + got[w][0][m][...].astype(F32) + got[2 + w][0][m][...].astype(F32)
+            we[m, slab_rows(chip, w)] = tot.astype(BF16)
+    snd.start(ers.slab(chip, 1 - core), esibr, rmisc.at[2], sib)
+    e_own = loads.local(ers.slab(chip, core), eg_out.at[core])
+
+    ars.merge(add_into)
+    zs = []
+    def own_piece(q, w):
+        return pl.ds(pl.multiple_of((c - core + w) * per + q * rp, 16), rp)
+
+    for rs, buf, fx, fy, zrecv, rz in (
+        (brs, wb, bfx, bfy, zrb, rzb), (ars, wa, afx, afy, zra, rza)
+    ):
+        rs.wait()
+        for w in range(2):
+            buf[slab_rows(chip, w)] = (
+                buf[slab_rows(chip, w)].astype(F32) + fx[w].astype(F32) + fy[w].astype(F32)
+            ).astype(BF16)
+        for dz in range(1, nz):
+            q = pc.zto(dz)
+            for w in range(2):
+                snd.start(
+                    buf.at[own_piece(q, w)], zrecv.at[dz - 1, w], rz.at[2 * dz + w], (c, q)
+                )
+    arrived(esibr, rmisc.at[2])
+    e_sib = loads.local(esibr, eg_out.at[1 - core])
+    for k, (buf, zrecv, rz, fin, get) in enumerate(
+        ((wb, zrb, rzb, fb, frb), (wa, zra, rza, fa, fra))
+    ):
+        for w in range(2):
+            tot = buf[own_piece(z, w)].astype(F32)
+            for dz in range(1, nz):
+                arrived(zrecv.at[dz - 1, w], rz.at[2 * dz + w])
+                tot = tot + zrecv[dz - 1, w].astype(F32)
+            fin[w] = tot
+        snd.start(fin.at[1 - core], get, rmisc.at[3 + k], sib)
+    arrived(frb, rmisc.at[3])
+    db_out[core] = fb[core]
+    db_out[1 - core] = frb[...]
+    arrived(fra, rmisc.at[4])
+    da_out[core] = fa[core]
+    da_out[1 - core] = fra[...]
+    e_own.wait()
+    e_sib.wait()
+    for i in range(nz - 1):
+        for cp in gz_copies(i):
+            cp.wait_send()
+        oz_copy(i).wait_send()
+    snd.drain()
+
+
+def cfg_eloc(cfg):
+    return 2
+
+
+def back_call(cfg, wa, wb, we, q, kv, lse, ob, xa, h1, xm, g, gt, h, cot, cos, sin):
+    nctx, nz, width, rp, t0, heads, fc = cfg
+    nch, t2, dp = nctx // 2, 2 * t0, nctx * nz * rp
+    ca, cb = wa.shape[1], wb.shape[1]
+    keys = nch * t2
+    rows = nz * t2
+    per = nz * rp
+    vm = pl.BlockSpec(memory_space=pltpu.VMEM)
+    hb = pl.BlockSpec(memory_space=pltpu.HBM)
+    sds = jax.ShapeDtypeStruct
+    dma = pltpu.SemaphoreType.DMA
+    v = pltpu.VMEM
+    return pl.pallas_call(
+        functools.partial(back_kernel, cfg),
+        out_shape=(
+            sds((t0, dp), F32), sds((t0, dp), F32), sds((2, 3, per, fc), BF16),
+            sds((2, rp, ca), F32), sds((2, rp, cb), F32),
+        ) + (sds((2, 3, per, fc), BF16),) * 3,
+        in_specs=[hb] * 12 + [vm] * 4,
+        out_specs=(vm, vm, hb, vm, vm, hb, hb, hb),
+        scratch_shapes=[
+            v((dp, ca), BF16), v((dp, cb), BF16), v((3, dp, fc), BF16),
+            v((t2, heads * HEAD), BF16), v((keys, 2 * HEAD), BF16), v((t2, 128), F32),
+            v((t2, heads * HEAD), BF16), v((t2, dp), BF16), v((t0, dp), F32),
+            v((rows, dp), BF16), v((rows, dp), BF16), v((rows, 128), F32),
+            v((rows, 2 * fc), BF16), v((rows, fc), BF16),
+            v((nz, t0, dp), BF16), v((nz, t0, dp), BF16), v((nz, t0, dp), BF16),
+            v((nz - 1, t0, dp), BF16),
+            v((nz, t0, dp), BF16), v((nz - 1, t0, dp), BF16),
+            v((nz, t0, 128), F32), v((nz, t0, 128), F32), v((nz, t0, 128), F32),
+            v((nz - 1, t0, 128), F32),
+            v((t2, dp), BF16), v((keys, 2 * HEAD), F32), v((keys, 2 * HEAD), BF16),
+            v((nch - 1, t2, 2 * HEAD), BF16), v((t2, ca - 128), BF16),
+            v((t2, dp), F32), v((t0, dp), F32), v((dp, 128), F32),
+            v((3, per, fc), BF16),
+            v((2, per, ca), BF16), v((2, per, ca), BF16), v((2, per, ca), BF16),
+            v((2, per, cb), BF16), v((2, per, cb), BF16), v((2, per, cb), BF16),
+            v((nz - 1, 2, rp, ca), BF16), v((nz - 1, 2, rp, cb), BF16),
+            v((2, rp, ca), F32), v((2, rp, cb), F32), v((rp, ca), F32), v((rp, cb), F32),
+            v((t2, 128), F32),
+            dma((60,)), dma((40,)), dma((2 * nz,)), dma((2 * nz,)), dma((2 * nz,)), dma((2 * nz,)),
+            dma((nz,)), dma((nz,)), dma((nz,)), dma((nz,)), dma((5,)), dma((6,)), dma((6,)),
+            dma((6,)), dma((nch,)), dma((2 * nz,)), dma((2 * nz,)),
+        ],
+        compiler_params=pltpu.CompilerParams(
+            collective_id=1, has_side_effects=True, vmem_limit_bytes=64 * 2**20
+        ),
+        name="back",
+    )(wa, wb, we, q, kv, lse, ob, xa, h1, xm, g, gt, h, cot, cos, sin)
+
+
+def body(hidden, routes, cot, na, wq, wk, wv, wo, nm, wr, wg, wu, wd):
+    cfg, h, g, mask, cos, sin, pa, pb, we = prepare(
+        hidden, routes, cot, na, wq, wk, wv, wo, nm, wr, wg, wu, wd
+    )
+    nctx, nz, width, rp, t0, heads, fc = cfg
+    t2, dp = 2 * t0, nctx * nz * rp
+    r = attend_call(cfg, h, g, mask, cos, sin, pa, pb, we)
+    wa, wb, wf, q, kv, lse, ob, xa, h1, xm, gall, gt = r
+    xm = xm.reshape(nz * t2, dp)
+    gall = gall.reshape(nz * t2, dp)
+    gt = gt.reshape(nz * t2, 128)
+    out, ig, eg, da, db, *_ = back_call(
+        cfg, wa, wb, wf, q, kv, lse, ob, xa, h1, xm, gall, gt, h, cot[0], cos, sin
+    )
+    qw = heads * HEAD
+    kw = qw + 2 * HEAD
+    ext = da[0, :, kw:] + da[1, :, kw:]
+    both = lambda x, lo, hi: jnp.concatenate([x[0, :, lo:hi], x[1, :, lo:hi]], axis=1)[None]
+    eg = jnp.transpose(eg.astype(F32), (1, 2, 0, 3))
+    experts = wr.shape[2]
+    return (
+        out[None], ig[None], ext[:, 8][None], both(da, 0, qw), both(da, qw, qw + HEAD),
+        both(da, qw + HEAD, kw), both(db, 0, qw), ext[:, 9][None], ext[:, :experts][None],
+        eg[0][None], eg[1][None], eg[2][None],
+    )
 
 
 def shifted(value, axis, steps):
@@ -354,7 +1217,7 @@
     return (grad_after_attn + grad_before, layer_grads, expert_grads)
 
 
-def body(
+def plain_body(
     hidden_in,
     routes,
     cotangent,
@@ -441,7 +1304,7 @@
 
 def solution(mesh):
     return jax.shard_map(
-        body,
+        body if mesh.shape["ctx"] == 8 and mesh.shape["wsh"] == 4 else plain_body,
         mesh=mesh,
         in_specs=(
             P("wsh", "ctx", None),

time: 1430 us -> 364 us (0.25)
  waiting for transfers between devices: 680 us -> 0 us
  blocking collectives: 376 us -> 0 us
  Pallas kernels: 0 us -> 330 us
  local copies, waits for them, and re-layouts: 140 us -> 18 us
  matrix products: 107 us -> 0 us
  other arithmetic: 70.1 us -> 10.6 us
  starting transfers between devices: 28.7 us -> 0 us
  between operations: 16 us -> 0.83 us
    reduce_scatter x4 -> x0, waiting for transfers between devices: 482 us -> none  [the longest x1 142 us: backward_layer(): lax.psum_scatter(query_term, ('ctx', 'wsh'), scatter_dimension=0, tiled=T...]
    pallas_call x0 -> x2, Pallas kernels: none -> 330 us  [the longest x1 183 us: back_call(): pl.pallas_call(functools.partial(back_kernel, cfg), out_shape=(sds((t0, d...]
    all_gather x5 -> x0, blocking collectives: 298 us -> none  [the longest x1 125 us: body(): lax.all_gather(w_router[layer_number], ('ctx', 'wsh'), axis=0, tiled=True)]
    all_to_all x4 -> x0, waiting for transfers between devices: 108 us -> none  [the longest x1 55.7 us: forward_layer(): lax.all_to_all(produced, 'wsh', split_axis=0, concat_axis=0, tiled=True)]
    dot_general x29 -> x0, matrix products: 105 us -> none  [the longest x1 9.17 us: backward_layer(): jnp.einsum('sjcd,djf->sjcf', grad_arrived, down_w, preferred_element_type...]
    unnamed x2 -> x0, blocking collectives: 77.8 us -> none
    unnamed x13 -> x0, waiting for transfers between devices: 59.5 us -> none
    convert_element_type x8 -> x0, local copies, waits for them, and re-layouts: 48.8 us -> none  [the longest x3 37.7 us: backward_layer(): expert_grads = (lax.psum_scatter(jnp.einsum('sjcd,sjcf->djf', arrived, gr...]
  transfers between devices with their start and end apart: 23 -> 0, of which waited for: 15 -> 0; matrix products, arithmetic and copies ran while one was open for 21% -> 0% of each run, Pallas kernels for 0% -> 0%
where the time goes in v1:
time: 364 us; the launch traced here: 360 us
  Pallas kernels  330 us (91%)
  local copies, waits for them, and re-layouts  18 us (5%)
  other arithmetic  10.6 us (3%)
    pallas_call x1, Pallas kernels, back_call(): pl.pallas_call(functools.partial(back_kernel, cfg), out_shape=(sds((t0, d...  183 us
    pallas_call x1, Pallas kernels, attend_call(): pl.pallas_call(functools.partial(attend_kernel, cfg), out_shape=(sds((dp,...  147 us
    unnamed x24, local copies, waits for them, and re-layouts  10.4 us

profile of v1, /device:TPU:15, one launch (start us, length us, event | category | flops | bytes accessed | tf_op | source)
XLA Modules:
  0.0 359.6 jit_solution(16264344813341740343)
XLA Ops:
  0.7 0.8 copy.46
  1.5 0.8 copy.47
  2.3 0.8 copy.45
  3.0 0.8 fusion.3
  3.8 1.4 convert_reduce_fusion.mask_ref
  5.3 0.9 fusion.2
  6.4 0.7 pad_maximum_fusion.1.pa_ref
  7.1 0.9 slice_bitcast_fusion.11
  8.1 0.7 pad_maximum_fusion.2.pb_ref
  8.8 0.5 fusion
  9.3 0.8 pad_maximum_fusion.3
  10.1 0.8 bitcast_convert_fusion.g_ref
  11.6 0.9 copy-done.6
  12.6 1.4 pad_maximum_fusion.we_ref
  14.1 147.2 %attend.1 = (bf16[1536,1152]{1,0:T(8,128)(2,1)}, bf16[1536,768]{1,0:T(8,128)(2,1)}, bf16[3,1536,768]{2,1,0:T(8,128)(2,1)}, bf16[256,768]{1,0:T(8,128)(2,1)}, bf1...) custom-call(bf16[128,1536]{1,0:T(8,128)(2,1)} %bitcast.87, ...), custom_call_target="tpu_custom_call" | custom-call | tf_op jit(solution)/shard_map/attend/pallas_call | solution.py:327
  161.3 183.0 %back.1 = (f32[128,1536]{1,0:T(8,128)}, f32[128,1536]{1,0:T(8,128)}, bf16[2,3,192,768]{3,2,1,0:T(8,128)(2,1)}, f32[2,48,1152]{2,1,0:T(8,128)}, f32[2,48,768]{2,1...) custom-call(bf16[1536,1152]{1,0:T(8,128)(2,1)} %get-tuple-element.29, ...), custom_call_target="tpu_custom_call" | custom-call | tf_op jit(solution)/shard_map/back/pallas_call | solution.py:814
  344.3 1.0 slice_bitcast_fusion.14
  345.3 1.0 slice_bitcast_fusion.9
  346.3 0.7 maximum_bitcast_fusion.3
  347.0 0.6 maximum_bitcast_fusion.6
  347.6 0.7 slice_reduce_fusion
  348.3 0.7 copy.50
  349.0 0.6 maximum_bitcast_fusion.5
  349.6 1.0 slice_bitcast_fusion.7
  350.6 0.7 maximum_bitcast_fusion.4
  351.4 0.3 convert_bitcast_fusion
  351.7 0.4 fusion.1
  352.1 1.9 copy.53
  354.0 1.9 copy.52
  356.0 1.9 copy.51
  357.9 0.9 copy.59
  358.8 0.9 copy.60
  (27 shorter events, 1.0 us)
Async XLA Ops:
  0.6 9.5 %copy-start = (f32[1,128,1536]{2,1,0:T(8,128)S(1)}, f32[1,128,1536]{2,1,0:T(8,128)}, u32[]{:S(2)}) copy-start(f32[1,128,1536]{2,1,0:T(8,128)} %param.15) | copy-start | bytes 2359300
  6.3 4.6 %copy-start.4 = (bf16[1,192,2,768]{3,2,1,0:T(2,128)(2,1)S(1)}, bf16[1,192,2,768]{3,2,1,0:T(2,128)(2,1)}, u32[]{:S(2)}) copy-start(bf16[1,192,2,768]{3,2,1,0:T(2,128)(2,1)} %param.23) | copy-start | bytes 1769476
  10.1 1.2 copy-start.5
  11.4 1.1 copy-start.6
  344.3 7.1 %copy-start.1 = (bf16[2,3,192,768]{3,2,1,0:T(8,128)(2,1)S(1)}, bf16[2,3,192,768]{3,2,1,0:T(8,128)(2,1)}, u32[]{:S(2)}) copy-start(bf16[2,3,192,768]{3,2,1,0:T(8,128)(2,1)} %get-tuple-element.45) | copy-start | bytes 5308420
  355.9 1.9 copy-start.3
  355.9 2.8 copy-start.2

commit v2 on v0

--- a/solution.py
+++ b/solution.py
@@ -1,17 +1,836 @@
+import functools
 import jax
 import jax.numpy as jnp
+import numpy as np
 from jax import lax
+from jax.experimental import pallas as pl
+from jax.experimental.pallas import tpu as pltpu
 from jax.sharding import PartitionSpec as P
 
 QUERY_HEADS = 12
 KEY_VALUE_HEADS = 2
 HEAD_DIM = 128
-TOP = 4
 CAP = 128
-
-
 NORM_EPSILON = 1e-06
 ROTARY_BASE = 1000000.0
+MESH = pl.DeviceIdType.MESH
+HEAD = 128
+TOP = 4
+EPS = 1e-06
+BASE = 1000000.0
+F32 = jnp.float32
+BF16 = jnp.bfloat16
+
+
+def dot(a, b):
+    return lax.dot_general(a, b, (((1,), (0,)), ((), ())), preferred_element_type=F32)
+
+
+def dot_t(a, b):
+    return lax.dot_general(a, b, (((1,), (1,)), ((), ())), preferred_element_type=F32)
+
+
+def t_dot(a, b):
+    return lax.dot_general(a, b, (((0,), (0,)), ((), ())), preferred_element_type=F32)
+
+
+class Place:
+    def __init__(self, nctx, nz):
+        self.nctx, self.nz, self.nch = nctx, nz, nctx // 2
+        self.c = lax.axis_index("ctx")
+        self.z = lax.axis_index("wsh")
+        self.chip = self.c // 2
+        self.core = self.c % 2
+        self.sib = self.chip * 2 + 1 - self.core
+        self.square = self.nch == 4
+
+    def xchip(self):
+        return self.chip + 1 - 2 * (self.chip % 2)
+
+    def ychip(self):
+        return (self.chip + 2) % 4
+
+    def near(self, k):
+        s = 0
+        for here in range(self.nz):
+            order = sorted(
+                (v for v in range(self.nz) if v != here), key=lambda v: (abs(v - here), v)
+            )
+            s = jnp.where(self.z == here, order[k - 1], s)
+        return s
+
+    def onward(self, s):
+        to = jnp.where(s < self.z, self.z + 1, self.z - 1)
+        return to, jnp.logical_and(to >= 0, to < self.nz)
+
+    def zto(self, dz):
+        return (self.z + dz) % self.nz
+
+    def zfrom(self, dz):
+        return (self.z + self.nz - dz) % self.nz
+
+
+class Sends:
+    def __init__(self, sems, count):
+        self.sems, self.count, self.used, self.live = sems, count, 0, []
+
+    def start(self, src, dst, rsem, dev, when=None):
+        assert self.used < self.count
+        cp = pltpu.make_async_remote_copy(
+            src_ref=src,
+            dst_ref=dst,
+            send_sem=self.sems.at[self.used],
+            recv_sem=rsem,
+            device_id=dev,
+            device_id_type=MESH,
+        )
+        if when is None:
+            cp.start()
+        else:
+            pl.when(when)(cp.start)
+        self.used += 1
+        self.live.append((cp, when))
+
+    def local(self, src, dst):
+        assert self.used < self.count
+        cp = pltpu.make_async_copy(src, dst, self.sems.at[self.used])
+        cp.start()
+        self.used += 1
+        return cp
+
+    def drain(self):
+        for cp, when in self.live:
+            if when is None:
+                cp.wait_send()
+            else:
+                pl.when(when)(cp.wait_send)
+        self.live = []
+
+
+def arrived(ref, sem):
+    pltpu.make_async_copy(ref, ref, sem).wait()
+
+
+def greet(pl_, plane=True, column=True):
+    bar = pltpu.get_barrier_semaphore()
+    n = 0
+    if plane:
+        for k in range(1, pl_.nctx):
+            pl.semaphore_signal(
+                bar, inc=1, device_id=((pl_.c + k) % pl_.nctx, pl_.z), device_id_type=MESH
+            )
+            n += 1
+    if column:
+        for k in range(1, pl_.nz):
+            pl.semaphore_signal(bar, inc=1, device_id=(pl_.c, pl_.zto(k)), device_id_type=MESH)
+            n += 1
+    pl.semaphore_wait(bar, n)
+
+
+def rms(x, width):
+    return lax.rsqrt(jnp.sum(x * x, axis=-1, keepdims=True) * (1.0 / width) + EPS)
+
+
+def gain_row(extra, lane):
+    pick = (lax.broadcasted_iota(jnp.int32, (16, extra.shape[1]), 1) == lane).astype(BF16)
+    return dot_t(pick, extra)[0:1]
+
+
+def rope(x, cos, sin):
+    return x * cos + pltpu.roll(x, HEAD // 2, 1) * sin
+
+
+class Reduce:
+    def __init__(self, pc, snd, slab, first, fx, fy, sems):
+        self.pc, self.snd, self.slab = pc, snd, slab
+        self.first, self.fx, self.fy, self.sems = first, fx, fy, sems
+        self.x, self.y, self.d = pc.xchip(), pc.ychip(), 3 - pc.chip
+
+    def to(self, chip):
+        return (chip * 2 + self.pc.core, self.pc.z)
+
+    def diagonal(self):
+        self.snd.start(self.slab(self.d, 0), self.first.at[0], self.sems.at[0], self.to(self.x))
+        self.snd.start(self.slab(self.d, 1), self.first.at[1], self.sems.at[1], self.to(self.y))
+
+    def straight_x(self):
+        self.snd.start(self.slab(self.x, 0), self.fx.at[0], self.sems.at[2], self.to(self.x))
+
+    def straight_y(self):
+        self.snd.start(self.slab(self.y, 1), self.fy.at[1], self.sems.at[5], self.to(self.y))
+
+    def merge(self, add):
+        arrived(self.first.at[0], self.sems.at[0])
+        add(self.slab(self.y, 0), self.first.at[0])
+        self.snd.start(self.slab(self.y, 0), self.fy.at[0], self.sems.at[4], self.to(self.y))
+        arrived(self.first.at[1], self.sems.at[1])
+        add(self.slab(self.x, 1), self.first.at[1])
+        self.snd.start(self.slab(self.x, 1), self.fx.at[1], self.sems.at[3], self.to(self.x))
+
+    def wait(self):
+        for w in range(2):
+            arrived(self.fx.at[w], self.sems.at[2 + w])
+            arrived(self.fy.at[w], self.sems.at[4 + w])
+
+
+def add_into(dst, src):
+    dst[...] = (dst[...].astype(F32) + src[...].astype(F32)).astype(BF16)
+
+
+def layer_kernel(
+    cfg,
+    h_ref, routes_ref, cot_ref, wq_ref, wk_ref, wv_ref, wo_ref, ex_ref, eg_ref, eu_ref, ed_ref,
+    cos_in, sin_in,
+    out_ref, ig_ref, eg_out, eu_out, ed_out, gwq_out, gwk_out, gwv_out, gwo_out, ext_out,
+    efirst, efx, efy, ozr,
+    wa, wb, we, za, zb, hbuf, cosr, sinr,
+    qs, kv, lses, obs, xa, h1s, xm, gr, gts,
+    ggu, ap, keep, sibs, sibr, zr, okeep, kgg, sgg, rgg, zgg,
+    gat, gkv, gkvb, gkvr, graw, part, pget, exts,
+    esibr,
+    bfirst, bfx, bfy, qfirst, qfx, qfy, kfirst, kfx, kfy,
+    zrb, zrq, zrk, fb, fq, fk, frb, frq, frk, rowp,
+    ssem, lsem, ra, rb, re, rza, rzb_, rfw, rxm, rxf,
+    sib_s, sib_r, z_s, z_r, osib_s, osib_r, oz_s, oz_r, rmisc, esem, bsem,
+    qsem, ksem, rkv, rkvf, rzb, rzq, rzk,
+):
+    nctx, nz, width, rp, t0, heads, fc, _ = cfg
+    pc = Place(nctx, nz)
+    nch = pc.nch
+    t2 = 2 * t0
+    qw = heads * HEAD
+    kw = qw + 2 * HEAD
+    kx = wa.shape[1] - qw
+    dp = wa.shape[0]
+    core, z, c, chip = pc.core, pc.z, pc.c, pc.chip
+    per = nz * rp
+    snd = Sends(ssem, ssem.shape[0])
+    loads = Sends(lsem, lsem.shape[0])
+    sib = (pc.sib, z)
+    mine = pl.ds(pl.multiple_of(chip * t2, t2), t2)
+    mine0 = pl.ds(pl.multiple_of(core * t0, t0), t0)
+    sib0 = pl.ds(pl.multiple_of((1 - core) * t0, t0), t0)
+    xs, ys, ds = pc.xchip() * 2, pc.ychip() * 2, (3 - chip) * 2
+    nearest = [pc.near(k) for k in range(1, nz)]
+
+    def rows(cc, s):
+        return pl.ds(pl.multiple_of((cc * nz + s) * rp, 16), rp)
+
+    def slot(s, k):
+        return pl.ds(pl.multiple_of(s * t2 + k * t0, t0), t0)
+
+    def slab_rows(q, w):
+        return pl.ds(pl.multiple_of((q * 2 + w) * per, 16), per)
+
+    tables = [loads.local(cos_in.at[mine], cosr), loads.local(sin_in.at[mine], sinr)]
+    for k in range(2):
+        za[z, k, :, 0:qw] = wq_ref[:, k * qw:(k + 1) * qw]
+        za[z, k, :, qw:qw + HEAD] = wk_ref[:, k * HEAD:(k + 1) * HEAD]
+        za[z, k, :, qw + HEAD:kw] = wv_ref[:, k * HEAD:(k + 1) * HEAD]
+        za[z, k, :, kw:] = ex_ref[...]
+        zb[z, k] = wo_ref[:, k * qw:(k + 1) * qw]
+    own = slot(z, core)
+    gr[own] = cot_ref[...].astype(BF16)
+    hbuf[core] = h_ref[...]
+    greet(pc)
+
+    def chain_start(ref, rs):
+        here = ref.at[z]
+        snd.start(here, here, rs.at[z], (c, z + 1), when=z + 1 < nz)
+        snd.start(here, here, rs.at[z], (c, z - 1), when=z > 0)
+
+    def chain_step(ref, rs, s):
+        here = ref.at[s]
+        arrived(here, rs.at[s])
+        to, on = pc.onward(s)
+        snd.start(here, here, rs.at[s], (c, to), when=on)
+
+    def spread(src, dst, rs, s):
+        here = dst.at[rows(c, s)]
+        sem = rs.at[c * nz + s]
+        for q in (pc.xchip(), pc.ychip()):
+            for k in range(2):
+                snd.start(src.at[k], here, sem, (q * 2 + k, z))
+        snd.start(src.at[1 - core], here, sem, sib)
+
+    def forward(dst, rs, s):
+        for source, to in ((ys, pc.xchip()), (xs + 1, pc.ychip())):
+            here = dst.at[rows(source, s)]
+            sem = rs.at[source * nz + s]
+            arrived(here, sem)
+            snd.start(here, here, sem, (to * 2 + core, z))
+
+    def settle(dst, rs):
+        for cc in (pc.sib, xs, ys + 1, ds, ds + 1):
+            for s in range(nz):
+                arrived(dst.at[rows(cc, s)], rs.at[cc * nz + s])
+
+    chain_start(za, rza)
+    snd.start(hbuf.at[core], hbuf.at[core], rfw.at[0], sib)
+    keeps = [loads.local(za.at[z, core], wa.at[rows(c, z)])]
+    spread(za.at[z], wa, ra, z)
+    chain_start(zb, rzb_)
+    last = z
+    for s in nearest:
+        chain_step(za, rza, s)
+        spread(za.at[s], wa, ra, s)
+        keeps.append(loads.local(za.at[s, core], wa.at[rows(c, s)]))
+        forward(wa, ra, last)
+        last = s
+    forward(wa, ra, last)
+    keeps.append(loads.local(zb.at[z, core], wb.at[rows(c, z)]))
+    spread(zb.at[z], wb, rb, z)
+    for s in nearest:
+        chain_step(zb, rzb_, s)
+        spread(zb.at[s], wb, rb, s)
+        keeps.append(loads.local(zb.at[s, core], wb.at[rows(c, s)]))
+    for dz in range(1, nz):
+        snd.start(gr.at[own], gr.at[own], rxm.at[dz], (c, pc.zto(dz)))
+    snd.start(gr.at[own], gr.at[own], rxf.at[0], sib)
+
+    arrived(hbuf.at[1 - core], rfw.at[0])
+    for cp in keeps + tables:
+        cp.wait()
+    settle(wa, ra)
+    cos, sin = cosr[...], sinr[...]
+    extra = wa[:, kw:]
+    gain_a = gain_row(extra, 8)
+    gain_m = gain_row(extra, 9)
+    for k in range(2):
+        hk = hbuf[k].astype(F32)
+        xa[pl.ds(k * t0, t0)] = (hk * rms(hk, width) * gain_a).astype(BF16)
+    xav = xa[...]
+    kraw = dot(xav, wa[:, qw:kw])
+    kv[mine, 0:HEAD] = rope(kraw[:, :HEAD], cos, sin).astype(BF16)
+    kv[mine, HEAD:] = kraw[:, HEAD:].astype(BF16)
+    for k in range(1, nch):
+        snd.start(kv.at[mine], kv.at[mine], rkvf.at[k], (((chip + k) % nch) * 2 + core, z))
+    for hd in range(heads):
+        cols = slice(hd * HEAD, (hd + 1) * HEAD)
+        qs[:, cols] = rope(dot(xav, wa[:, cols]), cos, sin).astype(BF16)
+
+    def mats(m, cc):
+        return we.at[m, pl.ds(pl.multiple_of(cc * per, 16), per)]
+
+    experts_in = (eg_ref, eu_ref, ed_ref)
+    own_e = [loads.local(experts_in[m].at[core], mats(m, c)) for m in range(3)]
+
+    def expert_spread(m):
+        here = mats(m, c)
+        sem = re.at[m * nctx + c]
+        for q in (pc.xchip(), pc.ychip()):
+            for k in range(2):
+                snd.start(experts_in[m].at[k], here, sem, (q * 2 + k, z))
+        snd.start(experts_in[m].at[1 - core], here, sem, sib)
+
+    expert_spread(0)
+    for s in [z] + nearest:
+        forward(wb, rb, s)
+    expert_spread(1)
+    expert_spread(2)
+    for k in range(1, nch):
+        other = pl.ds(pl.multiple_of(((chip + nch - k) % nch) * t2, t2), t2)
+        arrived(kv.at[other], rkvf.at[k])
+
+    keys = nch * t2
+    scale = HEAD ** -0.5
+    ok = lax.broadcasted_iota(jnp.int32, (t2, keys), 1) <= (
+        chip * t2 + lax.broadcasted_iota(jnp.int32, (t2, keys), 0)
+    )
+    lane = lax.broadcasted_iota(jnp.int32, (t2, 128), 1)
+    lane0 = lax.broadcasted_iota(jnp.int32, (t0, 128), 1)
+    lses[...] = jnp.zeros((t2, 128), F32)
+
+    def head_forward(hd, carry):
+        cols = pl.ds(pl.multiple_of(hd * HEAD, HEAD), HEAD)
+        s = dot_t(qs[:, cols], kv[:, 0:HEAD]) * scale
+        s = jnp.where(ok, s, -1e30)
+        m = jnp.max(s, axis=-1, keepdims=True)
+        e = jnp.exp(s - m)
+        total = jnp.sum(e, axis=-1, keepdims=True)
+        lses[...] = jnp.where(lane == hd, m + jnp.log(total), lses[...])
+        p = (e * (1.0 / total)).astype(BF16)
+        obs[:, cols] = dot(p, kv[:, HEAD:]).astype(BF16)
+        return carry
+
+    lax.fori_loop(0, heads, head_forward, 0)
+    settle(wb, rb)
+    part[...] = dot_t(obs[...], wb[...])
+    snd.start(part.at[sib0], pget, rfw.at[1], sib)
+    arrived(pget, rfw.at[1])
+    h1 = h_ref[...].astype(F32) + part[mine0] + pget[...]
+    h1s[...] = h1
+    xmv = (h1 * rms(h1, width) * gain_m).astype(BF16)
+    xm[own] = xmv
+    chosen = routes_ref[:, 0:1] == lane0
+    for k in range(1, TOP):
+        chosen = jnp.logical_or(chosen, routes_ref[:, k:k + 1] == lane0)
+    logits = jnp.where(chosen, dot(xmv, extra), -1e30)
+    top = jnp.max(logits, axis=-1, keepdims=True)
+    e = jnp.where(chosen, jnp.exp(logits - top), 0.0)
+    gts[own] = e / jnp.sum(e, axis=-1, keepdims=True)
+    for i, buf in enumerate((xm, gts)):
+        here = buf.at[own]
+        snd.start(here, here, rxm.at[(1 + i) * nz + z], (c, z + 1), when=z + 1 < nz)
+        snd.start(here, here, rxm.at[(1 + i) * nz + z], (c, z - 1), when=z > 0)
+    for i, buf in enumerate((xm, gts)):
+        snd.start(buf.at[own], buf.at[own], rxf.at[(1 + i) * nz + z], sib)
+    for m in range(3):
+        for source, to in ((ys, pc.xchip()), (xs + 1, pc.ychip())):
+            here = mats(m, source)
+            sem = re.at[m * nctx + source]
+            arrived(here, sem)
+            snd.start(here, here, sem, (to * 2 + core, z))
+    for dz in range(1, nz):
+        here = gr.at[slot(pc.zfrom(dz), core)]
+        arrived(here, rxm.at[dz])
+        snd.start(here, here, rxf.at[dz], sib)
+    for s in nearest:
+        to, on = pc.onward(s)
+        for i, buf in enumerate((xm, gts)):
+            here = buf.at[slot(s, core)]
+            sem = rxm.at[(1 + i) * nz + s]
+            arrived(here, sem)
+            snd.start(here, here, sem, (c, to), when=on)
+            snd.start(here, here, rxf.at[(1 + i) * nz + s], sib)
+    for dz in range(nz):
+        arrived(gr.at[slot(pc.zfrom(dz), 1 - core)], rxf.at[dz])
+    for i, buf in enumerate((xm, gts)):
+        for s in range(nz):
+            arrived(buf.at[slot(s, 1 - core)], rxf.at[(1 + i) * nz + s])
+    for m in range(3):
+        for cc in (pc.sib, xs, ys + 1, ds, ds + 1):
+            arrived(mats(m, cc), re.at[m * nctx + cc])
+    for cp in own_e:
+        cp.wait()
+    snd.drain()
+
+    eloc = cfg_experts(cfg)
+    mine_e = z * eloc + (core * eloc) // 2
+
+    def zof(i):
+        return (z + 1 + i) % nz
+
+    def blk(i):
+        return pl.ds(pl.multiple_of(zof(i) * t2, t2), t2)
+
+    def copy_to_sib(src, dst, ss, rs):
+        return pltpu.make_async_remote_copy(
+            src_ref=src, dst_ref=dst, send_sem=ss, recv_sem=rs, device_id=sib, device_id_type=MESH
+        )
+
+    def copy_to_z(i, src, dst, ss, rs):
+        return pltpu.make_async_remote_copy(
+            src_ref=src, dst_ref=dst, send_sem=ss, recv_sem=rs, device_id=(c, zof(i)),
+            device_id_type=MESH,
+        )
+
+    def g_copies(i):
+        return (
+            copy_to_sib(sibs.at[i], sibr.at[i], sib_s.at[i], sib_r.at[i]),
+            copy_to_sib(sgg.at[i], rgg.at[i], sib_s.at[nz + i], sib_r.at[nz + i]),
+        )
+
+    def gz_copies(i):
+        return (
+            copy_to_z(i, keep.at[i], zr.at[i], z_s.at[i], z_r.at[i]),
+            copy_to_z(i, kgg.at[i], zgg.at[i], z_s.at[nz + i], z_r.at[nz + i]),
+        )
+
+    def g_settle(i):
+        for cp in g_copies(i):
+            cp.wait()
+        keep[i] = (keep[i].astype(F32) + sibr[i].astype(F32)).astype(BF16)
+        kgg[i] = kgg[i] + rgg[i]
+
+    def rows_back(i, carry):
+        x = xm[blk(i)]
+        g = gr[blk(i)]
+        gate = jnp.sum(jnp.where(lane == mine_e, gts[blk(i)], 0.0), axis=1, keepdims=True)
+        pre = dot(x, we[0])
+        up = dot(x, we[1])
+        ga0 = dot(g, we[2])
+        sg = 1.0 / (1.0 + jnp.exp(-pre))
+        silu = pre * sg
+        act = silu * up
+        ggc = jnp.sum(act * ga0, axis=1, keepdims=True)
+        ggl = jnp.where(lane == mine_e, ggc, 0.0)
+        gact = gate * ga0
+        gg = (gact * up * sg * (1.0 + pre * (1.0 - sg))).astype(BF16)
+        gu = (gact * silu).astype(BF16)
+        ap[blk(i)] = (gate * act).astype(BF16)
+        ggu[blk(i), 0:fc] = gg
+        ggu[blk(i), fc:] = gu
+        gb = (dot_t(gg, we[0]) + dot_t(gu, we[1])).astype(BF16)
+        part[0:t0] = gb[:t0].astype(F32)
+        part[t0:] = gb[t0:].astype(F32)
+        keep[i] = part[mine0].astype(BF16)
+        sibs[i] = part[sib0].astype(BF16)
+        rowp[...] = ggl
+        kgg[i] = rowp[mine0]
+        sgg[i] = rowp[sib0]
+        for cp in g_copies(i):
+            cp.start()
+
+        @pl.when(i > 0)
+        def _():
+            g_settle(i - 1)
+            for cp in gz_copies(i - 1):
+                cp.start()
+
+        return carry
+
+    lax.fori_loop(0, nz, rows_back, 0)
+    g_settle(nz - 1)
+
+    ers = [
+        Reduce(
+            pc, snd, lambda q, w, m=m: we.at[m, slab_rows(q, w)], efirst.at[m], efx.at[m],
+            efy.at[m], esem.at[m],
+        )
+        for m in range(3)
+    ]
+    order = (ers[0].d, ers[0].x, ers[0].y, chip)
+
+    def expert_step(n, rs):
+        for one in rs:
+            (one.diagonal, one.straight_x, one.straight_y, lambda: None)[n]()
+
+    for n, q in enumerate(order):
+        cols = pl.ds(pl.multiple_of(q * 2 * per, 128), 2 * per)
+        gw = t_dot(xm[:, cols], ggu[...])
+        we[0, cols] = gw[:, :fc].astype(BF16)
+        we[1, cols] = gw[:, fc:].astype(BF16)
+        expert_step(n, ers[:2])
+
+    def o_copy(i):
+        return copy_to_sib(sibs.at[i], sibr.at[i], osib_s.at[i], osib_r.at[i])
+
+    def oz_copy(i):
+        return copy_to_z(i, okeep.at[i], ozr.at[i], oz_s.at[i], oz_r.at[i])
+
+    def o_settle(i):
+        o_copy(i).wait()
+        okeep[i] = (okeep[i].astype(F32) + sibr[i].astype(F32)).astype(BF16)
+
+    def rows_out(i, carry):
+        part[...] = dot_t(ap[blk(i)], we[2])
+        okeep[i] = part[mine0].astype(BF16)
+        sibs[i] = part[sib0].astype(BF16)
+        o_copy(i).start()
+
+        @pl.when(i > 0)
+        def _():
+            o_settle(i - 1)
+            oz_copy(i - 1).start()
+
+        return carry
+
+    lax.fori_loop(0, nz, rows_out, 0)
+    o_settle(nz - 1)
+
+    for n, q in enumerate(order):
+        cols = pl.ds(pl.multiple_of(q * 2 * per, 128), 2 * per)
+        we[2, cols] = t_dot(gr[:, cols], ap[...]).astype(BF16)
+        expert_step(n, ers[2:])
+
+    gsum = keep[nz - 1].astype(F32)
+    ggs = kgg[nz - 1]
+    for i in range(nz - 1):
+        arrived(zr.at[i], z_r.at[i])
+        arrived(zgg.at[i], z_r.at[nz + i])
+        gsum = gsum + zr[i].astype(F32)
+        ggs = ggs + zgg[i]
+    gate = gts[own]
+    glog = (gate * (ggs - jnp.sum(gate * ggs, axis=1, keepdims=True))).astype(BF16)
+    extra = wa[:, kw:]
+    gxm = gsum + dot_t(glog, extra)
+    h1 = h1s[...]
+    r = rms(h1, width)
+    n = h1 * r
+    gy = gxm * gain_m
+    g1 = cot_ref[...] + r * (gy - n * (jnp.sum(gy * n, axis=1, keepdims=True) * (1.0 / width)))
+    ext = t_dot(xm[own], glog) + t_dot((gxm * n).astype(BF16), (lane0 == 9).astype(BF16))
+    exts[...] = ext
+    ig_ref[...] = g1
+    gat[mine0] = g1.astype(BF16)
+    snd.start(gat.at[mine0], gat.at[mine0], rmisc.at[0], sib)
+    arrived(gat.at[sib0], rmisc.at[0])
+    gav = gat[...]
+    go = dot(gav, wb[...]).astype(BF16)
+    brs = Reduce(pc, snd, lambda q, w: wb.at[slab_rows(q, w)], bfirst, bfx, bfy, bsem)
+
+    def out_grads(k, carry):
+        cols = pl.ds(pl.multiple_of(k * 2 * per, 128), 2 * per)
+        wb[cols] = t_dot(gat[:, cols], obs[...]).astype(BF16)
+        return carry
+
+    lax.fori_loop(0, nch, out_grads, 0)
+    brs.diagonal()
+    brs.straight_x()
+    brs.straight_y()
+    obs[...] = go
+
+    cos, sin = cosr[...], sinr[...]
+    gkv[...] = jnp.zeros(gkv.shape, F32)
+
+    def one_head(hd, carry):
+        cols = pl.ds(pl.multiple_of(hd * HEAD, HEAD), HEAD)
+        s = dot_t(qs[:, cols], kv[:, 0:HEAD]) * scale
+        pe = jnp.where(ok, jnp.exp(s - jnp.sum(jnp.where(lane == hd, lses[...], 0.0), axis=1, keepdims=True)), 0.0)
+        gp = dot_t(obs[:, cols], kv[:, HEAD:])
+        delta = jnp.sum(pe * gp, axis=-1, keepdims=True)
+        gs = (pe * (gp - delta)).astype(BF16)
+        gq = dot(gs, kv[:, 0:HEAD]) * scale
+        graw[:, cols] = rope(gq, cos, -sin).astype(BF16)
+        gkv[:, 0:HEAD] += t_dot(gs, qs[:, cols])
+        gkv[:, HEAD:] += t_dot(pe.astype(BF16), obs[:, cols])
+        return carry
+
+    lax.fori_loop(0, heads, one_head, 0)
+    gkvb[...] = gkv[...].astype(BF16)
+    for k in range(1, nch):
+        q = (chip + k) % nch
+        snd.start(
+            gkvb.at[pl.ds(pl.multiple_of(q * t2, t2), t2)], gkvr.at[k - 1], rkv.at[k],
+            (q * 2 + core, z),
+        )
+
+    def fetch(src, room, spot):
+        here = room.at[pl.ds(spot // 2 * per, per), pl.ds(spot % 2 * fc, fc)]
+        return here, loads.local(src, here)
+
+    def add_far(dst, src):
+        here, cp = fetch(src, gr, 0)
+        cp.wait()
+        add_into(dst, here)
+
+    part[...] = dot_t(graw[:, :qw], wa[:, :qw])
+
+    def query_grads(k, carry):
+        cols = pl.ds(pl.multiple_of(k * 2 * per, 128), 2 * per)
+        wa[cols, 0:qw] = t_dot(xa[:, cols], graw[:, 0:qw]).astype(BF16)
+        return carry
+
+    lax.fori_loop(0, nch, query_grads, 0)
+    qrs = Reduce(
+        pc, snd, lambda q, w: wa.at[slab_rows(q, w), pl.ds(0, qw)], qfirst, qfx, qfy, qsem
+    )
+    qrs.diagonal()
+    qrs.straight_x()
+    qrs.straight_y()
+    brs.merge(add_into)
+    ers[0].merge(add_far)
+    gk = gkv[mine]
+    for k in range(1, nch):
+        arrived(gkvr.at[k - 1], rkv.at[k])
+        gk = gk + gkvr[k - 1].astype(F32)
+    graw[:, qw:qw + HEAD] = rope(gk[:, :HEAD] * scale, cos, -sin).astype(BF16)
+    graw[:, qw + HEAD:] = gk[:, HEAD:].astype(BF16)
+    part[...] += dot_t(graw[:, qw:], wa[:, qw:kw])
+    snd.start(part.at[sib0], pget, rmisc.at[1], sib)
+
+    def key_grads(k, carry):
+        cols = pl.ds(pl.multiple_of(k * 2 * per, 128), 2 * per)
+        wa[cols, qw:kw] = t_dot(xa[:, cols], graw[:, qw:]).astype(BF16)
+        return carry
+
+    lax.fori_loop(0, nch, key_grads, 0)
+    arrived(pget, rmisc.at[1])
+    gxa = part[mine0] + pget[...]
+    h = h_ref[...].astype(F32)
+    r = rms(h, width)
+    n = h * r
+    gy = gxa * gain_a
+    ig_ref[...] += r * (gy - n * (jnp.sum(gy * n, axis=1, keepdims=True) * (1.0 / width)))
+    wa[:, kw:] = (
+        exts[...] + t_dot((gxa * n).astype(BF16), (lane0 == 8).astype(BF16))
+    ).astype(BF16)
+    krs = Reduce(
+        pc, snd, lambda q, w: wa.at[slab_rows(q, w), pl.ds(qw, kx)], kfirst, kfx, kfy, ksem
+    )
+    krs.diagonal()
+    krs.straight_x()
+    krs.straight_y()
+    qrs.merge(add_into)
+    ers[1].merge(add_far)
+    krs.merge(add_into)
+    ers[2].merge(add_far)
+
+    osum = okeep[nz - 1].astype(F32) + h1s[...]
+    room = [xm.at[pl.ds(i * t0, t0)] for i in range(nz - 1)]
+    got = []
+    for i in range(nz - 1):
+        arrived(ozr.at[i], oz_r.at[i])
+        got.append(loads.local(ozr.at[i], room[i]))
+    for i in range(nz - 1):
+        got[i].wait()
+        osum = osum + room[i][...].astype(F32)
+    out_ref[...] = osum
+
+    def piece(q, w):
+        return pl.ds(pl.multiple_of((chip * 2 + w) * per + q * rp, 16), rp)
+
+    groups = (
+        (brs, lambda rows: wb.at[rows], zrb, rzb, fb, frb),
+        (qrs, lambda rows: wa.at[rows, pl.ds(0, qw)], zrq, rzq, fq, frq),
+        (krs, lambda rows: wa.at[rows, pl.ds(qw, kx)], zrk, rzk, fk, frk),
+    )
+    for rs, at, zrecv, rz, _, _ in groups:
+        rs.wait()
+        for w in range(2):
+            dst = rs.slab(chip, w)
+            dst[...] = (
+                dst[...].astype(F32) + rs.fx[w].astype(F32) + rs.fy[w].astype(F32)
+            ).astype(BF16)
+        for dz in range(1, nz):
+            q = pc.zto(dz)
+            for w in range(2):
+                snd.start(at(piece(q, w)), zrecv.at[dz - 1, w], rz.at[2 * dz + w], (c, q))
+
+    e_own = []
+    for m in range(3):
+        ers[m].wait()
+        got = [
+            fetch(src.at[m, w], room, 2 * m + w)
+            for src, room in ((efx, gr), (efy, xm)) for w in range(2)
+        ]
+        for _, cp in got:
+            cp.wait()
+        for w in range(2):
+            dst = ers[m].slab(chip, w)
+            tot = dst[...].astype(F32) + got[w][0][...].astype(F32)
+            dst[...] = (tot + got[2 + w][0][...].astype(F32)).astype(BF16)
+        snd.start(ers[m].slab(chip, 1 - core), esibr.at[m], rmisc.at[2 + m], sib)
+        e_own.append(loads.local(ers[m].slab(chip, core), (eg_out, eu_out, ed_out)[m].at[core]))
+    for k, (rs, at, zrecv, rz, fin, get) in enumerate(groups):
+        for w in range(2):
+            tot = at(piece(z, w))[...].astype(F32)
+            for dz in range(1, nz):
+                arrived(zrecv.at[dz - 1, w], rz.at[2 * dz + w])
+                tot = tot + zrecv[dz - 1, w].astype(F32)
+            fin[w] = tot
+        snd.start(fin.at[1 - core], get, rmisc.at[5 + k], sib)
+    for m in range(3):
+        arrived(esibr.at[m], rmisc.at[2 + m])
+        e_own.append(loads.local(esibr.at[m], (eg_out, eu_out, ed_out)[m].at[1 - core]))
+
+    def half(k, count):
+        return pl.ds(pl.multiple_of(k * count, 128), count)
+
+    for k, (out, count, fin, get, off) in enumerate((
+        (gwo_out, qw, fb, frb, 0), (gwq_out, qw, fq, frq, 0),
+        (gwk_out, HEAD, fk, frk, 0), (gwv_out, HEAD, fk, frk, HEAD),
+    )):
+        if k < 3:
+            arrived(get, rmisc.at[5 + k])
+        out[:, half(core, count)] = fin[core, :, off:off + count]
+        out[:, half(1 - core, count)] = get[:, off:off + count]
+    ext_out[...] = fk[core, :, 2 * HEAD:] + frk[:, 2 * HEAD:]
+    for cp in e_own:
+        cp.wait()
+    for i in range(nz - 1):
+        for cp in gz_copies(i):
+            cp.wait_send()
+        oz_copy(i).wait_send()
+    snd.drain()
+
+
+def cfg_experts(cfg):
+    return cfg[7]
+
+
+def layer_call(cfg, args):
+    nctx, nz, width, rp, t0, heads, fc, eloc = cfg
+    nch, t2, dp = nctx // 2, 2 * t0, nctx * nz * rp
+    qw = heads * HEAD
+    kx = 3 * HEAD
+    ca = qw + kx
+    keys = nch * t2
+    rows = nz * t2
+    per = nz * rp
+    vm = pl.BlockSpec(memory_space=pltpu.VMEM)
+    hb = pl.BlockSpec(memory_space=pltpu.HBM)
+    sds = jax.ShapeDtypeStruct
+    dma = pltpu.SemaphoreType.DMA
+    v = pltpu.VMEM
+    return pl.pallas_call(
+        functools.partial(layer_kernel, cfg),
+        out_shape=(
+            sds((t0, dp), F32), sds((t0, dp), F32),
+            sds((2, per, fc), BF16), sds((2, per, fc), BF16), sds((2, per, fc), BF16),
+            sds((rp, 2 * qw), F32), sds((rp, 2 * HEAD), F32), sds((rp, 2 * HEAD), F32),
+            sds((rp, 2 * qw), F32), sds((rp, 128), F32),
+        ) + (sds((3, 2, per, fc), BF16),) * 3 + (sds((nz - 1, t0, dp), BF16),),
+        in_specs=[vm] * 8 + [hb] * 5,
+        out_specs=(vm, vm, hb, hb, hb, vm, vm, vm, vm, vm, hb, hb, hb, hb),
+        scratch_shapes=[
+            v((dp, ca), BF16), v((dp, qw), BF16), v((3, dp, fc), BF16),
+            v((nz, 2, rp, ca), BF16), v((nz, 2, rp, qw), BF16), v((2, t0, dp), BF16),
+            v((t2, HEAD), F32), v((t2, HEAD), F32),
+            v((t2, qw), BF16), v((keys, 2 * HEAD), BF16), v((t2, 128), F32), v((t2, qw), BF16),
+            v((t2, dp), BF16), v((t0, dp), F32),
+            v((rows, dp), BF16), v((rows, dp), BF16), v((rows, 128), F32),
+            v((rows, 2 * fc), BF16), v((rows, fc), BF16),
+            v((nz, t0, dp), BF16), v((nz, t0, dp), BF16), v((nz, t0, dp), BF16),
+            v((nz - 1, t0, dp), BF16), v((nz, t0, dp), BF16),
+            v((nz, t0, 128), F32), v((nz, t0, 128), F32), v((nz, t0, 128), F32),
+            v((nz - 1, t0, 128), F32),
+            v((t2, dp), BF16), v((keys, 2 * HEAD), F32), v((keys, 2 * HEAD), BF16),
+            v((nch - 1, t2, 2 * HEAD), BF16), v((t2, ca - 128), BF16),
+            v((t2, dp), F32), v((t0, dp), F32), v((dp, 128), F32),
+            v((3, per, fc), BF16),
+            v((2, per, qw), BF16), v((2, per, qw), BF16), v((2, per, qw), BF16),
+            v((2, per, qw), BF16), v((2, per, qw), BF16), v((2, per, qw), BF16),
+            v((2, per, kx), BF16), v((2, per, kx), BF16), v((2, per, kx), BF16),
+            v((nz - 1, 2, rp, qw), BF16), v((nz - 1, 2, rp, qw), BF16),
+            v((nz - 1, 2, rp, kx), BF16),
+            v((2, rp, qw), F32), v((2, rp, qw), F32), v((2, rp, kx), F32),
+            v((rp, qw), F32), v((rp, qw), F32), v((rp, kx), F32),
+            v((t2, 128), F32),
+            dma((270,)), dma((60,)), dma((nctx * nz,)), dma((nctx * nz,)), dma((3 * nctx,)),
+            dma((nz,)), dma((nz,)), dma((2,)), dma((3 * nz,)), dma((3 * nz,)),
+            dma((2 * nz,)), dma((2 * nz,)), dma((2 * nz,)), dma((2 * nz,)),
+            dma((nz,)), dma((nz,)), dma((nz,)), dma((nz,)), dma((8,)), dma((3, 6)), dma((6,)),
+            dma((6,)), dma((6,)), dma((nch,)), dma((nch,)), dma((2 * nz,)), dma((2 * nz,)),
+            dma((2 * nz,)),
+        ],
+        compiler_params=pltpu.CompilerParams(
+            collective_id=0, has_side_effects=True, vmem_limit_bytes=64 * 2**20
+        ),
+        name="layer",
+    )(*args)
+
+
+def body(hidden, routes, cot, na, wq, wk, wv, wo, nm, wr, wg, wu, wd):
+    nctx, nz = lax.axis_size("ctx"), lax.axis_size("wsh")
+    t0, width = hidden.shape[1], hidden.shape[2]
+    rp = wq.shape[1]
+    eloc, ff = wg.shape[2], wg.shape[3]
+    heads = wq.shape[2] // HEAD // 2
+    fc = eloc * ff // 2
+    cfg = (nctx, nz, width, rp, t0, heads, fc, eloc)
+    experts = wr.shape[2]
+    extra = jnp.concatenate(
+        [wr[0], na[0][:, None], nm[0][:, None], jnp.zeros((rp, 128 - experts - 2), BF16)], axis=1
+    )
+    pos = np.arange(nctx * t0, dtype=np.float32)
+    freq = np.float32(BASE) ** (-np.arange(HEAD // 2, dtype=np.float32) * 2.0 / HEAD)
+    ang = pos[:, None] * freq.astype(np.float32)[None, :]
+    cos, sin = np.cos(ang), np.sin(ang)
+    cosf = jnp.asarray(np.concatenate([cos, cos], axis=1), F32)
+    sinf = jnp.asarray(np.concatenate([-sin, sin], axis=1), F32)
+    halves = [jnp.transpose(w[0], (1, 0, 2)) for w in (wg, wu, wd)]
+    r = layer_call(
+        cfg,
+        (hidden[0], routes[0, 0], cot[0], wq[0], wk[0], wv[0], wo[0], extra, *halves, cosf, sinf),
+    )
+    out, ig, eg, eu, ed, gwq, gwk, gwv, gwo, ext = r[:10]
+    back = lambda x: jnp.transpose(x.astype(F32), (1, 0, 2))[None]
+    return (
+        out[None], ig[None], ext[:, 8][None], gwq[None], gwk[None], gwv[None], gwo[None],
+        ext[:, 9][None], ext[:, :experts][None], back(eg), back(eu), back(ed),
+    )
 
 
 def shifted(value, axis, steps):
@@ -354,7 +1173,7 @@
     return (grad_after_attn + grad_before, layer_grads, expert_grads)
 
 
-def body(
+def plain_body(
     hidden_in,
     routes,
     cotangent,
@@ -441,7 +1260,7 @@
 
 def solution(mesh):
     return jax.shard_map(
-        body,
+        body if mesh.shape["ctx"] == 8 and mesh.shape["wsh"] == 4 else plain_body,
         mesh=mesh,
         in_specs=(
             P("wsh", "ctx", None),

time: 1430 us -> 310 us (0.22)
  waiting for transfers between devices: 680 us -> 0 us
  blocking collectives: 376 us -> 0 us
  Pallas kernels: 0 us -> 282 us
  local copies, waits for them, and re-layouts: 140 us -> 21.5 us
  matrix products: 107 us -> 0 us
  other arithmetic: 70.1 us -> 2.02 us
  starting transfers between devices: 28.7 us -> 0 us
  between operations: 16 us -> 0.72 us
    reduce_scatter x4 -> x0, waiting for transfers between devices: 482 us -> none  [the longest x1 142 us: backward_layer(): lax.psum_scatter(query_term, ('ctx', 'wsh'), scatter_dimension=0, tiled=T...]
    all_gather x5 -> x0, blocking collectives: 298 us -> none  [the longest x1 125 us: body(): lax.all_gather(w_router[layer_number], ('ctx', 'wsh'), axis=0, tiled=True)]
    pallas_call x0 -> x1, Pallas kernels: none -> 282 us  [layer_call(): pl.pallas_call(functools.partial(layer_kernel, cfg), out_shape=(sds((t0,...]
    all_to_all x4 -> x0, waiting for transfers between devices: 108 us -> none  [the longest x1 55.7 us: forward_layer(): lax.all_to_all(produced, 'wsh', split_axis=0, concat_axis=0, tiled=True)]
    dot_general x29 -> x0, matrix products: 105 us -> none  [the longest x1 9.17 us: backward_layer(): jnp.einsum('sjcd,djf->sjcf', grad_arrived, down_w, preferred_element_type...]
    unnamed x2 -> x0, blocking collectives: 77.8 us -> none
    unnamed x13 -> x0, waiting for transfers between devices: 59.5 us -> none
    convert_element_type x8 -> x0, local copies, waits for them, and re-layouts: 48.8 us -> none  [the longest x3 37.7 us: backward_layer(): expert_grads = (lax.psum_scatter(jnp.einsum('sjcd,sjcf->djf', arrived, gr...]
  transfers between devices with their start and end apart: 23 -> 0, of which waited for: 15 -> 0; matrix products, arithmetic and copies ran while one was open for 21% -> 0% of each run, Pallas kernels for 0% -> 0%
where the time goes in v2:
time: 310 us; the launch traced here: 306 us
  Pallas kernels  282 us (91%)
  local copies, waits for them, and re-layouts  21.5 us (7%)
    pallas_call x1, Pallas kernels, layer_call(): pl.pallas_call(functools.partial(layer_kernel, cfg), out_shape=(sds((t0,...  282 us
    unnamed x35, local copies, waits for them, and re-layouts  17.6 us

profile of v2, /device:TPU:15, one launch (start us, length us, event | category | flops | bytes accessed | tf_op | source)
XLA Modules:
  0.0 306.4 jit_solution(13879705453286559746)
XLA Ops:
  0.6 0.0 copy-start.4
  0.7 0.1 pad.3.clone
  0.7 0.8 copy.40
  1.6 0.8 copy.41
  2.3 0.8 copy.39
  3.1 0.7 maximum_maximum_fusion.ex_ref
  3.8 1.4 copy.38
  5.2 2.0 copy.54
  7.2 0.0 copy-done.4
  7.2 0.9 copy.53
  8.1 0.0 copy-done.5
  8.1 0.9 copy.52
  8.9 282.2 %layer.1 = (f32[128,1536]{1,0:T(8,128)}, f32[128,1536]{1,0:T(8,128)}, bf16[2,192,768]{2,1,0:T(8,128)(2,1)}, bf16[2,192,768]{2,1,0:T(8,128)(2,1)}, bf16[2,192,768...) custom-call(bf16[128,1536]{1,0:T(8,128)(2,1)} %bitcast.53, ...), custom_call_target="tpu_custom_call" | custom-call | tf_op jit(solution)/shard_map/layer/pallas_call | solution.py:757
  291.2 1.5 slice_reduce_fusion
  292.7 0.7 slice_bitcast_fusion
  293.4 0.7 copy.45
  294.1 1.1 convert_bitcast_fusion.2
  295.2 0.0 copy-start.2
  295.2 0.0 copy-start.3
  295.3 1.9 copy.46
  297.2 0.0 copy-done.2
  297.2 0.2 convert_bitcast_fusion
  297.4 1.9 copy.48
  299.3 1.9 copy.47
  301.2 0.9 copy.61
  302.1 0.5 copy-done
  302.7 0.9 copy.62
  303.5 0.2 copy-done.7
  303.8 0.7 copy.63
  304.5 0.6 copy.64
  305.1 0.6 copy.65
  305.7 0.7 copy.66
  (13 shorter events, 0.0 us)
Async XLA Ops:
  0.6 6.5 %copy-start.4 = (bf16[1,192,2,768]{3,2,1,0:T(2,128)(2,1)S(1)}, bf16[1,192,2,768]{3,2,1,0:T(2,128)(2,1)}, u32[]{:S(2)}) copy-start(bf16[1,192,2,768]{3,2,1,0:T(2,128)(2,1)} %param.26) | copy-start | bytes 1769476
  5.2 2.9 copy-start.5
  295.2 1.9 copy-start.2
  295.2 1.9 copy-start.3
  299.3 1.9 copy-start.1
  301.2 1.4 copy-start
  302.7 1.1 copy-start.7
  302.7 1.8 copy-start.9
  302.7 2.4 copy-start.8
  302.7 3.1 copy-start.6

commit v3 on v2

--- a/solution.py
+++ b/solution.py
@@ -54,14 +54,11 @@
         s = 0
         for here in range(self.nz):
             order = sorted(
-                (v for v in range(self.nz) if v != here), key=lambda v: (abs(v - here), v)
+                (v for v in range(self.nz) if v != here),
+                key=lambda v: (abs(v - here), 2 * v // self.nz != 2 * here // self.nz),
             )
             s = jnp.where(self.z == here, order[k - 1], s)
         return s
-
-    def onward(self, s):
-        to = jnp.where(s < self.z, self.z + 1, self.z - 1)
-        return to, jnp.logical_and(to >= 0, to < self.nz)
 
     def zto(self, dz):
         return (self.z + dz) % self.nz
@@ -111,20 +108,14 @@
     pltpu.make_async_copy(ref, ref, sem).wait()
 
 
-def greet(pl_, plane=True, column=True):
+def greet(pc):
     bar = pltpu.get_barrier_semaphore()
-    n = 0
-    if plane:
-        for k in range(1, pl_.nctx):
-            pl.semaphore_signal(
-                bar, inc=1, device_id=((pl_.c + k) % pl_.nctx, pl_.z), device_id_type=MESH
-            )
-            n += 1
-    if column:
-        for k in range(1, pl_.nz):
-            pl.semaphore_signal(bar, inc=1, device_id=(pl_.c, pl_.zto(k)), device_id_type=MESH)
-            n += 1
-    pl.semaphore_wait(bar, n)
+    for k in range(1, pc.nctx):
+        to = ((pc.c + k) % pc.nctx, pc.z)
+        pl.semaphore_signal(bar, inc=1, device_id=to, device_id_type=MESH)
+    for k in range(1, pc.nz):
+        pl.semaphore_signal(bar, inc=1, device_id=(pc.c, pc.zto(k)), device_id_type=MESH)
+    return lambda: pl.semaphore_wait(bar, pc.nctx + pc.nz - 2)
 
 
 def rms(x, width):
@@ -141,17 +132,18 @@
 
 
 class Reduce:
-    def __init__(self, pc, snd, slab, first, fx, fy, sems):
+    def __init__(self, pc, snd, slab, first, fx, fy, sems, far=None):
         self.pc, self.snd, self.slab = pc, snd, slab
         self.first, self.fx, self.fy, self.sems = first, fx, fy, sems
         self.x, self.y, self.d = pc.xchip(), pc.ychip(), 3 - pc.chip
+        self.far = far or (lambda w: slab(self.d, w))
 
     def to(self, chip):
         return (chip * 2 + self.pc.core, self.pc.z)
 
     def diagonal(self):
-        self.snd.start(self.slab(self.d, 0), self.first.at[0], self.sems.at[0], self.to(self.x))
-        self.snd.start(self.slab(self.d, 1), self.first.at[1], self.sems.at[1], self.to(self.y))
+        self.snd.start(self.far(0), self.first.at[0], self.sems.at[0], self.to(self.x))
+        self.snd.start(self.far(1), self.first.at[1], self.sems.at[1], self.to(self.y))
 
     def straight_x(self):
         self.snd.start(self.slab(self.x, 0), self.fx.at[0], self.sems.at[2], self.to(self.x))
@@ -179,18 +171,19 @@
 
 def layer_kernel(
     cfg,
-    h_ref, routes_ref, cot_ref, wq_ref, wk_ref, wv_ref, wo_ref, ex_ref, eg_ref, eu_ref, ed_ref,
+    h_ref, routes_ref, cot_ref, wq_ref, wk_ref, wv_ref, wo_ref, ga_ref, gm_ref, wr_ref,
+    eg_ref, eu_ref, ed_ref,
     cos_in, sin_in,
     out_ref, ig_ref, eg_out, eu_out, ed_out, gwq_out, gwk_out, gwv_out, gwo_out, ext_out,
     efirst, efx, efy, ozr,
-    wa, wb, we, za, zb, hbuf, cosr, sinr,
+    wk, wq, wb, we, zk, zq, zb, hbuf, cosr, sinr, square,
     qs, kv, lses, obs, xa, h1s, xm, gr, gts,
     ggu, ap, keep, sibs, sibr, zr, okeep, kgg, sgg, rgg, zgg,
     gat, gkv, gkvb, gkvr, graw, part, pget, exts,
     esibr,
     bfirst, bfx, bfy, qfirst, qfx, qfy, kfirst, kfx, kfy,
     zrb, zrq, zrk, fb, fq, fk, frb, frq, frk, rowp,
-    ssem, lsem, ra, rb, re, rza, rzb_, rfw, rxm, rxf,
+    ssem, lsem, rwk, rwq, rwb, re, rzk_, rzq_, rzb_, rfw, rxm, rxf,
     sib_s, sib_r, z_s, z_r, osib_s, osib_r, oz_s, oz_r, rmisc, esem, bsem,
     qsem, ksem, rkv, rkvf, rzb, rzq, rzk,
 ):
@@ -200,10 +193,11 @@
     t2 = 2 * t0
     qw = heads * HEAD
     kw = qw + 2 * HEAD
-    kx = wa.shape[1] - qw
-    dp = wa.shape[0]
+    kx = wk.shape[1]
+    dp = wk.shape[0]
     core, z, c, chip = pc.core, pc.z, pc.c, pc.chip
     per = nz * rp
+    met = greet(pc)
     snd = Sends(ssem, ssem.shape[0])
     loads = Sends(lsem, lsem.shape[0])
     sib = (pc.sib, z)
@@ -219,39 +213,41 @@
     def slot(s, k):
         return pl.ds(pl.multiple_of(s * t2 + k * t0, t0), t0)
 
+    def both_parts(s):
+        return pl.ds(pl.multiple_of(s * 2 * rp, 16), 2 * rp)
+
+    def part_of(s, k):
+        return pl.ds(pl.multiple_of((s * 2 + k) * rp, 16), rp)
+
     def slab_rows(q, w):
         return pl.ds(pl.multiple_of((q * 2 + w) * per, 16), per)
 
     tables = [loads.local(cos_in.at[mine], cosr), loads.local(sin_in.at[mine], sinr)]
+    square[...] = jnp.zeros(square.shape, F32)
+    experts = wr_ref.shape[0]
+    square[0:experts, 0:rp] = wr_ref[...].astype(F32)
+    square[8:9, 0:rp] = ga_ref[...].astype(F32)
+    square[9:10, 0:rp] = gm_ref[...].astype(F32)
+    ex = square[...].T[0:rp].astype(BF16)
     for k in range(2):
-        za[z, k, :, 0:qw] = wq_ref[:, k * qw:(k + 1) * qw]
-        za[z, k, :, qw:qw + HEAD] = wk_ref[:, k * HEAD:(k + 1) * HEAD]
-        za[z, k, :, qw + HEAD:kw] = wv_ref[:, k * HEAD:(k + 1) * HEAD]
-        za[z, k, :, kw:] = ex_ref[...]
-        zb[z, k] = wo_ref[:, k * qw:(k + 1) * qw]
+        at = part_of(z, k)
+        zk[at, 0:HEAD] = wk_ref[:, k * HEAD:(k + 1) * HEAD]
+        zk[at, HEAD:2 * HEAD] = wv_ref[:, k * HEAD:(k + 1) * HEAD]
+        zk[at, 2 * HEAD:] = ex
+        zq[at] = wq_ref[:, k * qw:(k + 1) * qw]
+        zb[at] = wo_ref[:, k * qw:(k + 1) * qw]
     own = slot(z, core)
     gr[own] = cot_ref[...].astype(BF16)
     hbuf[core] = h_ref[...]
-    greet(pc)
-
-    def chain_start(ref, rs):
-        here = ref.at[z]
-        snd.start(here, here, rs.at[z], (c, z + 1), when=z + 1 < nz)
-        snd.start(here, here, rs.at[z], (c, z - 1), when=z > 0)
-
-    def chain_step(ref, rs, s):
-        here = ref.at[s]
-        arrived(here, rs.at[s])
-        to, on = pc.onward(s)
-        snd.start(here, here, rs.at[s], (c, to), when=on)
+    met()
 
     def spread(src, dst, rs, s):
         here = dst.at[rows(c, s)]
         sem = rs.at[c * nz + s]
         for q in (pc.xchip(), pc.ychip()):
             for k in range(2):
-                snd.start(src.at[k], here, sem, (q * 2 + k, z))
-        snd.start(src.at[1 - core], here, sem, sib)
+                snd.start(src.at[part_of(s, k)], here, sem, (q * 2 + k, z))
+        snd.start(src.at[part_of(s, 1 - core)], here, sem, sib)
 
     def forward(dst, rs, s):
         for source, to in ((ys, pc.xchip()), (xs + 1, pc.ychip())):
@@ -265,49 +261,60 @@
             for s in range(nz):
                 arrived(dst.at[rows(cc, s)], rs.at[cc * nz + s])
 
-    chain_start(za, rza)
+    packs = ((zk, rzk_, wk, rwk), (zq, rzq_, wq, rwq), (zb, rzb_, wb, rwb))
+    for ref, rs, _, _ in packs:
+        for s in nearest:
+            here = ref.at[both_parts(z)]
+            snd.start(here, here, rs.at[z], (c, s))
+    for s in nearest:
+        snd.start(gr.at[own], gr.at[own], rxm.at[z], (c, s))
+    keeps = ([], [], [])
     snd.start(hbuf.at[core], hbuf.at[core], rfw.at[0], sib)
-    keeps = [loads.local(za.at[z, core], wa.at[rows(c, z)])]
-    spread(za.at[z], wa, ra, z)
-    chain_start(zb, rzb_)
-    last = z
-    for s in nearest:
-        chain_step(za, rza, s)
-        spread(za.at[s], wa, ra, s)
-        keeps.append(loads.local(za.at[s, core], wa.at[rows(c, s)]))
-        forward(wa, ra, last)
-        last = s
-    forward(wa, ra, last)
-    keeps.append(loads.local(zb.at[z, core], wb.at[rows(c, z)]))
-    spread(zb.at[z], wb, rb, z)
-    for s in nearest:
-        chain_step(zb, rzb_, s)
-        spread(zb.at[s], wb, rb, s)
-        keeps.append(loads.local(zb.at[s, core], wb.at[rows(c, s)]))
-    for dz in range(1, nz):
-        snd.start(gr.at[own], gr.at[own], rxm.at[dz], (c, pc.zto(dz)))
-    snd.start(gr.at[own], gr.at[own], rxf.at[0], sib)
-
+    for (ref, _, dst, rs), kept in zip(packs, keeps):
+        spread(ref, dst, rs, z)
+        kept.append(loads.local(ref.at[part_of(z, core)], dst.at[rows(c, z)]))
+    snd.start(gr.at[own], gr.at[own], rxf.at[z], sib)
+
+    def column(which):
+        ref, zs, dst, rs = packs[which]
+        for s in nearest:
+            arrived(ref.at[both_parts(s)], zs.at[s])
+            spread(ref, dst, rs, s)
+            keeps[which].append(loads.local(ref.at[part_of(s, core)], dst.at[rows(c, s)]))
+
+    def onward(which):
+        _, _, dst, rs = packs[which]
+        for s in [z] + nearest:
+            forward(dst, rs, s)
+
+    def have(which):
+        _, _, dst, rs = packs[which]
+        for cp in keeps[which]:
+            cp.wait()
+        settle(dst, rs)
+
+    column(0)
+    onward(0)
+    column(1)
     arrived(hbuf.at[1 - core], rfw.at[0])
-    for cp in keeps + tables:
+    for cp in tables:
         cp.wait()
-    settle(wa, ra)
+    have(0)
     cos, sin = cosr[...], sinr[...]
-    extra = wa[:, kw:]
+    extra = wk[:, 2 * HEAD:]
     gain_a = gain_row(extra, 8)
     gain_m = gain_row(extra, 9)
     for k in range(2):
         hk = hbuf[k].astype(F32)
         xa[pl.ds(k * t0, t0)] = (hk * rms(hk, width) * gain_a).astype(BF16)
     xav = xa[...]
-    kraw = dot(xav, wa[:, qw:kw])
+    kraw = dot(xav, wk[:, :2 * HEAD])
     kv[mine, 0:HEAD] = rope(kraw[:, :HEAD], cos, sin).astype(BF16)
     kv[mine, HEAD:] = kraw[:, HEAD:].astype(BF16)
     for k in range(1, nch):
         snd.start(kv.at[mine], kv.at[mine], rkvf.at[k], (((chip + k) % nch) * 2 + core, z))
-    for hd in range(heads):
-        cols = slice(hd * HEAD, (hd + 1) * HEAD)
-        qs[:, cols] = rope(dot(xav, wa[:, cols]), cos, sin).astype(BF16)
+    onward(1)
+    column(2)
 
     def mats(m, cc):
         return we.at[m, pl.ds(pl.multiple_of(cc * per, 16), per)]
@@ -323,11 +330,26 @@
                 snd.start(experts_in[m].at[k], here, sem, (q * 2 + k, z))
         snd.start(experts_in[m].at[1 - core], here, sem, sib)
 
+    def expert_onward(m):
+        for source, to in ((ys, pc.xchip()), (xs + 1, pc.ychip())):
+            here = mats(m, source)
+            sem = re.at[m * nctx + source]
+            arrived(here, sem)
+            snd.start(here, here, sem, (to * 2 + core, z))
+
+    def expert_have(m):
+        for cc in (pc.sib, xs, ys + 1, ds, ds + 1):
+            arrived(mats(m, cc), re.at[m * nctx + cc])
+        own_e[m].wait()
+
+    expert_spread(2)
+    have(1)
+    for hd in range(heads):
+        cols = slice(hd * HEAD, (hd + 1) * HEAD)
+        qs[:, cols] = rope(dot(xav, wq[:, cols]), cos, sin).astype(BF16)
+    onward(2)
     expert_spread(0)
-    for s in [z] + nearest:
-        forward(wb, rb, s)
     expert_spread(1)
-    expert_spread(2)
     for k in range(1, nch):
         other = pl.ds(pl.multiple_of(((chip + nch - k) % nch) * t2, t2), t2)
         arrived(kv.at[other], rkvf.at[k])
@@ -354,7 +376,8 @@
         return carry
 
     lax.fori_loop(0, heads, head_forward, 0)
-    settle(wb, rb)
+    expert_onward(2)
+    have(2)
     part[...] = dot_t(obs[...], wb[...])
     snd.start(part.at[sib0], pget, rfw.at[1], sib)
     arrived(pget, rfw.at[1])
@@ -362,54 +385,69 @@
     h1s[...] = h1
     xmv = (h1 * rms(h1, width) * gain_m).astype(BF16)
     xm[own] = xmv
-    chosen = routes_ref[:, 0:1] == lane0
-    for k in range(1, TOP):
-        chosen = jnp.logical_or(chosen, routes_ref[:, k:k + 1] == lane0)
+    picks = jnp.zeros((128, t0), F32)
+    for k in range(TOP):
+        row = lax.broadcasted_iota(jnp.int32, (128, t0), 0)
+        picks = picks + (routes_ref[k:k + 1, :] == row).astype(F32)
+    chosen = picks.T > 0.0
     logits = jnp.where(chosen, dot(xmv, extra), -1e30)
     top = jnp.max(logits, axis=-1, keepdims=True)
     e = jnp.where(chosen, jnp.exp(logits - top), 0.0)
     gts[own] = e / jnp.sum(e, axis=-1, keepdims=True)
-    for i, buf in enumerate((xm, gts)):
-        here = buf.at[own]
-        snd.start(here, here, rxm.at[(1 + i) * nz + z], (c, z + 1), when=z + 1 < nz)
-        snd.start(here, here, rxm.at[(1 + i) * nz + z], (c, z - 1), when=z > 0)
+    for s in nearest:
+        for i, buf in enumerate((xm, gts)):
+            snd.start(buf.at[own], buf.at[own], rxm.at[(1 + i) * nz + z], (c, s))
     for i, buf in enumerate((xm, gts)):
         snd.start(buf.at[own], buf.at[own], rxf.at[(1 + i) * nz + z], sib)
-    for m in range(3):
-        for source, to in ((ys, pc.xchip()), (xs + 1, pc.ychip())):
-            here = mats(m, source)
-            sem = re.at[m * nctx + source]
-            arrived(here, sem)
-            snd.start(here, here, sem, (to * 2 + core, z))
-    for dz in range(1, nz):
-        here = gr.at[slot(pc.zfrom(dz), core)]
-        arrived(here, rxm.at[dz])
-        snd.start(here, here, rxf.at[dz], sib)
+    expert_onward(0)
+    expert_onward(1)
     for s in nearest:
-        to, on = pc.onward(s)
+        here = gr.at[slot(s, core)]
+        arrived(here, rxm.at[s])
+        snd.start(here, here, rxf.at[s], sib)
+    for s in nearest:
         for i, buf in enumerate((xm, gts)):
             here = buf.at[slot(s, core)]
-            sem = rxm.at[(1 + i) * nz + s]
-            arrived(here, sem)
-            snd.start(here, here, sem, (c, to), when=on)
+            arrived(here, rxm.at[(1 + i) * nz + s])
             snd.start(here, here, rxf.at[(1 + i) * nz + s], sib)
-    for dz in range(nz):
-        arrived(gr.at[slot(pc.zfrom(dz), 1 - core)], rxf.at[dz])
-    for i, buf in enumerate((xm, gts)):
+    for s in range(nz):
+        arrived(gr.at[slot(s, 1 - core)], rxf.at[s])
+    expert_have(2)
+
+    def rows_first(i, carry):
+        at = pl.ds(pl.multiple_of(i * t2, t2), t2)
+        ggu[at, 0:fc] = dot(gr[at], we[2]).astype(BF16)
+        return carry
+
+    lax.fori_loop(0, nz, rows_first, 0)
+    for i, buf in ((1, xm), (2, gts)):
         for s in range(nz):
-            arrived(buf.at[slot(s, 1 - core)], rxf.at[(1 + i) * nz + s])
-    for m in range(3):
-        for cc in (pc.sib, xs, ys + 1, ds, ds + 1):
-            arrived(mats(m, cc), re.at[m * nctx + cc])
-    for cp in own_e:
-        cp.wait()
+            arrived(buf.at[slot(s, 1 - core)], rxf.at[i * nz + s])
+    expert_have(0)
+
+    def rows_pre(i, carry):
+        at = pl.ds(pl.multiple_of(i * t2, t2), t2)
+        pre = dot(xm[at], we[0])
+        high = pre.astype(BF16)
+        ap[at] = high
+        ggu[at, fc:] = (pre - high.astype(F32)).astype(BF16)
+        return carry
+
+    lax.fori_loop(0, nz, rows_pre, 0)
+    expert_have(1)
     snd.drain()
 
     eloc = cfg_experts(cfg)
     mine_e = z * eloc + (core * eloc) // 2
 
+    def seat(source, at):
+        return jnp.where(source > at, source - 1, source)
+
     def zof(i):
-        return (z + 1 + i) % nz
+        s = z
+        for k in range(nz - 1):
+            s = jnp.where(i == k, nearest[nz - 2 - k], s)
+        return s
 
     def blk(i):
         return pl.ds(pl.multiple_of(zof(i) * t2, t2), t2)
@@ -432,9 +470,10 @@
         )
 
     def gz_copies(i):
+        to = seat(z, zof(i))
         return (
-            copy_to_z(i, keep.at[i], zr.at[i], z_s.at[i], z_r.at[i]),
-            copy_to_z(i, kgg.at[i], zgg.at[i], z_s.at[nz + i], z_r.at[nz + i]),
+            copy_to_z(i, keep.at[i], zr.at[to], z_s.at[i], z_r.at[to]),
+            copy_to_z(i, kgg.at[i], zgg.at[to], z_s.at[nz + i], z_r.at[nz + to]),
         )
 
     def g_settle(i):
@@ -443,32 +482,29 @@
         keep[i] = (keep[i].astype(F32) + sibr[i].astype(F32)).astype(BF16)
         kgg[i] = kgg[i] + rgg[i]
 
-    def rows_back(i, carry):
+    def rows_mid(i, carry):
         x = xm[blk(i)]
-        g = gr[blk(i)]
         gate = jnp.sum(jnp.where(lane == mine_e, gts[blk(i)], 0.0), axis=1, keepdims=True)
-        pre = dot(x, we[0])
+        pre = ap[blk(i)].astype(F32) + ggu[blk(i), fc:].astype(F32)
         up = dot(x, we[1])
-        ga0 = dot(g, we[2])
+        ga0 = ggu[blk(i), 0:fc].astype(F32)
         sg = 1.0 / (1.0 + jnp.exp(-pre))
         silu = pre * sg
         act = silu * up
         ggc = jnp.sum(act * ga0, axis=1, keepdims=True)
-        ggl = jnp.where(lane == mine_e, ggc, 0.0)
+        rowp[...] = jnp.where(lane == mine_e, ggc, 0.0)
+        kgg[i] = rowp[mine0]
+        sgg[i] = rowp[sib0]
         gact = gate * ga0
-        gg = (gact * up * sg * (1.0 + pre * (1.0 - sg))).astype(BF16)
-        gu = (gact * silu).astype(BF16)
         ap[blk(i)] = (gate * act).astype(BF16)
-        ggu[blk(i), 0:fc] = gg
-        ggu[blk(i), fc:] = gu
-        gb = (dot_t(gg, we[0]) + dot_t(gu, we[1])).astype(BF16)
-        part[0:t0] = gb[:t0].astype(F32)
-        part[t0:] = gb[t0:].astype(F32)
+        ggu[blk(i), 0:fc] = (gact * up * sg * (1.0 + pre * (1.0 - sg))).astype(BF16)
+        ggu[blk(i), fc:] = (gact * silu).astype(BF16)
+        return carry
+
+    def rows_back(i, carry):
+        part[...] = dot_t(ggu[blk(i), 0:fc], we[0]) + dot_t(ggu[blk(i), fc:], we[1])
         keep[i] = part[mine0].astype(BF16)
         sibs[i] = part[sib0].astype(BF16)
-        rowp[...] = ggl
-        kgg[i] = rowp[mine0]
-        sgg[i] = rowp[sib0]
         for cp in g_copies(i):
             cp.start()
 
@@ -480,13 +516,14 @@
 
         return carry
 
-    lax.fori_loop(0, nz, rows_back, 0)
-    g_settle(nz - 1)
-
+    lax.fori_loop(0, nz, rows_mid, 0)
+
+    far = (zq, zb)
     ers = [
         Reduce(
             pc, snd, lambda q, w, m=m: we.at[m, slab_rows(q, w)], efirst.at[m], efx.at[m],
-            efy.at[m], esem.at[m],
+            efy.at[m], esem.at[m], (lambda w, m=m: far[m].at[pl.ds(w * per, per)])
+            if m < 2 else None,
         )
         for m in range(3)
     ]
@@ -499,15 +536,23 @@
     for n, q in enumerate(order):
         cols = pl.ds(pl.multiple_of(q * 2 * per, 128), 2 * per)
         gw = t_dot(xm[:, cols], ggu[...])
-        we[0, cols] = gw[:, :fc].astype(BF16)
-        we[1, cols] = gw[:, fc:].astype(BF16)
+        if n == 0:
+            zq[...] = gw[:, :fc].astype(BF16)
+            zb[...] = gw[:, fc:].astype(BF16)
+        else:
+            we[0, cols] = gw[:, :fc].astype(BF16)
+            we[1, cols] = gw[:, fc:].astype(BF16)
         expert_step(n, ers[:2])
+        if n == 0:
+            lax.fori_loop(0, nz, rows_back, 0)
+            g_settle(nz - 1)
 
     def o_copy(i):
         return copy_to_sib(sibs.at[i], sibr.at[i], osib_s.at[i], osib_r.at[i])
 
     def oz_copy(i):
-        return copy_to_z(i, okeep.at[i], ozr.at[i], oz_s.at[i], oz_r.at[i])
+        to = seat(z, zof(i))
+        return copy_to_z(i, okeep.at[i], ozr.at[to], oz_s.at[i], oz_r.at[to])
 
     def o_settle(i):
         o_copy(i).wait()
@@ -533,6 +578,18 @@
         cols = pl.ds(pl.multiple_of(q * 2 * per, 128), 2 * per)
         we[2, cols] = t_dot(gr[:, cols], ap[...]).astype(BF16)
         expert_step(n, ers[2:])
+
+    def fetch(src, room, spot):
+        here = room.at[pl.ds(spot // 2 * per, per), pl.ds(spot % 2 * fc, fc)]
+        return here, loads.local(src, here)
+
+    def add_far(dst, src):
+        here, cp = fetch(src, gr, 0)
+        cp.wait()
+        add_into(dst, here)
+
+    ers[0].merge(add_far)
+    ers[1].merge(add_far)
 
     gsum = keep[nz - 1].astype(F32)
     ggs = kgg[nz - 1]
@@ -543,7 +600,7 @@
         ggs = ggs + zgg[i]
     gate = gts[own]
     glog = (gate * (ggs - jnp.sum(gate * ggs, axis=1, keepdims=True))).astype(BF16)
-    extra = wa[:, kw:]
+    extra = wk[:, 2 * HEAD:]
     gxm = gsum + dot_t(glog, extra)
     h1 = h1s[...]
     r = rms(h1, width)
@@ -596,43 +653,33 @@
             (q * 2 + core, z),
         )
 
-    def fetch(src, room, spot):
-        here = room.at[pl.ds(spot // 2 * per, per), pl.ds(spot % 2 * fc, fc)]
-        return here, loads.local(src, here)
-
-    def add_far(dst, src):
-        here, cp = fetch(src, gr, 0)
-        cp.wait()
-        add_into(dst, here)
-
-    part[...] = dot_t(graw[:, :qw], wa[:, :qw])
+    part[...] = dot_t(graw[:, :qw], wq[...])
 
     def query_grads(k, carry):
         cols = pl.ds(pl.multiple_of(k * 2 * per, 128), 2 * per)
-        wa[cols, 0:qw] = t_dot(xa[:, cols], graw[:, 0:qw]).astype(BF16)
+        wq[cols] = t_dot(xa[:, cols], graw[:, 0:qw]).astype(BF16)
         return carry
 
     lax.fori_loop(0, nch, query_grads, 0)
     qrs = Reduce(
-        pc, snd, lambda q, w: wa.at[slab_rows(q, w), pl.ds(0, qw)], qfirst, qfx, qfy, qsem
+        pc, snd, lambda q, w: wq.at[slab_rows(q, w)], qfirst, qfx, qfy, qsem
     )
     qrs.diagonal()
     qrs.straight_x()
     qrs.straight_y()
     brs.merge(add_into)
-    ers[0].merge(add_far)
     gk = gkv[mine]
     for k in range(1, nch):
         arrived(gkvr.at[k - 1], rkv.at[k])
         gk = gk + gkvr[k - 1].astype(F32)
     graw[:, qw:qw + HEAD] = rope(gk[:, :HEAD] * scale, cos, -sin).astype(BF16)
     graw[:, qw + HEAD:] = gk[:, HEAD:].astype(BF16)
-    part[...] += dot_t(graw[:, qw:], wa[:, qw:kw])
+    part[...] += dot_t(graw[:, qw:], wk[:, :2 * HEAD])
     snd.start(part.at[sib0], pget, rmisc.at[1], sib)
 
     def key_grads(k, carry):
         cols = pl.ds(pl.multiple_of(k * 2 * per, 128), 2 * per)
-        wa[cols, qw:kw] = t_dot(xa[:, cols], graw[:, qw:]).astype(BF16)
+        wk[cols, 0:2 * HEAD] = t_dot(xa[:, cols], graw[:, qw:]).astype(BF16)
         return carry
 
     lax.fori_loop(0, nch, key_grads, 0)
@@ -643,17 +690,16 @@
     n = h * r
     gy = gxa * gain_a
     ig_ref[...] += r * (gy - n * (jnp.sum(gy * n, axis=1, keepdims=True) * (1.0 / width)))
-    wa[:, kw:] = (
+    wk[:, 2 * HEAD:] = (
         exts[...] + t_dot((gxa * n).astype(BF16), (lane0 == 8).astype(BF16))
     ).astype(BF16)
     krs = Reduce(
-        pc, snd, lambda q, w: wa.at[slab_rows(q, w), pl.ds(qw, kx)], kfirst, kfx, kfy, ksem
+        pc, snd, lambda q, w: wk.at[slab_rows(q, w)], kfirst, kfx, kfy, ksem
     )
     krs.diagonal()
     krs.straight_x()
     krs.straight_y()
     qrs.merge(add_into)
-    ers[1].merge(add_far)
     krs.merge(add_into)
     ers[2].merge(add_far)
 
@@ -673,8 +719,8 @@
 
     groups = (
         (brs, lambda rows: wb.at[rows], zrb, rzb, fb, frb),
-        (qrs, lambda rows: wa.at[rows, pl.ds(0, qw)], zrq, rzq, fq, frq),
-        (krs, lambda rows: wa.at[rows, pl.ds(qw, kx)], zrk, rzk, fk, frk),
+        (qrs, lambda rows: wq.at[rows], zrq, rzq, fq, frq),
+        (krs, lambda rows: wk.at[rows], zrk, rzk, fk, frk),
     )
     for rs, at, zrecv, rz, _, _ in groups:
         rs.wait()
@@ -683,10 +729,10 @@
             dst[...] = (
                 dst[...].astype(F32) + rs.fx[w].astype(F32) + rs.fy[w].astype(F32)
             ).astype(BF16)
-        for dz in range(1, nz):
-            q = pc.zto(dz)
+        for q in nearest[::-1]:
+            to = seat(z, q)
             for w in range(2):
-                snd.start(at(piece(q, w)), zrecv.at[dz - 1, w], rz.at[2 * dz + w], (c, q))
+                snd.start(at(piece(q, w)), zrecv.at[to, w], rz.at[2 * to + w], (c, q))
 
     e_own = []
     for m in range(3):
@@ -707,7 +753,7 @@
         for w in range(2):
             tot = at(piece(z, w))[...].astype(F32)
             for dz in range(1, nz):
-                arrived(zrecv.at[dz - 1, w], rz.at[2 * dz + w])
+                arrived(zrecv.at[dz - 1, w], rz.at[2 * dz - 2 + w])
                 tot = tot + zrecv[dz - 1, w].astype(F32)
             fin[w] = tot
         snd.start(fin.at[1 - core], get, rmisc.at[5 + k], sib)
@@ -762,12 +808,12 @@
             sds((rp, 2 * qw), F32), sds((rp, 2 * HEAD), F32), sds((rp, 2 * HEAD), F32),
             sds((rp, 2 * qw), F32), sds((rp, 128), F32),
         ) + (sds((3, 2, per, fc), BF16),) * 3 + (sds((nz - 1, t0, dp), BF16),),
-        in_specs=[vm] * 8 + [hb] * 5,
+        in_specs=[vm] * 10 + [hb] * 5,
         out_specs=(vm, vm, hb, hb, hb, vm, vm, vm, vm, vm, hb, hb, hb, hb),
         scratch_shapes=[
-            v((dp, ca), BF16), v((dp, qw), BF16), v((3, dp, fc), BF16),
-            v((nz, 2, rp, ca), BF16), v((nz, 2, rp, qw), BF16), v((2, t0, dp), BF16),
-            v((t2, HEAD), F32), v((t2, HEAD), F32),
+            v((dp, kx), BF16), v((dp, qw), BF16), v((dp, qw), BF16), v((3, dp, fc), BF16),
+            v((nz * 2 * rp, kx), BF16), v((nz * 2 * rp, qw), BF16), v((nz * 2 * rp, qw), BF16),
+            v((2, t0, dp), BF16), v((t2, HEAD), F32), v((t2, HEAD), F32), v((128, 128), F32),
             v((t2, qw), BF16), v((keys, 2 * HEAD), BF16), v((t2, 128), F32), v((t2, qw), BF16),
             v((t2, dp), BF16), v((t0, dp), F32),
             v((rows, dp), BF16), v((rows, dp), BF16), v((rows, 128), F32),
@@ -788,8 +834,8 @@
             v((2, rp, qw), F32), v((2, rp, qw), F32), v((2, rp, kx), F32),
             v((rp, qw), F32), v((rp, qw), F32), v((rp, kx), F32),
             v((t2, 128), F32),
-            dma((270,)), dma((60,)), dma((nctx * nz,)), dma((nctx * nz,)), dma((3 * nctx,)),
-            dma((nz,)), dma((nz,)), dma((2,)), dma((3 * nz,)), dma((3 * nz,)),
+            dma((270,)), dma((60,)), dma((nctx * nz,)), dma((nctx * nz,)), dma((nctx * nz,)),
+            dma((3 * nctx,)), dma((nz,)), dma((nz,)), dma((nz,)), dma((2,)), dma((3 * nz,)), dma((3 * nz,)),
             dma((2 * nz,)), dma((2 * nz,)), dma((2 * nz,)), dma((2 * nz,)),
             dma((nz,)), dma((nz,)), dma((nz,)), dma((nz,)), dma((8,)), dma((3, 6)), dma((6,)),
             dma((6,)), dma((6,)), dma((nch,)), dma((nch,)), dma((2 * nz,)), dma((2 * nz,)),
@@ -811,9 +857,6 @@
     fc = eloc * ff // 2
     cfg = (nctx, nz, width, rp, t0, heads, fc, eloc)
     experts = wr.shape[2]
-    extra = jnp.concatenate(
-        [wr[0], na[0][:, None], nm[0][:, None], jnp.zeros((rp, 128 - experts - 2), BF16)], axis=1
-    )
     pos = np.arange(nctx * t0, dtype=np.float32)
     freq = np.float32(BASE) ** (-np.arange(HEAD // 2, dtype=np.float32) * 2.0 / HEAD)
     ang = pos[:, None] * freq.astype(np.float32)[None, :]
@@ -823,7 +866,8 @@
     halves = [jnp.transpose(w[0], (1, 0, 2)) for w in (wg, wu, wd)]
     r = layer_call(
         cfg,
-        (hidden[0], routes[0, 0], cot[0], wq[0], wk[0], wv[0], wo[0], extra, *halves, cosf, sinf),
+        (hidden[0], routes[0, 0].T, cot[0], wq[0], wk[0], wv[0], wo[0], na, nm, wr[0].T, *halves,
+         cosf, sinf),
     )
     out, ig, eg, eu, ed, gwq, gwk, gwv, gwo, ext = r[:10]
     back = lambda x: jnp.transpose(x.astype(F32), (1, 0, 2))[None]

time: 310 us -> 292 us (0.942)
  Pallas kernels: 282 us -> 270 us
  local copies, waits for them, and re-layouts: 21.5 us -> 17.7 us
    pallas_call x1, Pallas kernels: 282 us -> 270 us  [layer_call(): pl.pallas_call(functools.partial(layer_kernel, cfg), out_shape=(sds((t0,...]
    unnamed x35 -> x33, local copies, waits for them, and re-layouts: 17.6 us -> 15.4 us
where the time goes in v3:
time: 292 us; the launch traced here: 290 us
  Pallas kernels  270 us (92%)
  local copies, waits for them, and re-layouts  17.7 us (6%)
    pallas_call x1, Pallas kernels, layer_call(): pl.pallas_call(functools.partial(layer_kernel, cfg), out_shape=(sds((t0,...  270 us
    unnamed x33, local copies, waits for them, and re-layouts  15.4 us

profile of v3, /device:TPU:15, one launch (start us, length us, event | category | flops | bytes accessed | tf_op | source)
XLA Modules:
  0.0 289.8 jit_solution(3319575682838139324)
XLA Ops:
  0.6 0.0 copy-start.4
  0.7 0.0 copy-start.5
  0.7 2.0 copy.46
  2.7 0.0 copy-done.4
  2.7 0.9 copy.45
  3.6 0.0 copy-done.5
  3.6 0.9 copy.44
  4.5 270.1 %layer.1 = (f32[128,1536]{1,0:T(8,128)}, f32[128,1536]{1,0:T(8,128)}, bf16[2,192,768]{2,1,0:T(8,128)(2,1)}, bf16[2,192,768]{2,1,0:T(8,128)(2,1)}, bf16[2,192,768...) custom-call(bf16[128,1536]{1,0:T(8,128)(2,1)} %bitcast.55, ...), custom_call_target="tpu_custom_call" | custom-call | tf_op jit(solution)/shard_map/layer/pallas_call | solution.py:803
  274.5 1.5 slice_reduce_fusion
  276.1 0.7 slice_bitcast_fusion
  276.8 0.7 copy.37
  277.5 1.1 convert_bitcast_fusion.2
  278.6 0.0 copy-start.2
  278.6 0.0 copy-start.3
  278.6 1.9 copy.38
  280.6 0.0 copy-done.2
  280.6 0.0 copy-done.3
  280.6 0.2 convert_bitcast_fusion
  280.8 1.9 copy.40
  282.7 1.9 copy.39
  284.6 0.0 copy-done.1
  284.6 0.9 copy.53
  285.5 0.5 copy-done
  286.0 0.9 copy.54
  286.9 0.2 copy-done.7
  287.1 0.7 copy.55
  287.9 0.0 copy-done.9
  287.9 0.6 copy.56
  288.5 0.0 copy-done.8
  288.5 0.6 copy.57
  289.1 0.0 copy-done.6
  289.1 0.7 copy.58
  (6 shorter events, 0.0 us)
Async XLA Ops:
  0.6 2.1 copy-start.4
  0.7 2.9 %copy-start.5 = (bf16[1,192,2,768]{3,2,1,0:T(2,128)(2,1)S(1)}, bf16[1,192,2,768]{3,2,1,0:T(2,128)(2,1)}, u32[]{:S(2)}) copy-start(bf16[1,192,2,768]{3,2,1,0:T(2,128)(2,1)} %param.27) | copy-start | bytes 1769476
  278.6 1.9 copy-start.2
  278.6 1.9 copy-start.3
  282.7 1.9 copy-start.1
  284.6 1.4 copy-start
  286.0 1.1 copy-start.7
  286.0 1.8 copy-start.9
  286.0 2.4 copy-start.8
  286.0 3.1 %copy-start.6 = (f32[48,1536]{1,0:T(8,128)S(1)}, f32[48,1536]{1,0:T(8,128)}, u32[]{:S(2)}) copy-start(f32[48,1536]{1,0:T(8,128)} %get-tuple-element.28) | copy-start | bytes 884740

commit v4 on v3

--- a/solution.py
+++ b/solution.py
@@ -95,13 +95,16 @@
         self.used += 1
         return cp
 
-    def drain(self):
-        for cp, when in self.live:
+    def take(self):
+        live, self.live = self.live, []
+        return live
+
+    def drain(self, live=None):
+        for cp, when in self.take() if live is None else live:
             if when is None:
                 cp.wait_send()
             else:
                 pl.when(when)(cp.wait_send)
-        self.live = []
 
 
 def arrived(ref, sem):
@@ -132,18 +135,17 @@
 
 
 class Reduce:
-    def __init__(self, pc, snd, slab, first, fx, fy, sems, far=None):
+    def __init__(self, pc, snd, slab, first, fx, fy, sems):
         self.pc, self.snd, self.slab = pc, snd, slab
         self.first, self.fx, self.fy, self.sems = first, fx, fy, sems
         self.x, self.y, self.d = pc.xchip(), pc.ychip(), 3 - pc.chip
-        self.far = far or (lambda w: slab(self.d, w))
 
     def to(self, chip):
         return (chip * 2 + self.pc.core, self.pc.z)
 
     def diagonal(self):
-        self.snd.start(self.far(0), self.first.at[0], self.sems.at[0], self.to(self.x))
-        self.snd.start(self.far(1), self.first.at[1], self.sems.at[1], self.to(self.y))
+        self.snd.start(self.slab(self.d, 0), self.first.at[0], self.sems.at[0], self.to(self.x))
+        self.snd.start(self.slab(self.d, 1), self.first.at[1], self.sems.at[1], self.to(self.y))
 
     def straight_x(self):
         self.snd.start(self.slab(self.x, 0), self.fx.at[0], self.sems.at[2], self.to(self.x))
@@ -174,11 +176,11 @@
     h_ref, routes_ref, cot_ref, wq_ref, wk_ref, wv_ref, wo_ref, ga_ref, gm_ref, wr_ref,
     eg_ref, eu_ref, ed_ref,
     cos_in, sin_in,
-    out_ref, ig_ref, eg_out, eu_out, ed_out, gwq_out, gwk_out, gwv_out, gwo_out, ext_out,
+    out_ref, ig_ref, eg_out, eu_out, ed_out, gwq_out, gwk_out, gwv_out, gwo_out, gna_out, gnm_out, gwr_out,
     efirst, efx, efy, ozr,
     wk, wq, wb, we, zk, zq, zb, hbuf, cosr, sinr, square,
     qs, kv, lses, obs, xa, h1s, xm, gr, gts,
-    ggu, ap, keep, sibs, sibr, zr, okeep, kgg, sgg, rgg, zgg,
+    ggu, ap, keep, sibs, sibr, zr, okeep, kgg, sgg, rgg, zgg, gtt,
     gat, gkv, gkvb, gkvr, graw, part, pget, exts,
     esibr,
     bfirst, bfx, bfy, qfirst, qfx, qfy, kfirst, kfx, kfy,
@@ -207,11 +209,18 @@
     xs, ys, ds = pc.xchip() * 2, pc.ychip() * 2, (3 - chip) * 2
     nearest = [pc.near(k) for k in range(1, nz)]
 
+    def line_send(src, sem, order):
+        for s in order:
+            snd.start(src, src, sem, (c, s))
+
     def rows(cc, s):
         return pl.ds(pl.multiple_of((cc * nz + s) * rp, 16), rp)
 
     def slot(s, k):
         return pl.ds(pl.multiple_of(s * t2 + k * t0, t0), t0)
+
+    def slot8(s, k):
+        return pl.ds(pl.multiple_of((s * 2 + k) * 8, 8), 8)
 
     def both_parts(s):
         return pl.ds(pl.multiple_of(s * 2 * rp, 16), 2 * rp)
@@ -263,11 +272,8 @@
 
     packs = ((zk, rzk_, wk, rwk), (zq, rzq_, wq, rwq), (zb, rzb_, wb, rwb))
     for ref, rs, _, _ in packs:
-        for s in nearest:
-            here = ref.at[both_parts(z)]
-            snd.start(here, here, rs.at[z], (c, s))
-    for s in nearest:
-        snd.start(gr.at[own], gr.at[own], rxm.at[z], (c, s))
+        line_send(ref.at[both_parts(z)], rs.at[z], nearest)
+    line_send(gr.at[own], rxm.at[z], nearest)
     keeps = ([], [], [])
     snd.start(hbuf.at[core], hbuf.at[core], rfw.at[0], sib)
     for (ref, _, dst, rs), kept in zip(packs, keeps):
@@ -316,40 +322,50 @@
     onward(1)
     column(2)
 
-    def mats(m, cc):
-        return we.at[m, pl.ds(pl.multiple_of(cc * per, 16), per)]
+    fh = fc // 2
+
+    def mats(m, j, cc):
+        at = pl.ds(pl.multiple_of(cc * per, 16), per)
+        return we.at[m, at, pl.ds(j * fh, fh)]
 
     experts_in = (eg_ref, eu_ref, ed_ref)
-    own_e = [loads.local(experts_in[m].at[core], mats(m, c)) for m in range(3)]
-
-    def expert_spread(m):
-        here = mats(m, c)
-        sem = re.at[m * nctx + c]
+    own_e = [
+        loads.local(experts_in[m].at[core], we.at[m, pl.ds(pl.multiple_of(c * per, 16), per)])
+        for m in range(3)
+    ]
+
+    def expert_spread(m, j):
+        here = mats(m, j, c)
+        sem = re.at[(2 * m + j) * nctx + c]
+        half = pl.ds(j * fh, fh)
         for q in (pc.xchip(), pc.ychip()):
             for k in range(2):
-                snd.start(experts_in[m].at[k], here, sem, (q * 2 + k, z))
-        snd.start(experts_in[m].at[1 - core], here, sem, sib)
-
-    def expert_onward(m):
+                snd.start(experts_in[m].at[k, :, half], here, sem, (q * 2 + k, z))
+        snd.start(experts_in[m].at[1 - core, :, half], here, sem, sib)
+
+    def expert_onward(m, j):
         for source, to in ((ys, pc.xchip()), (xs + 1, pc.ychip())):
-            here = mats(m, source)
-            sem = re.at[m * nctx + source]
+            here = mats(m, j, source)
+            sem = re.at[(2 * m + j) * nctx + source]
             arrived(here, sem)
             snd.start(here, here, sem, (to * 2 + core, z))
 
-    def expert_have(m):
+    def expert_have(m, j):
         for cc in (pc.sib, xs, ys + 1, ds, ds + 1):
-            arrived(mats(m, cc), re.at[m * nctx + cc])
-        own_e[m].wait()
-
-    expert_spread(2)
+            arrived(mats(m, j, cc), re.at[(2 * m + j) * nctx + cc])
+        if j == 0:
+            own_e[m].wait()
+
+    units = [(m, j) for j in range(2) for m in (2, 0, 1)]
+    dense_sends = snd.take()
+    expert_spread(*units[0])
     have(1)
     for hd in range(heads):
         cols = slice(hd * HEAD, (hd + 1) * HEAD)
         qs[:, cols] = rope(dot(xav, wq[:, cols]), cos, sin).astype(BF16)
     onward(2)
-    expert_spread(0)
-    expert_spread(1)
+    for unit in units[1:]:
+        expert_spread(*unit)
     for k in range(1, nch):
         other = pl.ds(pl.multiple_of(((chip + nch - k) % nch) * t2, t2), t2)
         arrived(kv.at[other], rkvf.at[k])
@@ -375,8 +391,15 @@
         obs[:, cols] = dot(p, kv[:, HEAD:]).astype(BF16)
         return carry
 
+    def tokens_in(i, s):
+        buf, at = tokens[i]
+        here = buf.at[at(s, core)]
+        arrived(here, rxm.at[i * nz + s])
+        snd.start(here, here, rxf.at[i * nz + s], sib)
+
+    tokens = ((gr, slot), (xm, slot), (gtt, slot8))
     lax.fori_loop(0, heads, head_forward, 0)
-    expert_onward(2)
+    expert_onward(*units[0])
     have(2)
     part[...] = dot_t(obs[...], wb[...])
     snd.start(part.at[sib0], pget, rfw.at[1], sib)
@@ -394,49 +417,41 @@
     top = jnp.max(logits, axis=-1, keepdims=True)
     e = jnp.where(chosen, jnp.exp(logits - top), 0.0)
     gts[own] = e / jnp.sum(e, axis=-1, keepdims=True)
+    gtt[slot8(z, core)] = gts[own].T[0:8]
+    for i in (2, 1):
+        buf, at = tokens[i]
+        line_send(buf.at[at(z, core)], rxm.at[i * nz + z], nearest[::-1])
+        snd.start(buf.at[at(z, core)], buf.at[at(z, core)], rxf.at[i * nz + z], sib)
+    for unit in units[1:]:
+        expert_onward(*unit)
     for s in nearest:
-        for i, buf in enumerate((xm, gts)):
-            snd.start(buf.at[own], buf.at[own], rxm.at[(1 + i) * nz + z], (c, s))
-    for i, buf in enumerate((xm, gts)):
-        snd.start(buf.at[own], buf.at[own], rxf.at[(1 + i) * nz + z], sib)
-    expert_onward(0)
-    expert_onward(1)
+        tokens_in(0, s)
     for s in nearest:
-        here = gr.at[slot(s, core)]
-        arrived(here, rxm.at[s])
-        snd.start(here, here, rxf.at[s], sib)
-    for s in nearest:
-        for i, buf in enumerate((xm, gts)):
-            here = buf.at[slot(s, core)]
-            arrived(here, rxm.at[(1 + i) * nz + s])
-            snd.start(here, here, rxf.at[(1 + i) * nz + s], sib)
+        for i in (1, 2):
+            tokens_in(i, s)
     for s in range(nz):
         arrived(gr.at[slot(s, 1 - core)], rxf.at[s])
-    expert_have(2)
-
-    def rows_first(i, carry):
+    def rows_first(i, carry, j):
         at = pl.ds(pl.multiple_of(i * t2, t2), t2)
-        ggu[at, 0:fc] = dot(gr[at], we[2]).astype(BF16)
+        ggu[at, 2 * j * fh:(2 * j + 1) * fh] = dot(
+            gr[at], we[2, :, j * fh:(j + 1) * fh]
+        ).astype(BF16)
         return carry
 
-    lax.fori_loop(0, nz, rows_first, 0)
-    for i, buf in ((1, xm), (2, gts)):
+    for j in range(2):
+        expert_have(2, j)
+        lax.fori_loop(0, nz, functools.partial(rows_first, j=j), 0)
+    for buf, at, i in ((xm, slot, 1), (gtt, slot8, 2)):
         for s in range(nz):
-            arrived(buf.at[slot(s, 1 - core)], rxf.at[i * nz + s])
-    expert_have(0)
-
-    def rows_pre(i, carry):
-        at = pl.ds(pl.multiple_of(i * t2, t2), t2)
-        pre = dot(xm[at], we[0])
-        high = pre.astype(BF16)
-        ap[at] = high
-        ggu[at, fc:] = (pre - high.astype(F32)).astype(BF16)
-        return carry
-
-    lax.fori_loop(0, nz, rows_pre, 0)
-    expert_have(1)
-    snd.drain()
-
+            arrived(buf.at[at(s, 1 - core)], rxf.at[i * nz + s])
+    square[...] = jnp.zeros(square.shape, F32)
+    for s in range(nz):
+        for k in range(2):
+            square[0:8] = gtt[slot8(s, k)]
+            gts[slot(s, k)] = square[...].T
+
+    mine128 = pl.ds(pl.multiple_of(core * 128, 128), 128)
+    sib128 = pl.ds(pl.multiple_of((1 - core) * 128, 128), 128)
     eloc = cfg_experts(cfg)
     mine_e = z * eloc + (core * eloc) // 2
 
@@ -482,27 +497,39 @@
         keep[i] = (keep[i].astype(F32) + sibr[i].astype(F32)).astype(BF16)
         kgg[i] = kgg[i] + rgg[i]
 
-    def rows_mid(i, carry):
+    def rows_mid(i, carry, j):
         x = xm[blk(i)]
+        cols = slice(j * fh, (j + 1) * fh)
+        first = slice(2 * j * fh, (2 * j + 1) * fh)
         gate = jnp.sum(jnp.where(lane == mine_e, gts[blk(i)], 0.0), axis=1, keepdims=True)
-        pre = ap[blk(i)].astype(F32) + ggu[blk(i), fc:].astype(F32)
-        up = dot(x, we[1])
-        ga0 = ggu[blk(i), 0:fc].astype(F32)
+        pre = dot(x, we[0, :, cols])
+        up = dot(x, we[1, :, cols])
+        ga0 = ggu[blk(i), first].astype(F32)
         sg = 1.0 / (1.0 + jnp.exp(-pre))
         silu = pre * sg
         act = silu * up
         ggc = jnp.sum(act * ga0, axis=1, keepdims=True)
-        rowp[...] = jnp.where(lane == mine_e, ggc, 0.0)
-        kgg[i] = rowp[mine0]
-        sgg[i] = rowp[sib0]
+        rowp[...] = jnp.where(lane == mine_e, ggc, 0.0).T[0:8]
+        if j == 0:
+            kgg[i] = rowp[:, mine128]
+            sgg[i] = rowp[:, sib128]
+        else:
+            kgg[i] += rowp[:, mine128]
+            sgg[i] += rowp[:, sib128]
         gact = gate * ga0
-        ap[blk(i)] = (gate * act).astype(BF16)
-        ggu[blk(i), 0:fc] = (gact * up * sg * (1.0 + pre * (1.0 - sg))).astype(BF16)
-        ggu[blk(i), fc:] = (gact * silu).astype(BF16)
+        ap[blk(i), cols] = (gate * act).astype(BF16)
+        ggu[blk(i), first] = (gact * up * sg * (1.0 + pre * (1.0 - sg))).astype(BF16)
+        ggu[blk(i), (2 * j + 1) * fh:(2 * j + 2) * fh] = (gact * silu).astype(BF16)
         return carry
 
     def rows_back(i, carry):
-        part[...] = dot_t(ggu[blk(i), 0:fc], we[0]) + dot_t(ggu[blk(i), fc:], we[1])
+        total = None
+        for k in range(4):
+            term = dot_t(
+                ggu[blk(i), k * fh:(k + 1) * fh], we[k % 2, :, k // 2 * fh:(k // 2 + 1) * fh]
+            )
+            total = term if total is None else total + term
+        part[...] = total
         keep[i] = part[mine0].astype(BF16)
         sibs[i] = part[sib0].astype(BF16)
         for cp in g_copies(i):
@@ -516,36 +543,51 @@
 
         return carry
 
-    lax.fori_loop(0, nz, rows_mid, 0)
-
     far = (zq, zb)
     ers = [
         Reduce(
             pc, snd, lambda q, w, m=m: we.at[m, slab_rows(q, w)], efirst.at[m], efx.at[m],
-            efy.at[m], esem.at[m], (lambda w, m=m: far[m].at[pl.ds(w * per, per)])
-            if m < 2 else None,
+            efy.at[m], esem.at[m],
         )
         for m in range(3)
     ]
     order = (ers[0].d, ers[0].x, ers[0].y, chip)
 
+    def chip_cols(q):
+        return pl.ds(pl.multiple_of(q * 2 * per, 128), 2 * per)
+
+    row_sends = snd.take()
+    for j in range(2):
+        expert_have(0, j)
+        expert_have(1, j)
+        lax.fori_loop(0, nz, functools.partial(rows_mid, j=j), 0)
+        if j == 0:
+            snd.drain(dense_sends)
+        half = pl.ds(j * fh, fh)
+        gw = t_dot(xm[:, chip_cols(order[0])], ggu[:, 2 * j * fh:2 * (j + 1) * fh])
+        for m in range(2):
+            far[m][:, j * fh:(j + 1) * fh] = gw[:, m * fh:(m + 1) * fh].astype(BF16)
+            for w, q in ((0, ers[m].x), (1, ers[m].y)):
+                snd.start(
+                    far[m].at[pl.ds(w * per, per), half], efirst.at[m, w, :, half],
+                    esem.at[m, w], ers[m].to(q),
+                )
+    snd.drain(row_sends)
+    lax.fori_loop(0, nz, rows_back, 0)
+    g_settle(nz - 1)
+
     def expert_step(n, rs):
         for one in rs:
             (one.diagonal, one.straight_x, one.straight_y, lambda: None)[n]()
 
     for n, q in enumerate(order):
-        cols = pl.ds(pl.multiple_of(q * 2 * per, 128), 2 * per)
+        if n == 0:
+            continue
+        cols = chip_cols(q)
         gw = t_dot(xm[:, cols], ggu[...])
-        if n == 0:
-            zq[...] = gw[:, :fc].astype(BF16)
-            zb[...] = gw[:, fc:].astype(BF16)
-        else:
-            we[0, cols] = gw[:, :fc].astype(BF16)
-            we[1, cols] = gw[:, fc:].astype(BF16)
+        for k in range(4):
+            we[k % 2, cols, k // 2 * fh:(k // 2 + 1) * fh] = gw[:, k * fh:(k + 1) * fh].astype(BF16)
         expert_step(n, ers[:2])
-        if n == 0:
-            lax.fori_loop(0, nz, rows_back, 0)
-            g_settle(nz - 1)
 
     def o_copy(i):
         return copy_to_sib(sibs.at[i], sibr.at[i], osib_s.at[i], osib_r.at[i])
@@ -598,6 +640,9 @@
         arrived(zgg.at[i], z_r.at[nz + i])
         gsum = gsum + zr[i].astype(F32)
         ggs = ggs + zgg[i]
+    square[...] = jnp.zeros(square.shape, F32)
+    square[0:8] = ggs
+    ggs = square[...].T
     gate = gts[own]
     glog = (gate * (ggs - jnp.sum(gate * ggs, axis=1, keepdims=True))).astype(BF16)
     extra = wk[:, 2 * HEAD:]
@@ -703,17 +748,6 @@
     krs.merge(add_into)
     ers[2].merge(add_far)
 
-    osum = okeep[nz - 1].astype(F32) + h1s[...]
-    room = [xm.at[pl.ds(i * t0, t0)] for i in range(nz - 1)]
-    got = []
-    for i in range(nz - 1):
-        arrived(ozr.at[i], oz_r.at[i])
-        got.append(loads.local(ozr.at[i], room[i]))
-    for i in range(nz - 1):
-        got[i].wait()
-        osum = osum + room[i][...].astype(F32)
-    out_ref[...] = osum
-
     def piece(q, w):
         return pl.ds(pl.multiple_of((chip * 2 + w) * per + q * rp, 16), rp)
 
@@ -722,7 +756,9 @@
         (qrs, lambda rows: wq.at[rows], zrq, rzq, fq, frq),
         (krs, lambda rows: wk.at[rows], zrk, rzk, fk, frk),
     )
-    for rs, at, zrecv, rz, _, _ in groups:
+
+    def column_out(which):
+        rs, at, zrecv, rz, _, _ = groups[which]
         rs.wait()
         for w in range(2):
             dst = rs.slab(chip, w)
@@ -734,8 +770,20 @@
             for w in range(2):
                 snd.start(at(piece(q, w)), zrecv.at[to, w], rz.at[2 * to + w], (c, q))
 
+    def column_in(which):
+        _, at, zrecv, rz, fin, get = groups[which]
+        for w in range(2):
+            tot = at(piece(z, w))[...].astype(F32)
+            for i in range(nz - 1):
+                arrived(zrecv.at[i, w], rz.at[2 * i + w])
+                tot = tot + zrecv[i, w].astype(F32)
+            fin[w] = tot
+        snd.start(fin.at[1 - core], get, rmisc.at[5 + which], sib)
+
     e_own = []
-    for m in range(3):
+    e_outs = (eg_out, eu_out, ed_out)
+
+    def expert_final(m):
         ers[m].wait()
         got = [
             fetch(src.at[m, w], room, 2 * m + w)
@@ -748,18 +796,33 @@
             tot = dst[...].astype(F32) + got[w][0][...].astype(F32)
             dst[...] = (tot + got[2 + w][0][...].astype(F32)).astype(BF16)
         snd.start(ers[m].slab(chip, 1 - core), esibr.at[m], rmisc.at[2 + m], sib)
-        e_own.append(loads.local(ers[m].slab(chip, core), (eg_out, eu_out, ed_out)[m].at[core]))
-    for k, (rs, at, zrecv, rz, fin, get) in enumerate(groups):
-        for w in range(2):
-            tot = at(piece(z, w))[...].astype(F32)
-            for dz in range(1, nz):
-                arrived(zrecv.at[dz - 1, w], rz.at[2 * dz - 2 + w])
-                tot = tot + zrecv[dz - 1, w].astype(F32)
-            fin[w] = tot
-        snd.start(fin.at[1 - core], get, rmisc.at[5 + k], sib)
-    for m in range(3):
+        e_own.append(loads.local(ers[m].slab(chip, core), e_outs[m].at[core]))
+
+    column_out(0)
+    expert_final(0)
+    expert_final(1)
+    osum = okeep[nz - 1].astype(F32) + h1s[...]
+    base = nz * t2 - (nz - 1) * t0
+    room = [xm.at[pl.ds(base + i * t0, t0)] for i in range(nz - 1)]
+    got = []
+    for i in range(nz - 1):
+        arrived(ozr.at[i], oz_r.at[i])
+        got.append(loads.local(ozr.at[i], room[i]))
+    for i in range(nz - 1):
+        got[i].wait()
+        osum = osum + room[i][...].astype(F32)
+    out_ref[...] = osum
+    column_out(1)
+    column_in(0)
+    column_out(2)
+    for m in range(2):
         arrived(esibr.at[m], rmisc.at[2 + m])
-        e_own.append(loads.local(esibr.at[m], (eg_out, eu_out, ed_out)[m].at[1 - core]))
+        e_own.append(loads.local(esibr.at[m], e_outs[m].at[1 - core]))
+    column_in(1)
+    expert_final(2)
+    column_in(2)
+    arrived(esibr.at[2], rmisc.at[4])
+    e_own.append(loads.local(esibr.at[2], e_outs[2].at[1 - core]))
 
     def half(k, count):
         return pl.ds(pl.multiple_of(k * count, 128), count)
@@ -772,7 +835,12 @@
             arrived(get, rmisc.at[5 + k])
         out[:, half(core, count)] = fin[core, :, off:off + count]
         out[:, half(1 - core, count)] = get[:, off:off + count]
-    ext_out[...] = fk[core, :, 2 * HEAD:] + frk[:, 2 * HEAD:]
+    square[...] = jnp.zeros(square.shape, F32)
+    square[0:rp] = fk[core, :, 2 * HEAD:] + frk[:, 2 * HEAD:]
+    turned = square[...].T
+    gwr_out[...] = turned[0:gwr_out.shape[0], 0:rp]
+    gna_out[...] = turned[8:9, 0:rp]
+    gnm_out[...] = turned[9:10, 0:rp]
     for cp in e_own:
         cp.wait()
     for i in range(nz - 1):
@@ -795,6 +863,7 @@
     keys = nch * t2
     rows = nz * t2
     per = nz * rp
+    experts = args[9].shape[0]
     vm = pl.BlockSpec(memory_space=pltpu.VMEM)
     hb = pl.BlockSpec(memory_space=pltpu.HBM)
     sds = jax.ShapeDtypeStruct
@@ -806,10 +875,10 @@
             sds((t0, dp), F32), sds((t0, dp), F32),
             sds((2, per, fc), BF16), sds((2, per, fc), BF16), sds((2, per, fc), BF16),
             sds((rp, 2 * qw), F32), sds((rp, 2 * HEAD), F32), sds((rp, 2 * HEAD), F32),
-            sds((rp, 2 * qw), F32), sds((rp, 128), F32),
+            sds((rp, 2 * qw), F32), sds((1, rp), F32), sds((1, rp), F32), sds((experts, rp), F32),
         ) + (sds((3, 2, per, fc), BF16),) * 3 + (sds((nz - 1, t0, dp), BF16),),
         in_specs=[vm] * 10 + [hb] * 5,
-        out_specs=(vm, vm, hb, hb, hb, vm, vm, vm, vm, vm, hb, hb, hb, hb),
+        out_specs=(vm, vm, hb, hb, hb) + (vm,) * 7 + (hb,) * 4,
         scratch_shapes=[
             v((dp, kx), BF16), v((dp, qw), BF16), v((dp, qw), BF16), v((3, dp, fc), BF16),
             v((nz * 2 * rp, kx), BF16), v((nz * 2 * rp, qw), BF16), v((nz * 2 * rp, qw), BF16),
@@ -820,8 +889,9 @@
             v((rows, 2 * fc), BF16), v((rows, fc), BF16),
             v((nz, t0, dp), BF16), v((nz, t0, dp), BF16), v((nz, t0, dp), BF16),
             v((nz - 1, t0, dp), BF16), v((nz, t0, dp), BF16),
-            v((nz, t0, 128), F32), v((nz, t0, 128), F32), v((nz, t0, 128), F32),
-            v((nz - 1, t0, 128), F32),
+            v((nz, 8, t0), F32), v((nz, 8, t0), F32), v((nz, 8, t0), F32),
+            v((nz - 1, 8, t0), F32),
+            v((nz * 2 * 8, t0), F32),
             v((t2, dp), BF16), v((keys, 2 * HEAD), F32), v((keys, 2 * HEAD), BF16),
             v((nch - 1, t2, 2 * HEAD), BF16), v((t2, ca - 128), BF16),
             v((t2, dp), F32), v((t0, dp), F32), v((dp, 128), F32),
@@ -833,9 +903,9 @@
             v((nz - 1, 2, rp, kx), BF16),
             v((2, rp, qw), F32), v((2, rp, qw), F32), v((2, rp, kx), F32),
             v((rp, qw), F32), v((rp, qw), F32), v((rp, kx), F32),
-            v((t2, 128), F32),
-            dma((270,)), dma((60,)), dma((nctx * nz,)), dma((nctx * nz,)), dma((nctx * nz,)),
-            dma((3 * nctx,)), dma((nz,)), dma((nz,)), dma((nz,)), dma((2,)), dma((3 * nz,)), dma((3 * nz,)),
+            v((8, t2), F32),
+            dma((300,)), dma((60,)), dma((nctx * nz,)), dma((nctx * nz,)), dma((nctx * nz,)),
+            dma((6 * nctx,)), dma((nz,)), dma((nz,)), dma((nz,)), dma((2,)), dma((3 * nz,)), dma((3 * nz,)),
             dma((2 * nz,)), dma((2 * nz,)), dma((2 * nz,)), dma((2 * nz,)),
             dma((nz,)), dma((nz,)), dma((nz,)), dma((nz,)), dma((8,)), dma((3, 6)), dma((6,)),
             dma((6,)), dma((6,)), dma((nch,)), dma((nch,)), dma((2 * nz,)), dma((2 * nz,)),
@@ -848,6 +918,23 @@
     )(*args)
 
 
+def pass_kernel(count, *refs):
+    for k in range(count):
+        refs[count + k][...] = refs[k][...]
+
+
+def pass_on(arrays):
+    count = len(arrays)
+    vm = pl.BlockSpec(memory_space=pltpu.VMEM)
+    return pl.pallas_call(
+        functools.partial(pass_kernel, count),
+        out_shape=tuple(jax.ShapeDtypeStruct(x.shape, x.dtype) for x in arrays),
+        in_specs=[vm] * count,
+        out_specs=(vm,) * count,
+        name="pass_on",
+    )(*arrays)
+
+
 def body(hidden, routes, cot, na, wq, wk, wv, wo, nm, wr, wg, wu, wd):
     nctx, nz = lax.axis_size("ctx"), lax.axis_size("wsh")
     t0, width = hidden.shape[1], hidden.shape[2]
@@ -856,7 +943,6 @@
     heads = wq.shape[2] // HEAD // 2
     fc = eloc * ff // 2
     cfg = (nctx, nz, width, rp, t0, heads, fc, eloc)
-    experts = wr.shape[2]
     pos = np.arange(nctx * t0, dtype=np.float32)
     freq = np.float32(BASE) ** (-np.arange(HEAD // 2, dtype=np.float32) * 2.0 / HEAD)
     ang = pos[:, None] * freq.astype(np.float32)[None, :]
@@ -869,11 +955,14 @@
         (hidden[0], routes[0, 0].T, cot[0], wq[0], wk[0], wv[0], wo[0], na, nm, wr[0].T, *halves,
          cosf, sinf),
     )
-    out, ig, eg, eu, ed, gwq, gwk, gwv, gwo, ext = r[:10]
+    out, ig, eg, eu, ed, gwq, gwk, gwv, gwo, gna, gnm, gwr = r[:12]
+    out, ig, gwq, gwk, gwv, gwo, gna, gnm, gwr = pass_on(
+        (out, ig, gwq, gwk, gwv, gwo, gna, gnm, gwr)
+    )
     back = lambda x: jnp.transpose(x.astype(F32), (1, 0, 2))[None]
     return (
-        out[None], ig[None], ext[:, 8][None], gwq[None], gwk[None], gwv[None], gwo[None],
-        ext[:, 9][None], ext[:, :experts][None], back(eg), back(eu), back(ed),
+        out[None], ig[None], gna, gwq[None], gwk[None], gwv[None], gwo[None],
+        gnm, gwr.T[None], back(eg), back(eu), back(ed),
     )
 
 

time: 292 us -> 285 us (0.976)
  local copies, waits for them, and re-layouts: 17.7 us -> 9.57 us
  Pallas kernels: 270 us -> 274 us
    unnamed x33 -> x16, local copies, waits for them, and re-layouts: 15.4 us -> 9.57 us
    pallas_call x0 -> x1, Pallas kernels: none -> 3.08 us  [pass_on(): pl.pallas_call(functools.partial(pass_kernel, count), out_shape=tuple((ja...]
where the time goes in v4:
time: 285 us; the launch traced here: 284 us
  Pallas kernels  274 us (96%)
  local copies, waits for them, and re-layouts  9.57 us (3%)
    pallas_call x1, Pallas kernels, layer_call(): pl.pallas_call(functools.partial(layer_kernel, cfg), out_shape=(sds((t0,...  271 us
    unnamed x16, local copies, waits for them, and re-layouts  9.57 us

profile of v4, /device:TPU:15, one launch (start us, length us, event | category | flops | bytes accessed | tf_op | source)
XLA Modules:
  0.0 284.4 jit_solution(2165321057144116542)
XLA Ops:
  0.6 0.0 copy-start.3
  0.7 0.0 copy-start.4
  0.7 2.0 copy.38
  2.7 0.0 copy-done.3
  2.7 0.9 copy.37
  3.6 0.0 copy-done.4
  3.6 0.9 copy.36
  4.5 270.8 %layer.1 = (f32[128,1536]{1,0:T(8,128)}, f32[128,1536]{1,0:T(8,128)}, bf16[2,192,768]{2,1,0:T(8,128)(2,1)}, bf16[2,192,768]{2,1,0:T(8,128)(2,1)}, bf16[2,192,768...) custom-call(bf16[128,1536]{1,0:T(8,128)(2,1)} %bitcast.52, ...), custom_call_target="tpu_custom_call" | custom-call | tf_op jit(solution)/shard_map/layer/pallas_call | solution.py:872
  275.2 0.0 copy-start.2
  275.2 3.1 %pass_on.1 = (f32[128,1536]{1,0:T(8,128)}, f32[128,1536]{1,0:T(8,128)}, f32[48,1536]{1,0:T(8,128)}, f32[48,256]{1,0:T(8,128)}, f32[48,256]{1,0:T(8,128)}, /*inde...) custom-call(f32[128,1536]{1,0:T(8,128)} %get-tuple-element.33.refs_0_, ...), custom_call_target="tpu_custom_call" | custom-call | tf_op jit(solution)/shard_map/pass_on/pallas_call | solution.py:929
  278.3 0.0 copy-done.2
  278.3 0.1 convert_bitcast_fusion.2
  278.4 0.0 copy-start
  278.4 0.0 copy-start.1
  278.4 1.9 copy.30
  280.4 0.0 copy-done
  280.4 0.0 copy-done.1
  280.4 0.2 convert_bitcast_fusion
  280.6 1.9 copy.32
  282.5 1.9 copy.31
Async XLA Ops:
  0.6 2.1 copy-start.3
  0.7 2.9 %copy-start.4 = (bf16[1,192,2,768]{3,2,1,0:T(2,128)(2,1)S(1)}, bf16[1,192,2,768]{3,2,1,0:T(2,128)(2,1)}, u32[]{:S(2)}) copy-start(bf16[1,192,2,768]{3,2,1,0:T(2,128)(2,1)} %param.27) | copy-start | bytes 1769476
  275.2 3.1 %copy-start.2 = (bf16[2,192,768]{2,1,0:T(8,128)(2,1)S(1)}, bf16[2,192,768]{2,1,0:T(8,128)(2,1)}, u32[]{:S(2)}) copy-start(bf16[2,192,768]{2,1,0:T(8,128)(2,1)} %get-tuple-element.51) | copy-start | bytes 1769476
  278.4 1.9 copy-start
  278.4 1.9 copy-start.1

commit v5 on v4

--- a/solution.py
+++ b/solution.py
@@ -918,21 +918,27 @@
     )(*args)
 
 
-def pass_kernel(count, *refs):
+def pass_kernel(count, pairs, *refs):
+    total = count + pairs
     for k in range(count):
-        refs[count + k][...] = refs[k][...]
-
-
-def pass_on(arrays):
-    count = len(arrays)
+        refs[total + k][...] = refs[k][...]
+    for k in range(count, total):
+        for half in range(2):
+            refs[total + k][:, half, :] = refs[k][half].astype(F32)
+
+
+def pass_on(arrays, pairs):
     vm = pl.BlockSpec(memory_space=pltpu.VMEM)
+    sds = jax.ShapeDtypeStruct
+    out_shape = [sds(x.shape, x.dtype) for x in arrays]
+    out_shape += [sds((x.shape[1], 2, x.shape[2]), F32) for x in pairs]
     return pl.pallas_call(
-        functools.partial(pass_kernel, count),
-        out_shape=tuple(jax.ShapeDtypeStruct(x.shape, x.dtype) for x in arrays),
-        in_specs=[vm] * count,
-        out_specs=(vm,) * count,
+        functools.partial(pass_kernel, len(arrays), len(pairs)),
+        out_shape=tuple(out_shape),
+        in_specs=[vm] * len(out_shape),
+        out_specs=(vm,) * len(out_shape),
         name="pass_on",
-    )(*arrays)
+    )(*arrays, *pairs)
 
 
 def body(hidden, routes, cot, na, wq, wk, wv, wo, nm, wr, wg, wu, wd):
@@ -956,13 +962,12 @@
          cosf, sinf),
     )
     out, ig, eg, eu, ed, gwq, gwk, gwv, gwo, gna, gnm, gwr = r[:12]
-    out, ig, gwq, gwk, gwv, gwo, gna, gnm, gwr = pass_on(
-        (out, ig, gwq, gwk, gwv, gwo, gna, gnm, gwr)
-    )
-    back = lambda x: jnp.transpose(x.astype(F32), (1, 0, 2))[None]
+    out, ig, gwq, gwk, gwv, gwo, gna, gnm, gwr, eg, eu, ed = pass_on(
+        (out, ig, gwq, gwk, gwv, gwo, gna, gnm, gwr), (eg, eu, ed)
+    )
     return (
         out[None], ig[None], gna, gwq[None], gwk[None], gwv[None], gwo[None],
-        gnm, gwr.T[None], back(eg), back(eu), back(ed),
+        gnm, gwr.T[None], eg[None], eu[None], ed[None],
     )
 
 

time: 285 us -> 280 us (0.982)
  local copies, waits for them, and re-layouts: 9.57 us -> 3.17 us
    unnamed x16 -> x5, local copies, waits for them, and re-layouts: 9.57 us -> 2.04 us
where the time goes in v5:
time: 280 us; the launch traced here: 279 us
  Pallas kernels  275 us (98%)
  local copies, waits for them, and re-layouts  3.17 us (1%)
    pallas_call x1, Pallas kernels, layer_call(): pl.pallas_call(functools.partial(layer_kernel, cfg), out_shape=(sds((t0,...  271 us

profile of v5, /device:TPU:15, one launch (start us, length us, event | category | flops | bytes accessed | tf_op | source)
XLA Modules:
  0.0 279.3 jit_solution(644667248769886725)
XLA Ops:
  0.6 0.0 copy-start
  0.7 0.0 copy-start.1
  0.7 2.0 copy.33
  2.7 0.0 copy-done
  2.7 0.0 copy-done.1
  2.7 1.1 copy_bitcast_fusion
  3.8 270.8 %layer.1 = (f32[128,1536]{1,0:T(8,128)}, f32[128,1536]{1,0:T(8,128)}, bf16[2,192,768]{2,1,0:T(8,128)(2,1)}, bf16[2,192,768]{2,1,0:T(8,128)(2,1)}, bf16[2,192,768...) custom-call(bf16[128,1536]{1,0:T(8,128)(2,1)} %bitcast.39, ...), custom_call_target="tpu_custom_call" | custom-call | tf_op jit(solution)/shard_map/layer/pallas_call | solution.py:872
  274.6 4.7 %pass_on.1 = (f32[128,1536]{1,0:T(8,128)}, f32[128,1536]{1,0:T(8,128)}, f32[48,1536]{1,0:T(8,128)}, f32[48,256]{1,0:T(8,128)}, f32[48,256]{1,0:T(8,128)}, /*inde...) custom-call(f32[128,1536]{1,0:T(8,128)} %get-tuple-element.36.refs_0, ...), custom_call_target="tpu_custom_call" | custom-call | tf_op jit(solution)/shard_map/pass_on/pallas_call | solution.py:935
Async XLA Ops:
  0.6 2.1 copy-start
  0.7 2.0 copy-start.1

commit v6 on v5

--- a/solution.py
+++ b/solution.py
@@ -744,8 +744,8 @@
     krs.diagonal()
     krs.straight_x()
     krs.straight_y()
+    krs.merge(add_into)
     qrs.merge(add_into)
-    krs.merge(add_into)
     ers[2].merge(add_far)
 
     def piece(q, w):

time: 280 us -> 280 us (level)
  no operation moved by 1% of the time
where the time goes in v6:
time: 280 us; the launch traced here: 279 us
  Pallas kernels  276 us (99%)
  local copies, waits for them, and re-layouts  3.17 us (1%)
    pallas_call x1, Pallas kernels, layer_call(): pl.pallas_call(functools.partial(layer_kernel, cfg), out_shape=(sds((t0,...  271 us

profile of v6, /device:TPU:15, one launch (start us, length us, event | category | flops | bytes accessed | tf_op | source)
XLA Modules:
  0.0 279.4 jit_solution(6984232267781356006)
XLA Ops:
  0.6 0.0 copy-start
  0.7 0.0 copy-start.1
  0.7 2.0 copy.33
  2.7 0.0 copy-done
  2.7 0.0 copy-done.1
  2.7 1.1 copy_bitcast_fusion
  3.8 270.8 %layer.1 = (f32[128,1536]{1,0:T(8,128)}, f32[128,1536]{1,0:T(8,128)}, bf16[2,192,768]{2,1,0:T(8,128)(2,1)}, bf16[2,192,768]{2,1,0:T(8,128)(2,1)}, bf16[2,192,768...) custom-call(bf16[128,1536]{1,0:T(8,128)(2,1)} %bitcast.39, ...), custom_call_target="tpu_custom_call" | custom-call | tf_op jit(solution)/shard_map/layer/pallas_call | solution.py:872
  274.7 4.7 %pass_on.1 = (f32[128,1536]{1,0:T(8,128)}, f32[128,1536]{1,0:T(8,128)}, f32[48,1536]{1,0:T(8,128)}, f32[48,256]{1,0:T(8,128)}, f32[48,256]{1,0:T(8,128)}, /*inde...) custom-call(f32[128,1536]{1,0:T(8,128)} %get-tuple-element.36.refs_0, ...), custom_call_target="tpu_custom_call" | custom-call | tf_op jit(solution)/shard_map/pass_on/pallas_call | solution.py:935
Async XLA Ops:
  0.6 2.1 copy-start
  0.7 2.0 copy-start.1
